TPU v7x, 128 devices: a whole 4x4x4 slice. The times are simulated.
128 devices in a mesh: row: 16 (over z_hi, y, core), col: 8 (over z_lo, x).
Axes of the slice: x: 4, y: 4, z: 4 (z_hi: 2, z_lo: 2; z = z_hi * 2 + z_lo), core: 2. Of those that a mesh axis runs over, the one named last changes fastest.
Arguments:
- field: float32 [512, 1024, 128], P('row', 'col'), may hold values from -6 to 6
- context: float32 [128, 256, 128], P('row', 'col'), may hold values from -6 to 6
- ctx_weight: float32 [128, 128], replicated, may hold values from -0.5 to 0.5
- norm_gains: float32 [5, 128], replicated, may hold values from 0.1 to 1.9
- expand_weight: float32 [128, 512], replicated, may hold values from -0.5 to 0.5
- depth_weight: float32 [3, 3, 512], replicated, may hold values from -2 to 2
- se_reduce: float32 [512, 32], replicated, may hold values from -4 to 4
- se_expand: float32 [32, 512], replicated, may hold values from -6 to 6
- project_weight: float32 [512, 128], replicated, may hold values from -0.25 to 0.25
- attn_qkv: float32 [2, 128, 384], replicated, may hold values from -3 to 3, as said below
- attn_out: float32 [2, 128, 128], replicated, may hold values from -0.5 to 0.5
- mlp_in: float32 [2, 128, 512], replicated, may hold values from -0.5 to 0.5
- mlp_out: float32 [2, 512, 128], replicated, may hold values from -0.25 to 0.25
Outputs:
- refined: float32 [512, 1024, 128], P('row', 'col')
Inputs may be any that keep to these rules, and one draw needn't show every extreme that they name: `attn_qkv`: projection weights.
All inputs are finite; a program needn't handle non-finite values.
Results may differ from a plain program's by a relative error of at most 0.0003.
Values sent between devices are 32-bit elements; how exact they have to be, the bound alone decides.
No kernel may reach another device: no remote copies, remote signals or barrier semaphores. Data moves between devices by JAX's collectives and lax.ppermute only.
A program may use at most 128 MiB of HBM per device.

v0:
```python
import math

import jax
import jax.numpy as jnp
from jax import lax
from jax.sharding import PartitionSpec as P

HEADS = 4
WINDOW = 8


PRECISE = lax.Precision.HIGHEST
EPSILON = 1e-05


def extended(block, sides, width):
    for axis, dim in sides:
        count = lax.axis_size(axis)
        forward = [(i, i + 1) for i in range(count - 1)]
        backward = [(target, source) for source, target in forward]
        low = lax.ppermute(
            lax.slice_in_dim(block, block.shape[dim] - width, None, axis=dim), axis, forward
        )
        high = lax.ppermute(lax.slice_in_dim(block, 0, width, axis=dim), axis, backward)
        block = jnp.concatenate([low, block, high], axis=dim)
    return block


def layer_norm(values, norm_gain):
    centre = jnp.mean(values, axis=-1, keepdims=True)
    shifted = values - centre
    spread = jnp.mean(shifted * shifted, axis=-1, keepdims=True)
    return shifted * lax.rsqrt(spread + EPSILON) * norm_gain


def interpolate(coarse_in, along):
    length = coarse_in.shape[along]
    before = lax.slice_in_dim(coarse_in, 0, length - 2, axis=along)
    middle = lax.slice_in_dim(coarse_in, 1, length - 1, axis=along)
    after_cell = lax.slice_in_dim(coarse_in, 2, length, axis=along)
    phases = [
        0.375 * before + 0.625 * middle,
        0.125 * before + 0.875 * middle,
        0.875 * middle + 0.125 * after_cell,
        0.625 * middle + 0.375 * after_cell,
    ]
    stacked = jnp.stack(phases, axis=along + 1)
    new_shape = list(coarse_in.shape)
    new_shape[along] = 4 * (length - 2)
    return stacked.reshape(new_shape)


def upsample(rimmed):
    return interpolate(interpolate(rimmed, 0), 1)


def depthwise(padded, kernel):
    out_rows = padded.shape[0] - 2
    out_cols = padded.shape[1] - 2
    summed = jnp.zeros((out_rows, out_cols, padded.shape[2]), jnp.float32)
    for row_off in range(3):
        for col_off in range(3):
            summed = (
                summed
                + padded[row_off : row_off + out_rows, col_off : col_off + out_cols]
                * kernel[row_off, col_off]
            )
    return summed


def attend(windows, norm_gain, qkv_weight, out_weight):
    number, length, channels = windows.shape
    head_dim = channels // HEADS
    normed = layer_norm(windows, norm_gain)
    projected = jnp.einsum("nlc,cd->nld", normed, qkv_weight, precision=PRECISE)
    queries = projected[:, :, :channels].reshape(number, length, HEADS, head_dim)
    keyed = projected[:, :, channels : 2 * channels].reshape(number, length, HEADS, head_dim)
    valued = projected[:, :, 2 * channels :].reshape(number, length, HEADS, head_dim)
    scores = jnp.einsum("nqhd,nkhd->nhqk", queries, keyed, precision=PRECISE) / math.sqrt(head_dim)
    weights = jax.nn.softmax(scores, axis=-1)
    blended = jnp.einsum("nhqk,nkhd->nqhd", weights, valued, precision=PRECISE).reshape(
        number, length, channels
    )
    return windows + jnp.einsum("nlc,cd->nld", blended, out_weight, precision=PRECISE)


def feed_forward(stream, norm_gain, weight_in, weight_out):
    inner = jax.nn.gelu(
        jnp.einsum("hwc,cf->hwf", layer_norm(stream, norm_gain), weight_in, precision=PRECISE)
    )
    return stream + jnp.einsum("hwf,fc->hwc", inner, weight_out, precision=PRECISE)


def to_blocks(stream):
    all_rows, all_cols, channels = stream.shape
    shaped = stream.reshape(all_rows // WINDOW, WINDOW, all_cols // WINDOW, WINDOW, channels)
    return shaped.transpose(0, 2, 1, 3, 4).reshape(-1, WINDOW * WINDOW, channels)


def from_blocks(windows, all_rows, all_cols):
    channels = windows.shape[-1]
    shaped = windows.reshape(all_rows // WINDOW, all_cols // WINDOW, WINDOW, WINDOW, channels)
    return shaped.transpose(0, 2, 1, 3, 4).reshape(all_rows, all_cols, channels)


def per_device(
    field,
    context,
    ctx_weight,
    norm_gains,
    expand_weight,
    depth_weight,
    se_reduce,
    se_expand,
    project_weight,
    attn_qkv,
    attn_out,
    mlp_in,
    mlp_out,
):
    tile_rows, tile_cols, channels = field.shape
    row_count = lax.axis_size("row")
    col_count = lax.axis_size("col")
    coarse = jnp.einsum("hwk,kc->hwc", context, ctx_weight, precision=PRECISE)
    rimmed = extended(coarse, (("row", 0), ("col", 1)), 1)
    stream = field + upsample(rimmed)
    hidden = jax.nn.gelu(
        jnp.einsum(
            "hwc,ce->hwe", layer_norm(stream, norm_gains[0]), expand_weight, precision=PRECISE
        )
    )
    padded = extended(hidden, (("row", 0), ("col", 1)), 1)
    active = jax.nn.gelu(depthwise(padded, depth_weight))
    summed = lax.psum(jnp.sum(active, axis=(0, 1)), ("row", "col"))
    pooled = summed / (tile_rows * tile_cols * row_count * col_count)
    squeezed = jax.nn.silu(jnp.dot(pooled, se_reduce, precision=PRECISE))
    gate_vec = jax.nn.sigmoid(jnp.dot(squeezed, se_expand, precision=PRECISE))
    stream = stream + jnp.einsum(
        "hwe,ec->hwc", active * gate_vec, project_weight, precision=PRECISE
    )
    stream = from_blocks(
        attend(to_blocks(stream), norm_gains[1], attn_qkv[0], attn_out[0]), tile_rows, tile_cols
    )
    stream = feed_forward(stream, norm_gains[2], mlp_in[0], mlp_out[0])
    row_step = tile_rows // row_count
    col_step = tile_cols // col_count
    spread_out = stream.reshape(row_step, row_count, col_step, col_count, channels)
    spread_out = spread_out.transpose(0, 2, 1, 3, 4).reshape(
        row_step, col_step, 1, row_count * col_count, channels
    )
    incoming = lax.all_to_all(spread_out, ("row", "col"), split_axis=3, concat_axis=2, tiled=True)
    item_count = incoming.shape[0]
    tokens = incoming.reshape(item_count, col_step, row_count, col_count, channels).transpose(
        0, 2, 3, 1, 4
    )
    tokens = tokens.reshape(
        item_count, WINDOW, row_count // WINDOW, WINDOW, tile_cols // WINDOW, channels
    )
    tokens = tokens.transpose(0, 2, 4, 1, 3, 5).reshape(-1, WINDOW * WINDOW, channels)
    attended = attend(tokens, norm_gains[3], attn_qkv[1], attn_out[1])
    restored = attended.reshape(
        item_count, row_count // WINDOW, tile_cols // WINDOW, WINDOW, WINDOW, channels
    )
    restored = restored.transpose(0, 3, 1, 4, 2, 5).reshape(
        item_count, row_count, col_count, col_step, channels
    )
    restored = restored.transpose(0, 3, 1, 2, 4).reshape(
        item_count, col_step, row_count * col_count, 1, channels
    )
    gathered = lax.all_to_all(restored, ("row", "col"), split_axis=2, concat_axis=3, tiled=True)
    gathered = gathered.reshape(row_step, col_step, row_count, col_count, channels).transpose(
        0, 2, 1, 3, 4
    )
    stream = gathered.reshape(tile_rows, tile_cols, channels)
    return feed_forward(stream, norm_gains[4], mlp_in[1], mlp_out[1])


def solution(mesh):
    placed = (
        P("row", "col", None),
        P("row", "col", None),
        P(),
        P(),
        P(),
        P(),
        P(),
        P(),
        P(),
        P(),
        P(),
        P(),
        P(),
    )
    return jax.shard_map(
        per_device, mesh=mesh, in_specs=placed, out_specs=P("row", "col", None), check_vma=False
    )
```

profile of v0, /device:TPU:0, one launch (start us, length us, event | category | flops | bytes accessed | tf_op | source)
XLA Modules:
  0.0 403.6 jit_solution(15310965681237609460)
XLA Ops:
  21.1 8.8 %fusion.6 = f32[32,128,512]{2,1,0:T(8,128)S(1)} fusion(f32[32,128,128]{2,1,0:T(8,128)S(1)} %get-tuple-element.8, f32[128]{0:T(128)S(1)} %get-tuple-element.45, f32[32,128]{1,0:T(8,128)S(1)} %add_rsqrt_fusion.4, f32[32,128]{1,0:T(8,128)S(1)} %broadcast_multiply_fusion.4, f32[128,512]{1,0:T(8,128)S(1)} %copy-done), kind=kOutput, calls=%fused_computation.12 | convolution fusion | flops 3239575552 | bytes 10781184 | tf_op jit(solution)/shard_map/hwc,ce->hwe/dot_general | solution.py:128
  42.8 4.3 %collective-permute-done.7 = f32[34,1,512]{2,1,0:T(1,128)S(1)} collective-permute-done((f32[34,1,512]{2,1,0:T(1,128)S(1)}, f32[34,1,512]{2,1,0:T(1,128)S(1)}, u32[]{:S(2)}, u32[]{:S(2)}) %collective-permute-start.7) | collective-permute-done | bytes 69664 | tf_op jit(solution)/shard_map/ppermute | solution.py:24
  47.0 6.2 %maximum_maximum_fusion = (f32[34,129,512]{2,1,0:T(8,128)S(1)}, f32[34,129,512]{2,1,0:T(8,128)}) fusion(f32[1,128,512]{2,1,0:T(8,128)S(1)} %collective-permute-done.5, f32[32,128,512]{2,1,0:T(8,128)S(1)} %fusion.6, f32[1,128,512]{2,1,0:T(8,128)S(1)} %collective-permute-done.4, f32[34,1,512]{2,1,0:T(1,128)S(1)} %collective-permute-done.6, ...), kind=kLoop, calls=%fused_computation.4 | loop fusion | flops 13473792 | bytes 27017216 | tf_op jit(solution)/shard_map/concatenate | solution.py:25
  53.3 22.0 %fusion.121 = (f32[512]{0:T(512)S(1)}, f32[32,128,512]{2,1,0:T(8,128)}) fusion(f32[512]{0:T(512)S(1)} %bitcast.203, f32[34,129,512]{2,1,0:T(8,128)} %get-tuple-element.10, f32[512]{0:T(512)S(1)} %bitcast.204, f32[1,128,512]{2,1,0:T(8,128)S(1)} %collective-permute-done.5, f32[32,128,512]{2,1,0:T(8,128)} %copy-done.2, f32[512]{0:T(512)S(1)} %bitcast.197, ...), kind=kLoop, calls=%fused_computation.184 | loop fusion | flops 58719744 | bytes 67653632 | tf_op jit(solution)/shard_map/reduce_sum | solution.py:134
  75.3 80.3 %psum.7 = f32[512]{0:T(512)S(1)} all-reduce(f32[512]{0:T(512)S(1)} %get-tuple-element.5), channel_id=1, replica_groups=mesh['row'=16,'col'=8] {'row','col'}, use_global_device_ids=true, to_apply=%region_3.0 | all-reduce | flops 512 | bytes 4096 | tf_op jit(solution)/shard_map/psum | solution.py:134
  155.9 9.4 %fusion.68 = f32[32,128,128]{2,1,0:T(8,128)S(1)} fusion(f32[32,128,128]{2,1,0:T(8,128)} %copy-done.3, f32[32,128,512]{2,1,0:T(8,128)} %get-tuple-element.6, f32[512]{0:T(512)S(1)} %add_divide_fusion, f32[512,128]{1,0:T(8,128)S(1)} %copy-done.11), kind=kOutput, calls=%fused_computation.97 | convolution fusion | flops 3223846912 | bytes 12847104 | tf_op jit(solution)/shard_map/hwe,ec->hwc/dot_general | solution.py:138
  170.7 5.7 %fusion.94 = f32[64,64,384]{2,1,0:T(8,128)S(1)} fusion(f32[64,64,128]{2,1,0:T(8,128)S(1)} %bitcast.185, f32[2,128,384]{2,1,0:T(8,128)S(1)} %copy-done.10), kind=kOutput, calls=%fused_computation.130 | convolution fusion | flops 2415919104 | bytes 8585216 | tf_op jit(solution)/shard_map/nlc,cd->nld/dot_general | solution.py:75
  179.5 3.8 copy.83
  183.3 3.8 copy.82
  189.8 16.3 %multiply_reduce_fusion.1 = (f32[64,4,64]{2,1,0:T(4,128)S(1)}, f32[64,4,64,64]{2,3,1,0:T(8,128)S(1)}) fusion(f32[64,64,4,32]{1,3,2,0:T(8,128)} %bitcast.176, f32[64,64,4,32]{1,3,2,0:T(8,128)} %bitcast.174), kind=kOutput, calls=%fused_computation.63 | convolution fusion | flops 404733952 | bytes 8454144 | tf_op jit(solution)/shard_map/nqhd,nkhd->nhqk/dot_general | solution.py:79
  208.9 9.4 %fusion.40 = f32[64,4,32,64]{3,2,1,0:T(8,128)S(1)} fusion(f32[64,64,4,32]{1,3,2,0:T(8,128)S(1)} %bitcast.189, f32[64,4,64,64]{2,3,1,0:T(8,128)S(1)} %get-tuple-element.48, f32[64,4,64]{2,1,0:T(4,128)S(1)} %fusion.48, f32[64,4,64]{2,1,0:T(4,128)S(1)} %get-tuple-element.47), kind=kOutput, calls=%fused_computation.55 | convolution fusion | flops 405798912 | bytes 8519680 | tf_op jit(solution)/shard_map/nhqk,nkhd->nqhd/dot_general | solution.py:81
  218.2 7.2 %fusion.129 = f32[64,64,128]{2,1,0:T(8,128)S(1)} fusion(f32[64,64,128]{2,1,0:T(8,128)S(1)} %bitcast.182, f32[64,64,128]{1,2,0:T(8,128)S(1)} %bitcast.191, f32[2,128,128]{2,1,0:T(8,128)S(1)} %copy-done.12), kind=kOutput, calls=%fused_computation.191 | convolution fusion | flops 805830656 | bytes 8454144 | tf_op jit(solution)/shard_map/nlc,cd->nld/dot_general | solution.py:84
  229.4 6.7 %fusion.84 = f32[32,128,512]{2,1,0:T(8,128)S(1)} fusion(f32[32,128,128]{2,1,0:T(8,128)S(1)} %bitcast.186, f32[2,128,512]{2,1,0:T(8,128)S(1)} %copy-done.9), kind=kOutput, calls=%fused_computation.116 | convolution fusion | flops 3221225472 | bytes 10747904 | tf_op jit(solution)/shard_map/hwc,cf->hwf/dot_general | solution.py:89
  236.1 8.7 %fusion.71 = f32[32,128,128]{2,1,0:T(8,128)S(1)} fusion(f32[32,128,128]{2,1,0:T(8,128)S(1)} %bitcast.193, f32[32,128,512]{2,1,0:T(8,128)S(1)} %fusion.84, f32[2,512,128]{2,1,0:T(8,128)S(1)} %copy-done.17), kind=kOutput, calls=%fused_computation.99 | convolution fusion | flops 3238526976 | bytes 12845056 | tf_op jit(solution)/shard_map/hwf,fc->hwc/dot_general | solution.py:91
  246.3 35.8 %all_to_all.8 = f32[2,16,1,128,128]{4,1,0,2,3:T(8,128)S(1)} all-to-all(f32[2,16,1,128,128]{4,1,0,2,3:T(8,128)S(1)} %copy.89), channel_id=1, replica_groups=mesh['row'=16,'col'=8] {'row','col'}, dimensions={3} | all-to-all | bytes 4194304 | tf_op jit(solution)/shard_map/all_to_all | solution.py:151
  288.7 5.7 %fusion.92 = f32[64,64,384]{2,1,0:T(8,128)S(1)} fusion(f32[64,64,128]{2,1,0:T(8,128)S(1)} %bitcast.187, f32[2,128,384]{2,1,0:T(8,128)S(1)} %copy-done.10), kind=kOutput, calls=%fused_computation.128 | convolution fusion | flops 2415919104 | bytes 8585216 | tf_op jit(solution)/shard_map/nlc,cd->nld/dot_general | solution.py:75
  297.5 3.8 copy.95
  301.2 3.8 copy.94
  307.8 16.7 %multiply_reduce_fusion = (f32[64,4,64]{2,1,0:T(4,128)S(1)}, f32[64,4,64,64]{2,3,1,0:T(8,128)S(1)}) fusion(f32[64,64,4,32]{1,3,2,0:T(8,128)} %bitcast.177, f32[64,64,4,32]{1,3,2,0:T(8,128)} %bitcast.175), kind=kOutput, calls=%fused_computation.62 | convolution fusion | flops 404733952 | bytes 8454144 | tf_op jit(solution)/shard_map/nqhd,nkhd->nhqk/dot_general | solution.py:79
  327.1 9.4 %fusion.38 = f32[64,4,32,64]{3,2,1,0:T(8,128)S(1)} fusion(f32[64,64,4,32]{1,3,2,0:T(8,128)S(1)} %bitcast.190, f32[64,4,64,64]{2,3,1,0:T(8,128)S(1)} %get-tuple-element.50, f32[64,4,64]{2,1,0:T(4,128)S(1)} %fusion.49, f32[64,4,64]{2,1,0:T(4,128)S(1)} %get-tuple-element.49), kind=kOutput, calls=%fused_computation.52 | convolution fusion | flops 405798912 | bytes 8519680 | tf_op jit(solution)/shard_map/nhqk,nkhd->nqhd/dot_general | solution.py:81
  336.5 6.9 %convolution_add_fusion = f32[64,64,128]{2,1,0:T(8,128)S(1)} fusion(f32[64,64,128]{2,1,0:T(8,128)S(1)} %bitcast.181, f32[64,64,128]{1,2,0:T(8,128)S(1)} %bitcast.192, f32[2,128,128]{2,1,0:T(8,128)S(1)} %copy-done.13), kind=kOutput, calls=%fused_computation.98 | convolution fusion | flops 805830656 | bytes 8454144 | tf_op jit(solution)/shard_map/nlc,cd->nld/dot_general | solution.py:84
  345.0 34.3 %all_to_all.9 = f32[2,16,128,1,128]{4,1,0,3,2:T(8,128)S(1)} all-to-all(f32[2,16,128,1,128]{4,1,0,3,2:T(8,128)S(1)} %copy.99), channel_id=1, replica_groups=mesh['row'=16,'col'=8] {'row','col'}, dimensions={2} | all-to-all | bytes 4194304 | tf_op jit(solution)/shard_map/all_to_all | solution.py:170
  386.8 6.7 %fusion.81 = f32[32,128,512]{2,1,0:T(8,128)S(1)} fusion(f32[32,128,128]{2,1,0:T(8,128)S(1)} %bitcast.183, f32[2,128,512]{2,1,0:T(8,128)S(1)} %copy-done.9), kind=kOutput, calls=%fused_computation.113 | convolution fusion | flops 3221225472 | bytes 10747904 | tf_op jit(solution)/shard_map/hwc,cf->hwf/dot_general | solution.py:89
  393.5 10.0 %fusion.74 = f32[32,128,128]{2,1,0:T(8,128)} fusion(f32[32,128,128]{2,1,0:T(8,128)S(1)} %bitcast.194, f32[32,128,512]{2,1,0:T(8,128)S(1)} %fusion.81, f32[2,512,128]{2,1,0:T(8,128)S(1)} %copy-done.18), kind=kOutput, calls=%fused_computation.100 | convolution fusion | flops 3238526976 | bytes 12845056 | tf_op jit(solution)/shard_map/hwf,fc->hwc/dot_general | solution.py:91
  (114 shorter events, 77.3 us)
Async XLA Ops:
  0.0 21.1 %copy-start = (f32[128,512]{1,0:T(8,128)S(1)}, f32[128,512]{1,0:T(8,128)}, u32[]{:S(2)}) copy-start(f32[128,512]{1,0:T(8,128)} %param.17) | copy-start | bytes 786436
  1.2 2.6 collective-permute-start
  2.5 5.0 %collective-permute-start.1 = (f32[1,32,128]{2,1,0:T(8,128)S(1)}, f32[1,32,128]{2,1,0:T(8,128)S(1)}, u32[]{:S(2)}, u32[]{:S(2)}) collective-permute-start(f32[1,32,128]{2,1,0:T(8,128)S(1)} %get-tuple-element.32), channel_id=1, source_target_pairs={{8,0},{16,8},{24,16},{32,24},{40,32},{48,40},{56,48},{64,56},{72,6... | collective-permute-start | bytes 49160 | tf_op jit(solution)/shard_map/ppermute | solution.py:24
  7.5 5.6 %collective-permute-start.2 = (f32[10,1,128]{2,1,0:T(1,128)S(1)}, f32[10,1,128]{2,1,0:T(1,128)S(1)}, u32[]{:S(2)}, u32[]{:S(2)}) collective-permute-start(f32[10,1,128]{2,1,0:T(1,128)S(1)} %get-tuple-element.29), channel_id=1, source_target_pairs={{0,1},{1,2},{2,3},{3,4},{4,5},{5,6},{6,7},{8,9},{9,10},{10,11},{11... | collective-permute-start | bytes 15368 | tf_op jit(solution)/shard_map/ppermute | solution.py:21
  10.9 5.5 %collective-permute-start.3 = (f32[10,1,128]{2,1,0:T(1,128)S(1)}, f32[10,1,128]{2,1,0:T(1,128)S(1)}, u32[]{:S(2)}, u32[]{:S(2)}) collective-permute-start(f32[10,1,128]{2,1,0:T(1,128)S(1)} %get-tuple-element.30), channel_id=1, source_target_pairs={{1,0},{2,1},{3,2},{4,3},{5,4},{6,5},{7,6},{9,8},{10,9},{11,10},{12... | collective-permute-start | bytes 15368 | tf_op jit(solution)/shard_map/ppermute | solution.py:24
  19.4 10.5 %copy-start.3 = (f32[32,128,128]{2,1,0:T(8,128)}, f32[32,128,128]{2,1,0:T(8,128)S(1)}, u32[]{:S(2)}) copy-start(f32[32,128,128]{2,1,0:T(8,128)S(1)} %get-tuple-element.8) | copy-start | bytes 6291460
  29.9 23.4 %copy-start.2 = (f32[32,128,512]{2,1,0:T(8,128)}, f32[32,128,512]{2,1,0:T(8,128)S(1)}, u32[]{:S(2)}) copy-start(f32[32,128,512]{2,1,0:T(8,128)S(1)} %fusion.6) | copy-start | bytes 25165828
  29.9 12.2 %copy-start.16 = (f32[3,3,512]{2,1,0:T(4,128)S(1)}, f32[3,3,512]{2,1,0:T(4,128)}, u32[]{:S(2)}) copy-start(f32[3,3,512]{2,1,0:T(4,128)} %param.18) | copy-start | bytes 55300
  29.9 4.3 %collective-permute-start.4 = (f32[1,128,512]{2,1,0:T(8,128)S(1)}, f32[1,128,512]{2,1,0:T(8,128)S(1)}, u32[]{:S(2)}, u32[]{:S(2)}) collective-permute-start(f32[1,128,512]{2,1,0:T(8,128)S(1)} %get-tuple-element.13), channel_id=1, source_target_pairs={{0,8},{8,16},{16,24},{24,32},{32,40},{40,48},{48,56},{56,64},{64,7... | collective-permute-start | bytes 786440 | tf_op jit(solution)/shard_map/ppermute | solution.py:21
  32.9 4.4 %collective-permute-start.5 = (f32[1,128,512]{2,1,0:T(8,128)S(1)}, f32[1,128,512]{2,1,0:T(8,128)S(1)}, u32[]{:S(2)}, u32[]{:S(2)}) collective-permute-start(f32[1,128,512]{2,1,0:T(8,128)S(1)} %get-tuple-element.14), channel_id=1, source_target_pairs={{8,0},{16,8},{24,16},{32,24},{40,32},{48,40},{56,48},{64,56},{72,6... | collective-permute-start | bytes 786440 | tf_op jit(solution)/shard_map/ppermute | solution.py:24
  37.4 5.3 %collective-permute-start.6 = (f32[34,1,512]{2,1,0:T(1,128)S(1)}, f32[34,1,512]{2,1,0:T(1,128)S(1)}, u32[]{:S(2)}, u32[]{:S(2)}) collective-permute-start(f32[34,1,512]{2,1,0:T(1,128)S(1)} %get-tuple-element.11), channel_id=1, source_target_pairs={{0,1},{1,2},{2,3},{3,4},{4,5},{5,6},{6,7},{8,9},{9,10},{10,11},{11... | collective-permute-start | bytes 208904 | tf_op jit(solution)/shard_map/ppermute | solution.py:21
  40.8 6.2 %collective-permute-start.7 = (f32[34,1,512]{2,1,0:T(1,128)S(1)}, f32[34,1,512]{2,1,0:T(1,128)S(1)}, u32[]{:S(2)}, u32[]{:S(2)}) collective-permute-start(f32[34,1,512]{2,1,0:T(1,128)S(1)} %get-tuple-element.12), channel_id=1, source_target_pairs={{1,0},{2,1},{3,2},{4,3},{5,4},{6,5},{7,6},{9,8},{10,9},{11,10},{12... | collective-permute-start | bytes 208904 | tf_op jit(solution)/shard_map/ppermute | solution.py:24
  53.3 102.3 %copy-start.14 = (f32[512,32]{0,1:T(8,128)S(1)}, f32[512,32]{0,1:T(8,128)}, u32[]{:S(2)}) copy-start(f32[512,32]{0,1:T(8,128)} %param.19) | copy-start | bytes 196612
  53.3 102.4 %copy-start.15 = (f32[32,512]{1,0:T(8,128)S(1)}, f32[32,512]{1,0:T(8,128)}, u32[]{:S(2)}) copy-start(f32[32,512]{1,0:T(8,128)} %param.20) | copy-start | bytes 196612
  53.3 102.6 %copy-start.11 = (f32[512,128]{1,0:T(8,128)S(1)}, f32[512,128]{1,0:T(8,128)}, u32[]{:S(2)}) copy-start(f32[512,128]{1,0:T(8,128)} %param.21) | copy-start | bytes 786436
  167.6 3.1 copy-start.10
  208.8 9.4 %copy-start.5 = (f32[4,16,8,8,128]{4,3,2,1,0:T(8,128)S(1)}, f32[4,16,8,8,128]{4,3,2,1,0:T(8,128)}, u32[]{:S(2)}) copy-start(f32[4,16,8,8,128]{4,3,2,1,0:T(8,128)} %copy.79) | copy-start | bytes 6291460
  208.8 9.4 %copy-start.12 = (f32[2,128,128]{2,1,0:T(8,128)S(1)}, f32[2,128,128]{2,1,0:T(8,128)}, u32[]{:S(2)}) copy-start(f32[2,128,128]{2,1,0:T(8,128)} %param.23) | copy-start | bytes 393220
  226.3 3.1 copy-start.9
  229.4 6.7 %copy-start.17 = (f32[2,512,128]{2,1,0:T(8,128)S(1)}, f32[2,512,128]{2,1,0:T(8,128)}, u32[]{:S(2)}) copy-start(f32[2,512,128]{2,1,0:T(8,128)} %param.25) | copy-start | bytes 1572868
  327.1 9.4 %copy-start.4 = (f32[2,2,16,8,8,128]{5,4,3,2,1,0:T(8,128)S(1)}, f32[2,2,16,8,8,128]{5,4,3,2,1,0:T(8,128)}, u32[]{:S(2)}) copy-start(f32[2,2,16,8,8,128]{5,4,3,2,1,0:T(8,128)} %copy.91) | copy-start | bytes 6291460
  327.1 9.4 %copy-start.13 = (f32[2,128,128]{2,1,0:T(8,128)S(1)}, f32[2,128,128]{2,1,0:T(8,128)}, u32[]{:S(2)}) copy-start(f32[2,128,128]{2,1,0:T(8,128)} %param.23) | copy-start | bytes 393220
  386.8 6.7 %copy-start.18 = (f32[2,512,128]{2,1,0:T(8,128)S(1)}, f32[2,512,128]{2,1,0:T(8,128)}, u32[]{:S(2)}) copy-start(f32[2,512,128]{2,1,0:T(8,128)} %param.25) | copy-start | bytes 1572868
  393.5 10.0 %copy-start.1 = (f32[128,512]{1,0:T(8,128)S(1)}, f32[128,512]{1,0:T(8,128)}, u32[]{:S(2)}) copy-start(f32[128,512]{1,0:T(8,128)} %param.17) | copy-start | bytes 786436
  (3 other events, 7.2 us)
where the time goes:
time: 407 us; the launch traced here: 404 us
  blocking collectives  150 us (37%)
  matrix products  129 us (32%)
  other arithmetic  52.6 us (13%)
  local copies, waits for them, and re-layouts  39.6 us (10%)
  starting transfers between devices  16.2 us (4%)
  waiting for transfers between devices  14.9 us (4%)
    psum x1, blocking collectives, per_device(): summed = lax.psum(jnp.sum(active, axis=(0, 1)), ('row', 'col'))  80.3 us
    all_to_all x1, blocking collectives, per_device(): lax.all_to_all(spread_out, ('row', 'col'), split_axis=3, concat_axis=2, t...  35.8 us
    all_to_all x1, blocking collectives, per_device(): lax.all_to_all(restored, ('row', 'col'), split_axis=2, concat_axis=3, til...  34.3 us
    dot_general x2, matrix products, attend(): jnp.einsum('nqhd,nkhd->nhqk', queries, keyed, precision=PRECISE)  32.9 us
    reduce_sum x1, other arithmetic, per_device(): summed = lax.psum(jnp.sum(active, axis=(0, 1)), ('row', 'col'))  22 us
    dot_general x2, matrix products, attend(): jnp.einsum('nhqk,nkhd->nqhd', weights, valued, precision=PRECISE)  18.7 us
    dot_general x2, matrix products, feed_forward(): jnp.einsum('hwf,fc->hwc', inner, weight_out, precision=PRECISE)  18.6 us
    ppermute x4, waiting for transfers between devices, extended(): lax.ppermute(lax.slice_in_dim(block, 0, width, axis=dim), axis, backward)  14.3 us
  transfers between devices with their start and end apart: 8, of which 5 were waited for; matrix products, arithmetic and copies ran while one was open for 0% of the time, Pallas kernels for 0%

commit v1 on v0

v1 whole, which is shorter than its diff:
```python
import math

import jax
import jax.numpy as jnp
import numpy as np
from jax import lax
from jax.experimental import pallas as pl
from jax.experimental.pallas import tpu as pltpu
from jax.sharding import Mesh
from jax.sharding import PartitionSpec as P

HEADS = 4
WINDOW = 8
CHANNELS = 128
EXPANDED = 512
MLP_HIDDEN = 512
SQUEEZE = 32
HEAD_DIM = CHANNELS // HEADS
CELLS = WINDOW * WINDOW
GROUP = 64
WIDE = 136
EPSILON = 1e-05
F32 = jnp.float32
BF16 = jnp.bfloat16
HIGHEST = lax.Precision.HIGHEST
CHUNKS = 2
STEP = 512
VMEM_LIMIT = 56 * 1024 * 1024

GELU_A = 2.0 * math.sqrt(2.0 / math.pi)
GELU_B = 4.0 * GELU_A * 0.044715


def gelu_of_half(half):
    return half * jnp.tanh(half * (GELU_A + GELU_B * (half * half))) + half


def split(x):
    high = x.astype(BF16)
    low = (x - high.astype(F32)).astype(BF16)
    return high, low


def dot(a, b):
    return jnp.dot(a, b, preferred_element_type=F32)


def rows_of(parts):
    return jnp.concatenate(parts, axis=0)


def lanes_of(parts):
    return jnp.concatenate(parts, axis=1)


def normed(x, gain):
    centre = jnp.mean(x, axis=-1, keepdims=True)
    shifted = x - centre
    spread = jnp.mean(shifted * shifted, axis=-1, keepdims=True)
    return shifted * lax.rsqrt(spread + EPSILON) * gain


def three(x):
    high, low = split(x)
    return lanes_of([high, low, high])


def stack_rows(weight):
    high, low = split(weight)
    return rows_of([high, high, low])


def deep_weight(weight):
    return lanes_of(split(weight))


def prepare_weights(qkv_ref, out_ref, in_ref, mlp_ref, k3, qv3, out3, in3, mlp_pair):
    scale = math.log2(math.e) / math.sqrt(HEAD_DIM)
    k3[...] = stack_rows(qkv_ref[0, :, CHANNELS : 2 * CHANNELS])
    turned = rows_of(
        [(qkv_ref[0, :, :CHANNELS] * scale).T, qkv_ref[0, :, 2 * CHANNELS :].T]
    )
    high, low = split(turned)
    qv3[...] = lanes_of([high, high, low])
    out3[...] = stack_rows(out_ref[0])
    in3[...] = stack_rows(0.5 * in_ref[0])
    mlp_pair[...] = deep_weight(mlp_ref[0])


PAIR = 2 * CELLS


def attention(pairs, gain, k3, qv3, out3):
    zero = jnp.zeros((HEAD_DIM, PAIR), F32)
    zero_block = jnp.zeros((2 * HEAD_DIM, PAIR), BF16)
    left = lax.broadcasted_iota(jnp.int32, (HEAD_DIM, PAIR), 1) < CELLS
    left_all = lax.broadcasted_iota(jnp.int32, (CHANNELS, PAIR), 1) < CELLS
    natural, turned = [], []
    for x in pairs:
        n = normed(x, gain)
        natural.append(three(n))
        high, low = split(n.T)
        turned.append(rows_of([high, low, high]))
    keys = dot(rows_of(natural), k3)
    both = dot(qv3, lanes_of(turned))
    scores = []
    for p in range(len(pairs)):
        key3 = three(keys[p * PAIR : (p + 1) * PAIR])
        query = both[:CHANNELS, p * PAIR : (p + 1) * PAIR]
        swapped = pltpu.roll(query, CELLS, 1)
        for second in range(2):
            here, there = (swapped, query) if second else (query, swapped)
            blocks_high, blocks_low = [], []
            for group in range(2):
                at = [slice(h * HEAD_DIM, (h + 1) * HEAD_DIM) for h in (2 * group, 2 * group + 1)]
                block = rows_of([jnp.where(left, here[at[0]], zero), jnp.where(left, zero, there[at[1]])])
                high, low = split(block)
                order = (lambda b: [b, zero_block]) if group == 0 else (lambda b: [zero_block, b])
                blocks_high.append(lanes_of(order(high)))
                blocks_low.append(lanes_of(order(low)))
            high, low = rows_of(blocks_high), rows_of(blocks_low)
            scores.append(dot(key3[second * CELLS : (second + 1) * CELLS], rows_of([high, high, low])))
    weights, scales = [], []
    for score in scores:
        weight = jnp.exp2(score - jnp.max(score, axis=0, keepdims=True))
        scales.append(1.0 / jnp.sum(weight, axis=0, keepdims=True))
        high, low = split(weight)
        weights.append(rows_of([high, high, low, low]))
    mixed = []
    for p in range(len(pairs)):
        value = both[CHANNELS:, p * PAIR : (p + 1) * PAIR]
        high = value.astype(BF16).astype(F32)
        low = pltpu.roll(value - high, CELLS, 1)
        first = jnp.where(left_all, high, low).astype(BF16)
        second = jnp.where(left_all, low, high).astype(BF16)
        mixed.append(dot(lanes_of([first, first]), weights[2 * p]))
        mixed.append(dot(lanes_of([second, second]), weights[2 * p + 1]))
    blended = []
    for p in range(len(pairs)):
        parts = []
        for h in range(HEADS):
            lanes = slice(128 * (h // 2), 128 * (h // 2) + 128)
            of_a, of_b = (
                mixed[2 * p + i][h * HEAD_DIM : (h + 1) * HEAD_DIM, lanes]
                * scales[2 * p + i][:, lanes]
                for i in range(2)
            )
            if h % 2:
                of_a = pltpu.roll(of_a, CELLS, 1)
            else:
                of_b = pltpu.roll(of_b, CELLS, 1)
            parts.append(jnp.where(left, of_a, of_b))
        blended.append(three(rows_of(parts).T))
    added = dot(rows_of(blended), out3)
    return [x + added[p * PAIR : (p + 1) * PAIR] for p, x in enumerate(pairs)]


def split_blocks(x, rows, make):
    highs, lows = [], []
    for r in range(0, x.shape[0], rows):
        made = [split(make(x[r : r + rows, c : c + 128])) for c in range(0, x.shape[1], 128)]
        highs.append(lanes_of([m[0] for m in made]))
        lows.append(lanes_of([m[1] for m in made]))
    return rows_of(highs), rows_of(lows)


def feed_forward(pairs, gain, in3, mlp_pair):
    inner = dot(rows_of([three(normed(x, gain)) for x in pairs]), in3)
    high, low = split_blocks(inner, 64, gelu_of_half)
    wide = dot(high, mlp_pair)
    rest = dot(low, mlp_pair[:, :CHANNELS])
    out = []
    for p, x in enumerate(pairs):
        at = slice(p * PAIR, (p + 1) * PAIR)
        out.append(x + (wide[at, :CHANNELS] + (wide[at, CHANNELS:] + rest[at])))
    return out


def column_weights():
    fine = np.zeros((WIDE, 40), np.float32)
    table = ((0.375, 0.625, 0.0), (0.125, 0.875, 0.0), (0.0, 0.875, 0.125), (0.0, 0.625, 0.375))

    def fill(at, column):
        k, o = column // 4, column % 4
        for step, weight in zip((-1, 0, 1), table[o]):
            if weight:
                fine[at, (k + step) % 40] = weight

    for column in range(129):
        fill(column, column)
    fill(135, -1)
    return np.concatenate([fine, fine], axis=1)


ROW_WEIGHTS = ((0.375, 0.625, -1), (0.125, 0.875, -1), (0.875, 0.125, 0), (0.625, 0.375, 0))


def lift_kernel(
    place_ref, field_ref, context_ref, above_ref, below_ref, before_ref, after_ref, up_ref,
    ctxw_ref, gains_ref, expand_ref, depth_ref, reduce_ref, lifted_ref, active_ref, sum_ref,
    lift, ctx, coarse, hid, expand3, total,
):
    step = pl.program_id(0)
    sublane = lax.broadcasted_iota(jnp.int32, (8, 128), 0)
    first_row, last_row = sublane == 0, sublane == 7

    @pl.when(step == 0)
    def _():
        expand3[...] = stack_rows(0.5 * expand_ref[...])
        total[...] = jnp.zeros_like(total)
        lift[0, :128] = above_ref[:128]
        lift[33, :128] = below_ref[:128]
        lift[1:33, :128] = field_ref[...]
        ctx[0, :32] = above_ref[128:]
        ctx[9, :32] = below_ref[128:]
        ctx[1:9, :32] = context_ref[...]
        zero = jnp.zeros((8, 128), F32)
        for e in range(44):
            after = jnp.broadcast_to(after_ref[e : e + 1], (8, 128))
            before = jnp.broadcast_to(before_ref[e : e + 1], (8, 128))
            group = jnp.where(first_row, after, jnp.where(last_row, before, zero))
            if e < 34:
                lift[e, 128:] = group
            else:
                ctx[e - 34, 32:] = group
        weight = stack_rows(ctxw_ref[...])
        projected = dot(three(ctx[...].reshape(400, CHANNELS)), weight)
        for k in range(10):
            high, low = split(projected[40 * k : 40 * k + 40])
            coarse[k] = dot(up_ref[...], rows_of([high, low]))

    has_after = jnp.where(place_ref[1] < 7, 1.0, 0.0)
    has_before = jnp.where(place_ref[1] > 0, 1.0, 0.0)
    inside = jnp.where(first_row, has_after, has_before)

    def hidden_rows(first, fine_first, k_first, count):
        parts = []
        for i in range(0, count, 2):
            two = []
            for j in (i, i + 1):
                k, o = (fine_first + j) // 4, (fine_first + j) % 4
                lower, upper, shift = ROW_WEIGHTS[o]
                at = k_first + k + shift
                x = lift[first + j] + (lower * coarse[at] + upper * coarse[at + 1])
                lift[first + j] = x
                two.append(x)
            parts.append(three(normed(rows_of(two), gains_ref[0:1])))
        made = dot(rows_of(parts), expand3[...])
        for i in range(count):
            for c in range(0, EXPANDED, 128):
                out = gelu_of_half(made[i * WIDE : (i + 1) * WIDE, c : c + 128])
                hid[first + i, :128, c : c + 128] = out[:128]
                hid[first + i, 128:, c : c + 128] = out[128:] * inside

    @pl.when(step == 0)
    def _():
        hidden_rows(0, -1, 1, 2)

        @pl.when(place_ref[0] == 0)
        def _():
            hid[0] = jnp.zeros((WIDE, EXPANDED), F32)

    hidden_rows(8 * step + 2, 1, 2 * step + 1, 4)
    hidden_rows(8 * step + 6, 5, 2 * step + 1, 4)

    @pl.when((step == 3) & (place_ref[0] == 15))
    def _():
        hid[33] = jnp.zeros((WIDE, EXPANDED), F32)

    lifted_ref[...] = lift[pl.ds(8 * step + 1, 8), :128]

    for part in range(EXPANDED // 128):
        lanes = slice(part * 128, (part + 1) * 128)
        taps = [
            [jnp.broadcast_to(0.5 * depth_ref[i, j : j + 1, lanes], (8, 128)) for j in range(3)]
            for i in range(3)
        ]

        def row(r, summed):
            def columns(g):
                seen = [hid[8 * step + r + i, 8 * g : 8 * g + 8, lanes] for i in range(3)]
                a, b, c = (
                    seen[0] * taps[0][j] + seen[1] * taps[1][j] + seen[2] * taps[2][j]
                    for j in range(3)
                )
                return pltpu.roll(a, 1, 0), b, pltpu.roll(c, 7, 0)

            halo = columns(16)
            held, here = halo[0], columns(0)
            for g in range(16):
                following = columns(g + 1) if g < 15 else halo
                out = gelu_of_half(
                    here[1]
                    + jnp.where(first_row, held, here[0])
                    + jnp.where(last_row, following[2], here[2])
                )
                active_ref[r, 8 * g : 8 * g + 8, lanes] = out
                summed = summed + out
                held, here = here[0], following
            return summed

        total[:, lanes] = lax.fori_loop(0, 8, row, total[:, lanes])

    @pl.when(step == 3)
    def _():
        squeezed = lax.dot_general(
            total[...], reduce_ref[...], (((1,), (1,)), ((), ())), precision=HIGHEST,
            preferred_element_type=F32,
        )
        squeezed = jnp.sum(squeezed, axis=0, keepdims=True)
        padded = lanes_of([squeezed, jnp.zeros((1, 128 - SQUEEZE), F32)])
        sum_ref[...] = jnp.broadcast_to(padded, sum_ref.shape)


def whole(shape):
    return pl.BlockSpec(shape, lambda *_: (0,) * len(shape))


def of_layer(array, layer):
    shape = (1,) + array.shape[1:]
    return pl.BlockSpec(shape, lambda *_: (layer,) + (0,) * (len(shape) - 1))


def lift_stage(place, args, copies):
    up = jnp.asarray(column_weights(), BF16)
    args = args[:6] + (up,) + args[6:]
    return pl.pallas_call(
        lift_kernel,
        grid=(4,),
        in_specs=[pl.BlockSpec(memory_space=pltpu.SMEM)] + [whole(a.shape) for a in args],
        out_specs=[
            pl.BlockSpec((8, 128, CHANNELS), lambda s: (s, 0, 0)),
            pl.BlockSpec((8, 128, EXPANDED), lambda s: (s, 0, 0)),
            whole((copies, 128)),
        ],
        out_shape=[
            jax.ShapeDtypeStruct((32, 128, CHANNELS), F32),
            jax.ShapeDtypeStruct((32, 128, EXPANDED), F32),
            jax.ShapeDtypeStruct((copies, 128), F32),
        ],
        scratch_shapes=[
            pltpu.VMEM((34, WIDE, CHANNELS), F32),
            pltpu.VMEM((10, 40, CHANNELS), F32),
            pltpu.VMEM((10, WIDE, CHANNELS), F32),
            pltpu.VMEM((34, WIDE, EXPANDED), F32),
            pltpu.VMEM((3 * CHANNELS, EXPANDED), BF16),
            pltpu.VMEM((8, EXPANDED), F32),
        ],
        compiler_params=pltpu.CompilerParams(vmem_limit_bytes=VMEM_LIMIT),
        cost_estimate=pl.CostEstimate(
            flops=8_000_000_000, bytes_accessed=14_000_000, transcendentals=0
        ),
    )(place, *args)


def block_kernel(
    cells_total, lifted_ref, active_ref, sums_ref, sexp_ref, project_ref, gains_ref, qkv_ref,
    aout_ref, min_ref, mout_ref, out_ref, project, *weights,
):
    @pl.when(pl.program_id(0) == 0)
    def _():
        pooled = jnp.sum(sums_ref[...], axis=0, keepdims=True) * (1.0 / cells_total)
        squeezed = pooled[:, :SQUEEZE]
        squeezed = squeezed * jax.nn.sigmoid(squeezed)
        wide = jnp.broadcast_to(squeezed, (CHANNELS, SQUEEZE))
        gate = jnp.dot(wide, sexp_ref[...], precision=HIGHEST, preferred_element_type=F32)
        project[...] = deep_weight(project_ref[...] * jax.nn.sigmoid(gate).T)
        prepare_weights(qkv_ref, aout_ref, min_ref, mout_ref, *weights)

    k3, qv3, out3, in3, mlp_pair = (w[...] for w in weights)
    highs, lows = [], []
    for w in range(STEP // CELLS):
        cells = active_ref[:, 8 * w : 8 * w + 8, :].reshape(CELLS, EXPANDED)
        high, low = split(cells)
        highs.append(high)
        lows.append(low)
    wide = dot(rows_of(highs), project[...])
    rest = dot(rows_of(lows), project[:, :CHANNELS])
    pairs = []
    for p in range(STEP // PAIR):
        at = slice(p * PAIR, (p + 1) * PAIR)
        x = rows_of(
            [lifted_ref[:, 8 * w : 8 * w + 8, :].reshape(CELLS, CHANNELS) for w in (2 * p, 2 * p + 1)]
        )
        pairs.append(x + (wide[at, :CHANNELS] + (wide[at, CHANNELS:] + rest[at])))
    pairs = attention(pairs, gains_ref[1:2], k3, qv3, out3)
    pairs = feed_forward(pairs, gains_ref[2:3], in3, mlp_pair)
    for p, x in enumerate(pairs):
        out_ref[p * PAIR : (p + 1) * PAIR] = x


WEIGHT_SCRATCH = [
    pltpu.VMEM((3 * CHANNELS, CHANNELS), BF16),
    pltpu.VMEM((2 * CHANNELS, 3 * CHANNELS), BF16),
    pltpu.VMEM((3 * CHANNELS, CHANNELS), BF16),
    pltpu.VMEM((3 * CHANNELS, MLP_HIDDEN), BF16),
    pltpu.VMEM((MLP_HIDDEN, 2 * CHANNELS), BF16),
]


def block_stage(chunk, lifted, active, sums, se_expand, project, gains, weights, cells_total):
    per_row = 128 // (STEP // 8)
    steps = 4 // CHUNKS * per_row
    row_base = chunk * (4 // CHUNKS)
    rest = (sums, se_expand, project, gains)

    def strip(channels):
        return pl.BlockSpec(
            (8, STEP // 8, channels), lambda s: (row_base + s // per_row, s % per_row, 0)
        )

    def body(*refs):
        block_kernel(cells_total, *refs)

    return pl.pallas_call(
        body,
        grid=(steps,),
        in_specs=[strip(CHANNELS), strip(EXPANDED)]
        + [whole(a.shape) for a in rest]
        + [of_layer(w, 0) for w in weights],
        out_specs=pl.BlockSpec((STEP, CHANNELS), lambda s: (s, 0)),
        out_shape=jax.ShapeDtypeStruct((steps * STEP, CHANNELS), F32),
        scratch_shapes=[pltpu.VMEM((EXPANDED, 2 * CHANNELS), BF16)] + WEIGHT_SCRATCH,
        compiler_params=pltpu.CompilerParams(vmem_limit_bytes=VMEM_LIMIT),
        cost_estimate=pl.CostEstimate(
            flops=14_000_000_000, bytes_accessed=8_000_000, transcendentals=0
        ),
    )(lifted, active, *rest, *weights)


def grid_kernel(x_ref, gains_ref, qkv_ref, aout_ref, min_ref, mout_ref, out_ref, *weights):
    @pl.when(pl.program_id(0) == 0)
    def _():
        prepare_weights(qkv_ref, aout_ref, min_ref, mout_ref, *weights)

    k3, qv3, out3, in3, mlp_pair = (w[...] for w in weights)
    flat_in = x_ref.reshape(STEP, CHANNELS)
    flat_out = out_ref.reshape(STEP, CHANNELS)
    windows = [flat_in[pl.ds(p, GROUP, stride=8), :] for p in range(8)]
    pairs = [rows_of(windows[i : i + 2]) for i in range(0, 8, 2)]
    pairs = attention(pairs, gains_ref[3:4], k3, qv3, out3)
    pairs = feed_forward(pairs, gains_ref[4:5], in3, mlp_pair)
    for p in range(8):
        flat_out[pl.ds(p, GROUP, stride=8), :] = pairs[p // 2][(p % 2) * GROUP : (p % 2 + 1) * GROUP]


def grid_stage(received, gains, weights):
    per_device = received.shape[1]
    block = pl.BlockSpec((GROUP, 8, CHANNELS), lambda s: (0, s, 0))
    return pl.pallas_call(
        grid_kernel,
        grid=(per_device // 8,),
        in_specs=[block, whole(gains.shape)] + [of_layer(w, 1) for w in weights],
        out_specs=block,
        out_shape=jax.ShapeDtypeStruct(received.shape, F32),
        scratch_shapes=WEIGHT_SCRATCH,
        compiler_params=pltpu.CompilerParams(vmem_limit_bytes=VMEM_LIMIT),
        cost_estimate=pl.CostEstimate(
            flops=14_000_000_000, bytes_accessed=4_000_000, transcendentals=0
        ),
    )(received, gains, *weights)


def neighbours(low_edge, high_edge, axis, count):
    forward = [(i, i + 1) for i in range(count - 1)]
    backward = [(i + 1, i) for i in range(count - 1)]
    return lax.ppermute(high_edge, axis, forward), lax.ppermute(low_edge, axis, backward)


def per_device(
    field, context, ctx_weight, norm_gains, expand_weight, depth_weight, se_reduce, se_expand,
    project_weight, attn_qkv, attn_out, mlp_in, mlp_out,
):
    row_axis = ("rg", "core")
    rows, cols = 16, 8
    row = lax.axis_index(row_axis)
    col = lax.axis_index("col")

    above, below = neighbours(
        jnp.concatenate([field[0], context[0]], axis=0),
        jnp.concatenate([field[-1], context[-1]], axis=0),
        row_axis,
        rows,
    )

    def edge(at, coarse_at):
        ends = [
            above[at : at + 1], field[:, at], below[at : at + 1],
            above[coarse_at : coarse_at + 1], context[:, coarse_at - 128],
            below[coarse_at : coarse_at + 1],
        ]
        return jnp.concatenate(ends, axis=0)

    before, after = neighbours(edge(0, 128), edge(127, 159), "col", cols)
    place = jnp.stack([row, col]).astype(jnp.int32)
    lifted, active, partial = lift_stage(
        place,
        (
            field, context, above, below, before, after, ctx_weight, norm_gains, expand_weight,
            depth_weight, se_reduce.T,
        ),
        rows,
    )

    def exchange(x, axes):
        return lax.all_to_all(x, axes, split_axis=0, concat_axis=0, tiled=True)

    partial = jnp.sum(exchange(partial[:, None, :], row_axis), axis=0, keepdims=True)
    sums = exchange(jnp.broadcast_to(partial, (cols, 1, 128)), "col")[:, 0, :]

    weights = (attn_qkv, attn_out, mlp_in, mlp_out)
    cells_total = rows * cols * field.shape[0] * field.shape[1]
    group = ("rg", "col")
    pieces = []
    for chunk in range(CHUNKS):
        mine = block_stage(
            chunk, lifted, active, sums, se_expand, project_weight, norm_gains, weights, cells_total
        )
        sent = exchange(mine.reshape(GROUP, -1, CHANNELS), group)
        back = exchange(grid_stage(sent, norm_gains, weights), group)
        windows = back.reshape(4 // CHUNKS, 16, WINDOW, WINDOW, CHANNELS)
        pieces.append(windows.transpose(0, 2, 1, 3, 4).reshape(-1, 128, CHANNELS))
    return jnp.concatenate(pieces, axis=0)


def solution(mesh):
    fine = Mesh(mesh.devices.reshape(8, 2, 8), ("rg", "core", "col"))
    tiled = P(("rg", "core"), "col", None)
    return jax.shard_map(
        per_device,
        mesh=fine,
        in_specs=(tiled, tiled) + (P(),) * 11,
        out_specs=tiled,
        check_vma=False,
    )
```

time: 407 us -> 180 us (0.44)
  matrix products: 129 us -> 0 us
  blocking collectives: 150 us -> 30.4 us
  Pallas kernels: 0 us -> 77.2 us
  other arithmetic: 52.6 us -> 2.1 us
  local copies, waits for them, and re-layouts: 39.6 us -> 4.72 us
  starting transfers between devices: 16.2 us -> 33.1 us
  waiting for transfers between devices: 14.9 us -> 31.8 us
    dot_general x17 -> x0, matrix products: 129 us -> none  [the longest x2 32.9 us: attend(): jnp.einsum('nqhd,nkhd->nhqk', queries, keyed, precision=PRECISE)]
    psum x1 -> x0, blocking collectives: 80.3 us -> none  [per_device(): summed = lax.psum(jnp.sum(active, axis=(0, 1)), ('row', 'col'))]
    pallas_call x0 -> x5, Pallas kernels: none -> 77.2 us  [the longest x2 29.9 us: block_stage(): pl.pallas_call(body, grid=(steps,), in_specs=[strip(CHANNELS), strip(EXPA...]
    reduce_sum x13 -> x1, other arithmetic: 39.8 us -> 0.03 us  [per_device(): jnp.sum(exchange(partial[:, None, :], row_axis), axis=0, keepdims=True)]
    all_to_all x2, blocking collectives: 70.1 us -> 30.4 us  [exchange(): return lax.all_to_all(x, axes, split_axis=0, concat_axis=0, tiled=True)]
    all_to_all x0 -> x4, waiting for transfers between devices: none -> 26 us  [exchange(): return lax.all_to_all(x, axes, split_axis=0, concat_axis=0, tiled=True)]
    all_to_all x0 -> x4, starting transfers between devices: none -> 25.8 us  [exchange(): return lax.all_to_all(x, axes, split_axis=0, concat_axis=0, tiled=True)]
    slice x11 -> x4, local copies, waits for them, and re-layouts: 26.8 us -> 1.79 us  [the longest x1 1 us: edge(): field[:, at]]
  transfers between devices with their start and end apart: 8 -> 8, of which waited for: 5 -> 6; matrix products, arithmetic and copies ran while one was open for 0% -> 2% of each run, Pallas kernels for 0% -> 23%
where the time goes in v1:
time: 180 us; the launch traced here: 179 us
  Pallas kernels  77.2 us (43%)
  starting transfers between devices  33.1 us (18%)
  waiting for transfers between devices  31.8 us (18%)
  blocking collectives  30.4 us (17%)
  local copies, waits for them, and re-layouts  4.72 us (3%)
  other arithmetic  2.1 us (1%)
    all_to_all x2, blocking collectives, exchange(): return lax.all_to_all(x, axes, split_axis=0, concat_axis=0, tiled=True)  30.4 us
    pallas_call x2, Pallas kernels, block_stage(): pl.pallas_call(body, grid=(steps,), in_specs=[strip(CHANNELS), strip(EXPA...  29.9 us
    pallas_call x2, Pallas kernels, grid_stage(): pl.pallas_call(grid_kernel, grid=(per_device // 8,), in_specs=[block, who...  26.3 us
    all_to_all x4, waiting for transfers between devices, exchange(): return lax.all_to_all(x, axes, split_axis=0, concat_axis=0, tiled=True)  26 us
    all_to_all x4, starting transfers between devices, exchange(): return lax.all_to_all(x, axes, split_axis=0, concat_axis=0, tiled=True)  25.8 us
    pallas_call x1, Pallas kernels, lift_stage(): pl.pallas_call(lift_kernel, grid=(4,), in_specs=[pl.BlockSpec(memory_spac...  21 us
    ppermute x2, waiting for transfers between devices, neighbours(): lax.ppermute(low_edge, axis, backward)  5.78 us
    ppermute x2, starting transfers between devices, neighbours(): lax.ppermute(high_edge, axis, forward)  4.68 us
  transfers between devices with their start and end apart: 8, of which 6 were waited for; matrix products, arithmetic and copies ran while one was open for 2% of the time, Pallas kernels for 23%

profile of v1, /device:TPU:0, one launch (start us, length us, event | category | flops | bytes accessed | tf_op | source)
XLA Modules:
  0.0 179.5 jit_solution(10413179245891116879)
XLA Ops:
  0.7 0.9 slice_bitcast_fusion
  1.6 1.3 collective-permute-start
  3.0 1.3 collective-permute-start.1
  4.3 1.0 fusion
  6.1 1.9 %collective-permute-done.1.below_ref = f32[160,128]{1,0:T(8,128)S(1)} collective-permute-done((f32[160,128]{1,0:T(8,128)S(1)}, f32[160,128]{1,0:T(8,128)S(1)}, u32[]{:S(2)}, u32[]{:S(2)}) %collective-permute-start.1) | collective-permute-done | bytes 81952 | tf_op jit(solution)/shard_map/ppermute | solution.py:467
  8.3 3.4 %collective-permute-start.2 = (f32[44,128]{1,0:T(8,128)S(1)}, f32[44,128]{1,0:T(8,128)S(1)}, u32[]{:S(2)}, u32[]{:S(2)}) collective-permute-start(f32[44,128]{1,0:T(8,128)S(1)} %concatenate.17), channel_id=1, source_target_pairs={{0,1},{1,2},{2,3},{3,4},{4,5},{5,6},{6,7},{8,9},{9,10},{10,11},{11... | collective-permute-start | bytes 67592 | tf_op jit(solution)/shard_map/ppermute | solution.py:467
  11.9 1.3 collective-permute-start.3
  13.8 3.8 %collective-permute-done.3.after_ref = f32[44,128]{1,0:T(8,128)S(1)} collective-permute-done((f32[44,128]{1,0:T(8,128)S(1)}, f32[44,128]{1,0:T(8,128)S(1)}, u32[]{:S(2)}, u32[]{:S(2)}) %collective-permute-start.3) | collective-permute-done | bytes 22560 | tf_op jit(solution)/shard_map/ppermute | solution.py:467
  18.2 21.0 %shard_map.136 = (f32[32,128,128]{2,1,0:T(8,128)}, f32[32,128,512]{2,1,0:T(8,128)}, f32[16,128]{1,0:T(8,128)}) custom-call(s32[2]{0:T(128)} %pad_add_fusion.place_ref, f32[32,128,128]{2,1,0:T(8,128)} %field_ref.1, f32[8,32,128]{2,1,0:T(8,128)} %context_ref.1, f32[160,128]{1,0:T(8,128)} %copy-done.2, f32[160,128]{1,0:T(8,128)} %copy-done.3, ...), custom_call_target="tpu_custom_call" | custom-call | flops 8000000000 | bytes 14000000 | tf_op jit(solution)/shard_map/pallas_call | solution.py:327
  39.2 18.8 %all_to_all.30 = f32[16,1,128]{2,1,0:T(1,128)S(1)} all-to-all(f32[16,1,128]{2,1,0:T(1,128)} %bitcast.47), channel_id=1, replica_groups=mesh['rg'=8,'core'=2,'col'=8] {'rg','core'}, dimensions={0} | all-to-all | bytes 16384 | tf_op jit(solution)/shard_map/all_to_all | solution.py:506
  58.0 11.6 %all_to_all.31 = f32[8,1,128]{2,1,0:T(1,128)} all-to-all(f32[8,1,128]{2,1,0:T(1,128)S(1)} %broadcast_in_dim.10), channel_id=1, replica_groups=mesh['rg'=8,'core'=2,'col'=8] {'col'}, dimensions={0} | all-to-all | bytes 8192 | tf_op jit(solution)/shard_map/all_to_all | solution.py:506
  69.7 15.0 %shard_map.139 = f32[2048,128]{1,0:T(8,128)} custom-call(f32[32,128,128]{2,1,0:T(8,128)} %get-tuple-element.8.refs_0_, f32[32,128,512]{2,1,0:T(8,128)} %get-tuple-element.9.refs_1_, f32[8,128]{1,0:T(8,128)} %bitcast.48, f32[32,512]{1,0:T(8,128)} %refs_3_.3, f32[512,128]{1,0:T(8,128)} %refs_4_.3, f32[5,128]{1,0:T(8,128)} %gains_ref.5, ...), custom_call_target="tpu_custom_call" | custom-call | flops 14000000000 | bytes 8000000 | tf_op jit(solution)/shard_map/pallas_call | solution.py:415
  84.7 4.7 %all-to-all-start.4 = ((f32[64,32,128]{2,1,0:T(8,128)}), f32[64,32,128]{2,1,0:T(8,128)S(1)}, u32[]{:S(2)}, u32[]{:S(2)}) async-start(f32[64,32,128]{2,1,0:T(8,128)} %bitcast.42), calls=%async_computation.4 | async-start | bytes 2097152 | tf_op jit(solution)/shard_map/all_to_all | solution.py:506
  89.3 15.0 %shard_map.137 = f32[2048,128]{1,0:T(8,128)} custom-call(f32[32,128,128]{2,1,0:T(8,128)} %get-tuple-element.8.refs_0_, f32[32,128,512]{2,1,0:T(8,128)} %get-tuple-element.9.refs_1_, f32[8,128]{1,0:T(8,128)} %bitcast.49, f32[32,512]{1,0:T(8,128)} %refs_3_.3, f32[512,128]{1,0:T(8,128)} %refs_4_.3, f32[5,128]{1,0:T(8,128)} %gains_ref.5, ...), custom_call_target="tpu_custom_call" | custom-call | flops 14000000000 | bytes 8000000 | tf_op jit(solution)/shard_map/pallas_call | solution.py:415
  104.3 2.7 %all-to-all-done.4.x_ref = f32[64,32,128]{2,1,0:T(8,128)S(1)} async-done(((f32[64,32,128]{2,1,0:T(8,128)}), f32[64,32,128]{2,1,0:T(8,128)S(1)}, u32[]{:S(2)}, u32[]{:S(2)}) %all-to-all-start.4) | async-done | bytes 1048608 | tf_op jit(solution)/shard_map/all_to_all | solution.py:506
  107.0 7.9 %all-to-all-start.2 = ((f32[64,32,128]{2,1,0:T(8,128)}), f32[64,32,128]{2,1,0:T(8,128)S(1)}, u32[]{:S(2)}, u32[]{:S(2)}) async-start(f32[64,32,128]{2,1,0:T(8,128)} %bitcast.41), calls=%async_computation.2 | async-start | bytes 2097152 | tf_op jit(solution)/shard_map/all_to_all | solution.py:506
  114.9 13.1 %shard_map.140 = f32[64,32,128]{2,1,0:T(8,128)} custom-call(f32[64,32,128]{2,1,0:T(8,128)} %copy-done, f32[5,128]{1,0:T(8,128)} %gains_ref.5, f32[2,128,384]{2,1,0:T(8,128)} %qkv_ref.3, f32[2,128,128]{2,1,0:T(8,128)} %aout_ref.3, f32[2,128,512]{2,1,0:T(8,128)} %min_ref.3, f32[2,512,128]{2,1,0:T(8,128)} %mout_ref.3), custom_call_target="tpu_custom_call" | custom-call | flops 14000000000 | bytes 4000000 | tf_op jit(solution)/shard_map/pallas_call | solution.py:450
  128.0 3.9 %all-to-all-done.2.x_ref = f32[64,32,128]{2,1,0:T(8,128)S(1)} async-done(((f32[64,32,128]{2,1,0:T(8,128)}), f32[64,32,128]{2,1,0:T(8,128)S(1)}, u32[]{:S(2)}, u32[]{:S(2)}) %all-to-all-start.2) | async-done | bytes 1048608 | tf_op jit(solution)/shard_map/all_to_all | solution.py:506
  131.9 6.4 %all-to-all-start.5 = ((f32[64,32,128]{2,1,0:T(8,128)}), f32[64,32,128]{2,1,0:T(8,128)S(1)}, u32[]{:S(2)}, u32[]{:S(2)}) async-start(f32[64,32,128]{2,1,0:T(8,128)} %shard_map.140), calls=%async_computation.5 | async-start | bytes 2097152 | tf_op jit(solution)/shard_map/all_to_all | solution.py:506
  138.3 13.1 %shard_map.138 = f32[64,32,128]{2,1,0:T(8,128)} custom-call(f32[64,32,128]{2,1,0:T(8,128)} %copy-done.1, f32[5,128]{1,0:T(8,128)} %gains_ref.5, f32[2,128,384]{2,1,0:T(8,128)} %qkv_ref.3, f32[2,128,128]{2,1,0:T(8,128)} %aout_ref.3, f32[2,128,512]{2,1,0:T(8,128)} %min_ref.3, f32[2,512,128]{2,1,0:T(8,128)} %mout_ref.3), custom_call_target="tpu_custom_call" | custom-call | flops 14000000000 | bytes 4000000 | tf_op jit(solution)/shard_map/pallas_call | solution.py:450
  151.4 3.5 %all-to-all-done.5 = f32[64,32,128]{2,1,0:T(8,128)S(1)} async-done(((f32[64,32,128]{2,1,0:T(8,128)}), f32[64,32,128]{2,1,0:T(8,128)S(1)}, u32[]{:S(2)}, u32[]{:S(2)}) %all-to-all-start.5) | async-done | bytes 1048608 | tf_op jit(solution)/shard_map/all_to_all | solution.py:506
  154.9 6.9 %all-to-all-start.3 = ((f32[64,32,128]{2,1,0:T(8,128)}), f32[64,32,128]{2,1,0:T(8,128)S(1)}, u32[]{:S(2)}, u32[]{:S(2)}) async-start(f32[64,32,128]{2,1,0:T(8,128)} %shard_map.138), calls=%async_computation.3 | async-start | bytes 2097152 | tf_op jit(solution)/shard_map/all_to_all | solution.py:506
  161.9 16.0 %all-to-all-done.3 = f32[64,32,128]{2,1,0:T(8,128)S(1)} async-done(((f32[64,32,128]{2,1,0:T(8,128)}), f32[64,32,128]{2,1,0:T(8,128)S(1)}, u32[]{:S(2)}, u32[]{:S(2)}) %all-to-all-start.3) | async-done | bytes 1048608 | tf_op jit(solution)/shard_map/all_to_all | solution.py:506
  178.0 1.5 pad_maximum_fusion
  (27 shorter events, 3.5 us)
Async XLA Ops:
  1.6 4.4 %collective-permute-start = (f32[160,128]{1,0:T(8,128)S(1)}, f32[160,128]{1,0:T(8,128)S(1)}, u32[]{:S(2)}, u32[]{:S(2)}) collective-permute-start(f32[160,128]{1,0:T(8,128)S(1)} %pad_maximum_fusion.1), channel_id=1, source_target_pairs={{0,8},{8,16},{16,24},{24,32},{32,40},{40,48},{48,56},{56,64},{64,7... | collective-permute-start | bytes 245768 | tf_op jit(solution)/shard_map/ppermute | solution.py:467
  3.0 5.1 %collective-permute-start.1 = (f32[160,128]{1,0:T(8,128)S(1)}, f32[160,128]{1,0:T(8,128)S(1)}, u32[]{:S(2)}, u32[]{:S(2)}) collective-permute-start(f32[160,128]{1,0:T(8,128)S(1)} %pad_maximum_fusion.2), channel_id=1, source_target_pairs={{8,0},{16,8},{24,16},{32,24},{40,32},{48,40},{56,48},{64,56},{72,6... | collective-permute-start | bytes 245768 | tf_op jit(solution)/shard_map/ppermute | solution.py:467
  6.0 11.6 %copy-start.2 = (f32[160,128]{1,0:T(8,128)}, f32[160,128]{1,0:T(8,128)S(1)}, u32[]{:S(2)}) copy-start(f32[160,128]{1,0:T(8,128)S(1)} %collective-permute-done.above_ref) | copy-start | bytes 245764
  8.0 9.6 %copy-start.3 = (f32[160,128]{1,0:T(8,128)}, f32[160,128]{1,0:T(8,128)S(1)}, u32[]{:S(2)}) copy-start(f32[160,128]{1,0:T(8,128)S(1)} %collective-permute-done.1.below_ref) | copy-start | bytes 245764
  8.3 5.5 %collective-permute-start.2 = (f32[44,128]{1,0:T(8,128)S(1)}, f32[44,128]{1,0:T(8,128)S(1)}, u32[]{:S(2)}, u32[]{:S(2)}) collective-permute-start(f32[44,128]{1,0:T(8,128)S(1)} %concatenate.17), channel_id=1, source_target_pairs={{0,1},{1,2},{2,3},{3,4},{4,5},{5,6},{6,7},{8,9},{9,10},{10,11},{11... | collective-permute-start | bytes 67592 | tf_op jit(solution)/shard_map/ppermute | solution.py:467
  11.9 5.7 %collective-permute-start.3 = (f32[44,128]{1,0:T(8,128)S(1)}, f32[44,128]{1,0:T(8,128)S(1)}, u32[]{:S(2)}, u32[]{:S(2)}) collective-permute-start(f32[44,128]{1,0:T(8,128)S(1)} %concatenate.18), channel_id=1, source_target_pairs={{1,0},{2,1},{3,2},{4,3},{5,4},{6,5},{7,6},{9,8},{10,9},{11,10},{12... | collective-permute-start | bytes 67592 | tf_op jit(solution)/shard_map/ppermute | solution.py:467
  13.8 3.8 %copy-start.4 = (f32[44,128]{1,0:T(8,128)}, f32[44,128]{1,0:T(8,128)S(1)}, u32[]{:S(2)}) copy-start(f32[44,128]{1,0:T(8,128)S(1)} %collective-permute-done.2.before_ref) | copy-start | bytes 67588
  17.6 0.6 copy-start.5
  84.7 22.4 %all-to-all-start.4 = ((f32[64,32,128]{2,1,0:T(8,128)}), f32[64,32,128]{2,1,0:T(8,128)S(1)}, u32[]{:S(2)}, u32[]{:S(2)}) async-start(f32[64,32,128]{2,1,0:T(8,128)} %bitcast.42), calls=%async_computation.4 | async-start | bytes 2097152 | tf_op jit(solution)/shard_map/all_to_all | solution.py:506
  107.0 7.9 %copy-start = (f32[64,32,128]{2,1,0:T(8,128)}, f32[64,32,128]{2,1,0:T(8,128)S(1)}, u32[]{:S(2)}) copy-start(f32[64,32,128]{2,1,0:T(8,128)S(1)} %all-to-all-done.4.x_ref) | copy-start | bytes 3145732
  107.0 24.9 %all-to-all-start.2 = ((f32[64,32,128]{2,1,0:T(8,128)}), f32[64,32,128]{2,1,0:T(8,128)S(1)}, u32[]{:S(2)}, u32[]{:S(2)}) async-start(f32[64,32,128]{2,1,0:T(8,128)} %bitcast.41), calls=%async_computation.2 | async-start | bytes 2097152 | tf_op jit(solution)/shard_map/all_to_all | solution.py:506
  131.9 6.4 %copy-start.1 = (f32[64,32,128]{2,1,0:T(8,128)}, f32[64,32,128]{2,1,0:T(8,128)S(1)}, u32[]{:S(2)}) copy-start(f32[64,32,128]{2,1,0:T(8,128)S(1)} %all-to-all-done.2.x_ref) | copy-start | bytes 3145732
  131.9 23.0 %all-to-all-start.5 = ((f32[64,32,128]{2,1,0:T(8,128)}), f32[64,32,128]{2,1,0:T(8,128)S(1)}, u32[]{:S(2)}, u32[]{:S(2)}) async-start(f32[64,32,128]{2,1,0:T(8,128)} %shard_map.140), calls=%async_computation.5 | async-start | bytes 2097152 | tf_op jit(solution)/shard_map/all_to_all | solution.py:506
  154.9 23.0 %all-to-all-start.3 = ((f32[64,32,128]{2,1,0:T(8,128)}), f32[64,32,128]{2,1,0:T(8,128)S(1)}, u32[]{:S(2)}, u32[]{:S(2)}) async-start(f32[64,32,128]{2,1,0:T(8,128)} %shard_map.138), calls=%async_computation.3 | async-start | bytes 2097152 | tf_op jit(solution)/shard_map/all_to_all | solution.py:506

commit v2 on v1

--- a/solution.py
+++ b/solution.py
@@ -60,6 +60,13 @@
     return shifted * lax.rsqrt(spread + EPSILON) * gain
 
 
+def normed_by_product(x, gain):
+    averaging = jnp.full((2 * CHANNELS, CHANNELS), 1.0 / CHANNELS, BF16)
+    shifted = x - dot(lanes_of(split(x)), averaging)
+    spread = dot(lanes_of(split(shifted * shifted)), averaging)
+    return shifted * lax.rsqrt(spread + EPSILON) * gain
+
+
 def three(x):
     high, low = split(x)
     return lanes_of([high, low, high])
@@ -88,22 +95,27 @@
 
 
 PAIR = 2 * CELLS
-
-
-def attention(pairs, gain, k3, qv3, out3):
+PART = 256
+
+
+def attend_and_feed(pairs, gains, k3, qv3, out3, in3, mlp_pair, finish):
     zero = jnp.zeros((HEAD_DIM, PAIR), F32)
     zero_block = jnp.zeros((2 * HEAD_DIM, PAIR), BF16)
     left = lax.broadcasted_iota(jnp.int32, (HEAD_DIM, PAIR), 1) < CELLS
     left_all = lax.broadcasted_iota(jnp.int32, (CHANNELS, PAIR), 1) < CELLS
+    if not isinstance(pairs, list):
+        pairs = yield from pairs
     natural, turned = [], []
     for x in pairs:
-        n = normed(x, gain)
+        n = normed(x, gains[0])
         natural.append(three(n))
         high, low = split(n.T)
         turned.append(rows_of([high, low, high]))
-    keys = dot(rows_of(natural), k3)
-    both = dot(qv3, lanes_of(turned))
-    scores = []
+    yield
+    keys = dot(rows_of(natural), k3[...])
+    both = dot(qv3[...], lanes_of(turned))
+    yield
+    sides, value_sides = [], []
     for p in range(len(pairs)):
         key3 = three(keys[p * PAIR : (p + 1) * PAIR])
         query = both[:CHANNELS, p * PAIR : (p + 1) * PAIR]
@@ -113,28 +125,31 @@
             blocks_high, blocks_low = [], []
             for group in range(2):
                 at = [slice(h * HEAD_DIM, (h + 1) * HEAD_DIM) for h in (2 * group, 2 * group + 1)]
-                block = rows_of([jnp.where(left, here[at[0]], zero), jnp.where(left, zero, there[at[1]])])
-                high, low = split(block)
+                block = [jnp.where(left, here[at[0]], zero), jnp.where(left, zero, there[at[1]])]
+                high, low = split(rows_of(block))
                 order = (lambda b: [b, zero_block]) if group == 0 else (lambda b: [zero_block, b])
                 blocks_high.append(lanes_of(order(high)))
                 blocks_low.append(lanes_of(order(low)))
             high, low = rows_of(blocks_high), rows_of(blocks_low)
-            scores.append(dot(key3[second * CELLS : (second + 1) * CELLS], rows_of([high, high, low])))
+            sides.append((key3[second * CELLS : (second + 1) * CELLS], rows_of([high, high, low])))
+        value = both[CHANNELS:, p * PAIR : (p + 1) * PAIR]
+        high = value.astype(BF16).astype(F32)
+        low = pltpu.roll(value - high, CELLS, 1)
+        first = jnp.where(left_all, high, low).astype(BF16)
+        second = jnp.where(left_all, low, high).astype(BF16)
+        value_sides += [lanes_of([first, first]), lanes_of([second, second])]
+    yield
+    scores = [dot(key, query) for key, query in sides]
+    yield
     weights, scales = [], []
     for score in scores:
         weight = jnp.exp2(score - jnp.max(score, axis=0, keepdims=True))
         scales.append(1.0 / jnp.sum(weight, axis=0, keepdims=True))
         high, low = split(weight)
         weights.append(rows_of([high, high, low, low]))
-    mixed = []
-    for p in range(len(pairs)):
-        value = both[CHANNELS:, p * PAIR : (p + 1) * PAIR]
-        high = value.astype(BF16).astype(F32)
-        low = pltpu.roll(value - high, CELLS, 1)
-        first = jnp.where(left_all, high, low).astype(BF16)
-        second = jnp.where(left_all, low, high).astype(BF16)
-        mixed.append(dot(lanes_of([first, first]), weights[2 * p]))
-        mixed.append(dot(lanes_of([second, second]), weights[2 * p + 1]))
+    yield
+    mixed = [dot(value, weight) for value, weight in zip(value_sides, weights)]
+    yield
     blended = []
     for p in range(len(pairs)):
         parts = []
@@ -151,8 +166,34 @@
                 of_b = pltpu.roll(of_b, CELLS, 1)
             parts.append(jnp.where(left, of_a, of_b))
         blended.append(three(rows_of(parts).T))
-    added = dot(rows_of(blended), out3)
-    return [x + added[p * PAIR : (p + 1) * PAIR] for p, x in enumerate(pairs)]
+    yield
+    added = dot(rows_of(blended), out3[...])
+    yield
+    pairs = [x + added[p * PAIR : (p + 1) * PAIR] for p, x in enumerate(pairs)]
+    parts = [three(normed(x, gains[1])) for x in pairs]
+    yield
+    inner = dot(rows_of(parts), in3[...])
+    yield
+    high, low = split_blocks(inner, 64, gelu_of_half)
+    yield
+    wide = dot(high, mlp_pair[...])
+    rest = dot(low, mlp_pair[:, :CHANNELS])
+    yield
+    for p, x in enumerate(pairs):
+        at = slice(p * PAIR, (p + 1) * PAIR)
+        finish(p, x + (wide[at, :CHANNELS] + (wide[at, CHANNELS:] + rest[at])))
+
+
+def staggered(groups):
+    waiting, running = list(groups), []
+    while waiting or running:
+        if waiting:
+            running.append(waiting.pop(0))
+        for group in list(running):
+            try:
+                next(group)
+            except StopIteration:
+                running.remove(group)
 
 
 def split_blocks(x, rows, make):
@@ -162,18 +203,6 @@
         highs.append(lanes_of([m[0] for m in made]))
         lows.append(lanes_of([m[1] for m in made]))
     return rows_of(highs), rows_of(lows)
-
-
-def feed_forward(pairs, gain, in3, mlp_pair):
-    inner = dot(rows_of([three(normed(x, gain)) for x in pairs]), in3)
-    high, low = split_blocks(inner, 64, gelu_of_half)
-    wide = dot(high, mlp_pair)
-    rest = dot(low, mlp_pair[:, :CHANNELS])
-    out = []
-    for p, x in enumerate(pairs):
-        at = slice(p * PAIR, (p + 1) * PAIR)
-        out.append(x + (wide[at, :CHANNELS] + (wide[at, CHANNELS:] + rest[at])))
-    return out
 
 
 def column_weights():
@@ -244,7 +273,7 @@
                 x = lift[first + j] + (lower * coarse[at] + upper * coarse[at + 1])
                 lift[first + j] = x
                 two.append(x)
-            parts.append(three(normed(rows_of(two), gains_ref[0:1])))
+            parts.append(three(normed_by_product(rows_of(two), gains_ref[0:1])))
         made = dot(rows_of(parts), expand3[...])
         for i in range(count):
             for c in range(0, EXPANDED, 128):
@@ -260,8 +289,11 @@
         def _():
             hid[0] = jnp.zeros((WIDE, EXPANDED), F32)
 
-    hidden_rows(8 * step + 2, 1, 2 * step + 1, 4)
-    hidden_rows(8 * step + 6, 5, 2 * step + 1, 4)
+    def four_hidden(t, carry):
+        hidden_rows(8 * step + 2 + 4 * t, 1, 2 * step + 1 + t, 4)
+        return carry
+
+    lax.fori_loop(0, 2, four_hidden, 0)
 
     @pl.when((step == 3) & (place_ref[0] == 15))
     def _():
@@ -299,7 +331,12 @@
                 held, here = here[0], following
             return summed
 
-        total[:, lanes] = lax.fori_loop(0, 8, row, total[:, lanes])
+        def four_rows(t, summed):
+            for i in range(4):
+                summed = row(4 * t + i, summed)
+            return summed
+
+        total[:, lanes] = lax.fori_loop(0, 2, four_rows, total[:, lanes])
 
     @pl.when(step == 3)
     def _():
@@ -367,26 +404,37 @@
         project[...] = deep_weight(project_ref[...] * jax.nn.sigmoid(gate).T)
         prepare_weights(qkv_ref, aout_ref, min_ref, mout_ref, *weights)
 
-    k3, qv3, out3, in3, mlp_pair = (w[...] for w in weights)
-    highs, lows = [], []
-    for w in range(STEP // CELLS):
-        cells = active_ref[:, 8 * w : 8 * w + 8, :].reshape(CELLS, EXPANDED)
-        high, low = split(cells)
-        highs.append(high)
-        lows.append(low)
-    wide = dot(rows_of(highs), project[...])
-    rest = dot(rows_of(lows), project[:, :CHANNELS])
-    pairs = []
-    for p in range(STEP // PAIR):
-        at = slice(p * PAIR, (p + 1) * PAIR)
-        x = rows_of(
-            [lifted_ref[:, 8 * w : 8 * w + 8, :].reshape(CELLS, CHANNELS) for w in (2 * p, 2 * p + 1)]
-        )
-        pairs.append(x + (wide[at, :CHANNELS] + (wide[at, CHANNELS:] + rest[at])))
-    pairs = attention(pairs, gains_ref[1:2], k3, qv3, out3)
-    pairs = feed_forward(pairs, gains_ref[2:3], in3, mlp_pair)
-    for p, x in enumerate(pairs):
-        out_ref[p * PAIR : (p + 1) * PAIR] = x
+    def cells_of(ref, w, channels):
+        at = pl.ds(pl.multiple_of(8 * w, 8), 8)
+        return ref[:, at, :].reshape(CELLS, channels)
+
+    def projected(start):
+        highs, lows = [], []
+        for w in range(PART // CELLS):
+            high, low = split(cells_of(active_ref, start + w, EXPANDED))
+            highs.append(high)
+            lows.append(low)
+        yield
+        wide = dot(rows_of(highs), project[...])
+        rest = dot(rows_of(lows), project[:, :CHANNELS])
+        yield
+        pairs = []
+        for p in range(PART // PAIR):
+            at = slice(p * PAIR, (p + 1) * PAIR)
+            x = rows_of([cells_of(lifted_ref, start + 2 * p + i, CHANNELS) for i in range(2)])
+            pairs.append(x + (wide[at, :CHANNELS] + (wide[at, CHANNELS:] + rest[at])))
+        return pairs
+
+    def group(part, carry):
+        def finish(p, x):
+            out_ref[pl.ds(pl.multiple_of(part * PART + p * PAIR, PAIR), PAIR)] = x
+
+        both_gains = (gains_ref[1:2], gains_ref[2:3])
+        start = part * (PART // CELLS)
+        staggered([attend_and_feed(projected(start), both_gains, *weights, finish)])
+        return carry
+
+    lax.fori_loop(0, STEP // PART, group, 0)
 
 
 WEIGHT_SCRATCH = [
@@ -428,37 +476,54 @@
     )(lifted, active, *rest, *weights)
 
 
-def grid_kernel(x_ref, gains_ref, qkv_ref, aout_ref, min_ref, mout_ref, out_ref, *weights):
+def grid_kernel(x_ref, gains_ref, qkv_ref, aout_ref, min_ref, mout_ref, *rest):
+    out_ref, *weights = rest[-6:]
+
     @pl.when(pl.program_id(0) == 0)
     def _():
         prepare_weights(qkv_ref, aout_ref, min_ref, mout_ref, *weights)
 
-    k3, qv3, out3, in3, mlp_pair = (w[...] for w in weights)
     flat_in = x_ref.reshape(STEP, CHANNELS)
     flat_out = out_ref.reshape(STEP, CHANNELS)
-    windows = [flat_in[pl.ds(p, GROUP, stride=8), :] for p in range(8)]
-    pairs = [rows_of(windows[i : i + 2]) for i in range(0, 8, 2)]
-    pairs = attention(pairs, gains_ref[3:4], k3, qv3, out3)
-    pairs = feed_forward(pairs, gains_ref[4:5], in3, mlp_pair)
-    for p in range(8):
-        flat_out[pl.ds(p, GROUP, stride=8), :] = pairs[p // 2][(p % 2) * GROUP : (p % 2 + 1) * GROUP]
-
-
-def grid_stage(received, gains, weights):
+
+    def group(part, carry):
+        first = part * 2
+        pairs = [rows_of([flat_in[pl.ds(first + p, GROUP, stride=8), :] for p in range(2)])]
+
+        def finish(p, x):
+            for i in range(2):
+                flat_out[pl.ds(first + i, GROUP, stride=8), :] = x[i * GROUP : (i + 1) * GROUP]
+
+        staggered([attend_and_feed(pairs, (gains_ref[3:4], gains_ref[4:5]), *weights, finish)])
+        return carry
+
+    lax.fori_loop(0, 4, group, 0)
+
+
+def grid_stage(received, gains, weights, chunk, earlier):
     per_device = received.shape[1]
-    block = pl.BlockSpec((GROUP, 8, CHANNELS), lambda s: (0, s, 0))
+    steps = per_device // 8
+    in_specs = [pl.BlockSpec((GROUP, 8, CHANNELS), lambda s: (0, s, 0)), whole(gains.shape)]
+    in_specs += [of_layer(w, 1) for w in weights]
+    args = (received, gains) + weights
+    aliases = {}
+    if earlier is not None:
+        in_specs.append(pl.BlockSpec(memory_space=pl.ANY))
+        aliases = {len(args): 0}
+        args += (earlier,)
     return pl.pallas_call(
         grid_kernel,
-        grid=(per_device // 8,),
-        in_specs=[block, whole(gains.shape)] + [of_layer(w, 1) for w in weights],
-        out_specs=block,
-        out_shape=jax.ShapeDtypeStruct(received.shape, F32),
+        grid=(steps,),
+        in_specs=in_specs,
+        out_specs=pl.BlockSpec((GROUP, 8, CHANNELS), lambda s: (0, chunk * steps + s, 0)),
+        out_shape=jax.ShapeDtypeStruct((GROUP, CHUNKS * per_device, CHANNELS), F32),
         scratch_shapes=WEIGHT_SCRATCH,
+        input_output_aliases=aliases,
         compiler_params=pltpu.CompilerParams(vmem_limit_bytes=VMEM_LIMIT),
         cost_estimate=pl.CostEstimate(
             flops=14_000_000_000, bytes_accessed=4_000_000, transcendentals=0
         ),
-    )(received, gains, *weights)
+    )(*args)
 
 
 def neighbours(low_edge, high_edge, axis, count):
@@ -499,28 +564,29 @@
             field, context, above, below, before, after, ctx_weight, norm_gains, expand_weight,
             depth_weight, se_reduce.T,
         ),
-        rows,
+        rows * cols,
     )
 
     def exchange(x, axes):
         return lax.all_to_all(x, axes, split_axis=0, concat_axis=0, tiled=True)
 
-    partial = jnp.sum(exchange(partial[:, None, :], row_axis), axis=0, keepdims=True)
-    sums = exchange(jnp.broadcast_to(partial, (cols, 1, 128)), "col")[:, 0, :]
+    sums = exchange(partial[:, None, :], ("rg", "core", "col"))[:, 0, :]
 
     weights = (attn_qkv, attn_out, mlp_in, mlp_out)
     cells_total = rows * cols * field.shape[0] * field.shape[1]
     group = ("rg", "col")
-    pieces = []
+    sent = []
     for chunk in range(CHUNKS):
         mine = block_stage(
             chunk, lifted, active, sums, se_expand, project_weight, norm_gains, weights, cells_total
         )
-        sent = exchange(mine.reshape(GROUP, -1, CHANNELS), group)
-        back = exchange(grid_stage(sent, norm_gains, weights), group)
-        windows = back.reshape(4 // CHUNKS, 16, WINDOW, WINDOW, CHANNELS)
-        pieces.append(windows.transpose(0, 2, 1, 3, 4).reshape(-1, 128, CHANNELS))
-    return jnp.concatenate(pieces, axis=0)
+        sent.append(exchange(mine.reshape(GROUP, -1, CHANNELS), group))
+    attended = None
+    for chunk in range(CHUNKS):
+        attended = grid_stage(sent[chunk], norm_gains, weights, chunk, attended)
+    back = exchange(attended, group)
+    halves = back.reshape(4 // CHUNKS, 16, 2, CHUNKS, WINDOW // 2, WINDOW, CHANNELS)
+    return halves.transpose(3, 0, 2, 4, 1, 5, 6).reshape(field.shape)
 
 
 def solution(mesh):

time: 180 us -> 226 us (1.26)
  Pallas kernels: 77.2 us -> 125 us
  blocking collectives: 30.4 us -> 65 us
  waiting for transfers between devices: 31.8 us -> 5.77 us
  starting transfers between devices: 33.1 us -> 22.6 us
  local copies, waits for them, and re-layouts: 4.72 us -> 7.09 us
    all_to_all x2, blocking collectives: 30.4 us -> 65 us  [exchange(): return lax.all_to_all(x, axes, split_axis=0, concat_axis=0, tiled=True)]
    pallas_call x2, Pallas kernels: 26.3 us -> 60 us  [grid_stage(): pl.pallas_call(grid_kernel, grid=(steps,), in_specs=in_specs, out_specs=p...]
    all_to_all x4 -> x2, waiting for transfers between devices: 26 us -> 0.01 us  [exchange(): return lax.all_to_all(x, axes, split_axis=0, concat_axis=0, tiled=True)]
    pallas_call x2, Pallas kernels: 29.9 us -> 43.9 us  [block_stage(): pl.pallas_call(body, grid=(steps,), in_specs=[strip(CHANNELS), strip(EXPA...]
    all_to_all x4 -> x2, starting transfers between devices: 25.8 us -> 15.3 us  [exchange(): return lax.all_to_all(x, axes, split_axis=0, concat_axis=0, tiled=True)]
  transfers between devices with their start and end apart: 8 -> 6, of which waited for: 6 -> 2; matrix products, arithmetic and copies ran while one was open for 2% -> 1% of each run, Pallas kernels for 23% -> 23%
where the time goes in v2:
time: 226 us
  Pallas kernels  125 us (55%)
  blocking collectives  65 us (29%)
  starting transfers between devices  22.6 us (10%)
  local copies, waits for them, and re-layouts  7.09 us (3%)
  waiting for transfers between devices  5.77 us (3%)
    all_to_all x2, blocking collectives, exchange(): return lax.all_to_all(x, axes, split_axis=0, concat_axis=0, tiled=True)  65 us
    pallas_call x2, Pallas kernels, grid_stage(): pl.pallas_call(grid_kernel, grid=(steps,), in_specs=in_specs, out_specs=p...  60 us
    pallas_call x2, Pallas kernels, block_stage(): pl.pallas_call(body, grid=(steps,), in_specs=[strip(CHANNELS), strip(EXPA...  43.9 us
    pallas_call x1, Pallas kernels, lift_stage(): pl.pallas_call(lift_kernel, grid=(4,), in_specs=[pl.BlockSpec(memory_spac...  20.6 us
    all_to_all x2, starting transfers between devices, exchange(): return lax.all_to_all(x, axes, split_axis=0, concat_axis=0, tiled=True)  15.3 us
    ppermute x2, waiting for transfers between devices, neighbours(): lax.ppermute(low_edge, axis, backward)  5.76 us
    ppermute x2, starting transfers between devices, neighbours(): lax.ppermute(high_edge, axis, forward)  4.68 us
  transfers between devices with their start and end apart: 6, of which 2 were waited for; matrix products, arithmetic and copies ran while one was open for 1% of the time, Pallas kernels for 23%

profile of v2, /device:TPU:0, one launch (start us, length us, event | category | flops | bytes accessed | tf_op | source)
XLA Modules:
  0.0 225.7 jit_solution(6367883704394617938)
XLA Ops:
  0.0 0.7 slice_bitcast_fusion.2
  0.7 0.9 slice_bitcast_fusion
  1.6 1.3 collective-permute-start
  3.0 1.3 collective-permute-start.1
  4.3 1.0 fusion
  5.3 0.8 fusion.1
  6.1 1.9 collective-permute-done.1.below_ref
  8.3 3.4 %collective-permute-start.2 = (f32[44,128]{1,0:T(8,128)S(1)}, f32[44,128]{1,0:T(8,128)S(1)}, u32[]{:S(2)}, u32[]{:S(2)}) collective-permute-start(f32[44,128]{1,0:T(8,128)S(1)} %concatenate.14), channel_id=1, source_target_pairs={{0,1},{1,2},{2,3},{3,4},{4,5},{5,6},{6,7},{8,9},{9,10},{10,11},{11... | collective-permute-start | bytes 67592 | tf_op jit(solution)/shard_map/ppermute | solution.py:532
  11.7 0.3 concatenate.15
  11.9 1.3 collective-permute-start.3
  13.2 0.6 pad_add_fusion.place_ref
  13.8 3.8 %collective-permute-done.3.after_ref = f32[44,128]{1,0:T(8,128)S(1)} collective-permute-done((f32[44,128]{1,0:T(8,128)S(1)}, f32[44,128]{1,0:T(8,128)S(1)}, u32[]{:S(2)}, u32[]{:S(2)}) %collective-permute-start.3) | collective-permute-done | bytes 22560 | tf_op jit(solution)/shard_map/ppermute | solution.py:532
  17.6 0.6 copy-done.5
  18.2 20.6 %shard_map.136 = (f32[32,128,128]{2,1,0:T(8,128)}, f32[32,128,512]{2,1,0:T(8,128)}, f32[128,128]{1,0:T(8,128)}) custom-call(s32[2]{0:T(128)} %pad_add_fusion.place_ref, f32[32,128,128]{2,1,0:T(8,128)} %field_ref.1, f32[8,32,128]{2,1,0:T(8,128)} %context_ref.1, f32[160,128]{1,0:T(8,128)} %copy-done.2, f32[160,128]{1,0:T(8,128)} %copy-done.3, ...), custom_call_target="tpu_custom_call" | custom-call | flops 8000000000 | bytes 14000000 | tf_op jit(solution)/shard_map/pallas_call | solution.py:364
  38.9 25.3 %all_to_all.20 = f32[128,1,128]{2,1,0:T(1,128)} all-to-all(f32[128,1,128]{2,1,0:T(1,128)} %bitcast.38), channel_id=1, replica_groups=mesh['rg'=8,'core'=2,'col'=8] {'rg','core','col'}, dimensions={0} | all-to-all | bytes 131072 | tf_op jit(solution)/shard_map/all_to_all | solution.py:571
  64.2 21.9 %shard_map.138 = f32[2048,128]{1,0:T(8,128)} custom-call(f32[32,128,128]{2,1,0:T(8,128)} %get-tuple-element.8.refs_0_, f32[32,128,512]{2,1,0:T(8,128)} %get-tuple-element.9.refs_1_, f32[128,128]{1,0:T(8,128)} %bitcast.36, f32[32,512]{1,0:T(8,128)} %refs_3_.3, f32[512,128]{1,0:T(8,128)} %refs_4_.3, f32[5,128]{1,0:T(8,128)} %gains_ref.5, ...), custom_call_target="tpu_custom_call" | custom-call | flops 14000000000 | bytes 8000000 | tf_op jit(solution)/shard_map/pallas_call | solution.py:463
  86.1 4.7 %all-to-all-start.2 = ((f32[64,32,128]{2,1,0:T(8,128)}), f32[64,32,128]{2,1,0:T(8,128)S(1)}, u32[]{:S(2)}, u32[]{:S(2)}) async-start(f32[64,32,128]{2,1,0:T(8,128)} %bitcast.35), calls=%async_computation.2 | async-start | bytes 2097152 | tf_op jit(solution)/shard_map/all_to_all | solution.py:571
  90.9 22.0 %shard_map.137 = f32[2048,128]{1,0:T(8,128)} custom-call(f32[32,128,128]{2,1,0:T(8,128)} %get-tuple-element.8.refs_0_, f32[32,128,512]{2,1,0:T(8,128)} %get-tuple-element.9.refs_1_, f32[128,128]{1,0:T(8,128)} %bitcast.37, f32[32,512]{1,0:T(8,128)} %refs_3_.3, f32[512,128]{1,0:T(8,128)} %refs_4_.3, f32[5,128]{1,0:T(8,128)} %gains_ref.5, ...), custom_call_target="tpu_custom_call" | custom-call | flops 14000000000 | bytes 8000000 | tf_op jit(solution)/shard_map/pallas_call | solution.py:463
  112.9 10.6 %all-to-all-start.1 = ((f32[64,32,128]{2,1,0:T(8,128)}), f32[64,32,128]{2,1,0:T(8,128)S(1)}, u32[]{:S(2)}, u32[]{:S(2)}) async-start(f32[64,32,128]{2,1,0:T(8,128)} %bitcast.34), calls=%async_computation.1 | async-start | bytes 2097152 | tf_op jit(solution)/shard_map/all_to_all | solution.py:571
  123.5 30.0 %shard_map.139.rest_0_ = f32[64,64,128]{2,1,0:T(8,128)} custom-call(f32[64,32,128]{2,1,0:T(8,128)} %copy-done, f32[5,128]{1,0:T(8,128)} %gains_ref.5, f32[2,128,384]{2,1,0:T(8,128)} %qkv_ref.3, f32[2,128,128]{2,1,0:T(8,128)} %aout_ref.3, f32[2,128,512]{2,1,0:T(8,128)} %min_ref.3, f32[2,512,128]{2,1,0:T(8,128)} %mout_ref.3), custom_call_target="tpu_custom_call" | custom-call | flops 14000000000 | bytes 4000000 | tf_op jit(solution)/shard_map/pallas_call | solution.py:514
  153.5 1.0 copy-done.1
  154.5 30.0 %shard_map.140 = f32[64,64,128]{2,1,0:T(8,128)} custom-call(f32[64,32,128]{2,1,0:T(8,128)} %copy-done.1, f32[5,128]{1,0:T(8,128)} %gains_ref.5, f32[2,128,384]{2,1,0:T(8,128)} %qkv_ref.3, f32[2,128,128]{2,1,0:T(8,128)} %aout_ref.3, f32[2,128,512]{2,1,0:T(8,128)} %min_ref.3, f32[2,512,128]{2,1,0:T(8,128)} %mout_ref.3, ...), custom_call_target="tpu_custom_call", output_to_operand_aliasing={{}: (6, {})} | custom-call | flops 14000000000 | bytes 4000000 | tf_op jit(solution)/shard_map/pallas_call | solution.py:514
  184.5 39.7 %all_to_all.21 = f32[64,64,128]{2,1,0:T(8,128)S(1)} all-to-all(f32[64,64,128]{2,1,0:T(8,128)} %shard_map.140), channel_id=1, replica_groups=mesh['rg'=8,'core'=2,'col'=8] {'rg','col'}, dimensions={0} | all-to-all | bytes 4194304 | tf_op jit(solution)/shard_map/all_to_all | solution.py:571
  224.1 1.6 copy.26
  (19 shorter events, 0.3 us)
Async XLA Ops:
  1.6 4.4 %collective-permute-start = (f32[160,128]{1,0:T(8,128)S(1)}, f32[160,128]{1,0:T(8,128)S(1)}, u32[]{:S(2)}, u32[]{:S(2)}) collective-permute-start(f32[160,128]{1,0:T(8,128)S(1)} %pad_maximum_fusion), channel_id=1, source_target_pairs={{0,8},{8,16},{16,24},{24,32},{32,40},{40,48},{48,56},{56,64},{64,7... | collective-permute-start | bytes 245768 | tf_op jit(solution)/shard_map/ppermute | solution.py:532
  3.0 5.1 %collective-permute-start.1 = (f32[160,128]{1,0:T(8,128)S(1)}, f32[160,128]{1,0:T(8,128)S(1)}, u32[]{:S(2)}, u32[]{:S(2)}) collective-permute-start(f32[160,128]{1,0:T(8,128)S(1)} %pad_maximum_fusion.1), channel_id=1, source_target_pairs={{8,0},{16,8},{24,16},{32,24},{40,32},{48,40},{56,48},{64,56},{72,6... | collective-permute-start | bytes 245768 | tf_op jit(solution)/shard_map/ppermute | solution.py:532
  6.0 11.6 %copy-start.2 = (f32[160,128]{1,0:T(8,128)}, f32[160,128]{1,0:T(8,128)S(1)}, u32[]{:S(2)}) copy-start(f32[160,128]{1,0:T(8,128)S(1)} %collective-permute-done.above_ref) | copy-start | bytes 245764
  8.0 9.6 %copy-start.3 = (f32[160,128]{1,0:T(8,128)}, f32[160,128]{1,0:T(8,128)S(1)}, u32[]{:S(2)}) copy-start(f32[160,128]{1,0:T(8,128)S(1)} %collective-permute-done.1.below_ref) | copy-start | bytes 245764
  8.3 5.6 %collective-permute-start.2 = (f32[44,128]{1,0:T(8,128)S(1)}, f32[44,128]{1,0:T(8,128)S(1)}, u32[]{:S(2)}, u32[]{:S(2)}) collective-permute-start(f32[44,128]{1,0:T(8,128)S(1)} %concatenate.14), channel_id=1, source_target_pairs={{0,1},{1,2},{2,3},{3,4},{4,5},{5,6},{6,7},{8,9},{9,10},{10,11},{11... | collective-permute-start | bytes 67592 | tf_op jit(solution)/shard_map/ppermute | solution.py:532
  11.9 5.7 %collective-permute-start.3 = (f32[44,128]{1,0:T(8,128)S(1)}, f32[44,128]{1,0:T(8,128)S(1)}, u32[]{:S(2)}, u32[]{:S(2)}) collective-permute-start(f32[44,128]{1,0:T(8,128)S(1)} %concatenate.15), channel_id=1, source_target_pairs={{1,0},{2,1},{3,2},{4,3},{5,4},{6,5},{7,6},{9,8},{10,9},{11,10},{12... | collective-permute-start | bytes 67592 | tf_op jit(solution)/shard_map/ppermute | solution.py:532
  13.8 3.8 %copy-start.4 = (f32[44,128]{1,0:T(8,128)}, f32[44,128]{1,0:T(8,128)S(1)}, u32[]{:S(2)}) copy-start(f32[44,128]{1,0:T(8,128)S(1)} %collective-permute-done.2.before_ref) | copy-start | bytes 67588
  17.6 0.6 copy-start.5
  86.1 26.7 %all-to-all-start.2 = ((f32[64,32,128]{2,1,0:T(8,128)}), f32[64,32,128]{2,1,0:T(8,128)S(1)}, u32[]{:S(2)}, u32[]{:S(2)}) async-start(f32[64,32,128]{2,1,0:T(8,128)} %bitcast.35), calls=%async_computation.2 | async-start | bytes 2097152 | tf_op jit(solution)/shard_map/all_to_all | solution.py:571
  112.9 10.6 %copy-start = (f32[64,32,128]{2,1,0:T(8,128)}, f32[64,32,128]{2,1,0:T(8,128)S(1)}, u32[]{:S(2)}) copy-start(f32[64,32,128]{2,1,0:T(8,128)S(1)} %all-to-all-done.2.x_ref) | copy-start | bytes 3145732
  112.9 40.6 %all-to-all-start.1 = ((f32[64,32,128]{2,1,0:T(8,128)}), f32[64,32,128]{2,1,0:T(8,128)S(1)}, u32[]{:S(2)}, u32[]{:S(2)}) async-start(f32[64,32,128]{2,1,0:T(8,128)} %bitcast.34), calls=%async_computation.1 | async-start | bytes 2097152 | tf_op jit(solution)/shard_map/all_to_all | solution.py:571
  153.5 1.0 copy-start.1

commit v3 on v2

v3 whole, which is shorter than its diff:
```python
import math

import jax
import jax.numpy as jnp
import numpy as np
from jax import lax
from jax.experimental import pallas as pl
from jax.experimental.pallas import tpu as pltpu
from jax.sharding import Mesh
from jax.sharding import PartitionSpec as P

HEADS = 4
WINDOW = 8
CHANNELS = 128
EXPANDED = 512
MLP_HIDDEN = 512
SQUEEZE = 32
HEAD_DIM = CHANNELS // HEADS
CELLS = WINDOW * WINDOW
GROUP = 64
WIDE = 136
EPSILON = 1e-05
F32 = jnp.float32
BF16 = jnp.bfloat16
HIGHEST = lax.Precision.HIGHEST
CHUNKS = 2
BLOCK_STEP = 1024
GRID_STEP = 2048
VMEM_LIMIT = 56 * 1024 * 1024

GELU_A = 2.0 * math.sqrt(2.0 / math.pi)
GELU_B = 4.0 * GELU_A * 0.044715


def gelu_of_half(half):
    return half * jnp.tanh(half * (GELU_A + GELU_B * (half * half))) + half


def split(x):
    high = x.astype(BF16)
    low = (x - high.astype(F32)).astype(BF16)
    return high, low


def dot(a, b):
    return jnp.dot(a, b, preferred_element_type=F32)


def rows_of(parts):
    return jnp.concatenate(parts, axis=0)


def lanes_of(parts):
    return jnp.concatenate(parts, axis=1)


def normed(x):
    shifted = x - jnp.mean(x, axis=-1, keepdims=True)
    spread = jnp.sum(shifted * shifted, axis=-1, keepdims=True)
    return shifted * lax.rsqrt(spread + CHANNELS * EPSILON)


def gained(weight, gain):
    column = jnp.broadcast_to(gain * math.sqrt(CHANNELS), (CHANNELS, CHANNELS)).T
    return lanes_of([weight[:, c : c + 128] * column for c in range(0, weight.shape[1], 128)])


def three(x):
    high, low = split(x)
    return lanes_of([high, low, high])


def stack_rows(weight):
    high, low = split(weight)
    return rows_of([high, high, low])


def deep_weight(weight):
    return lanes_of(split(weight))


def prepare_attention(qkv_ref, out_ref, gain, k3, qv3, out3):
    scale = math.log2(math.e) / math.sqrt(HEAD_DIM)
    k3[...] = stack_rows(gained(qkv_ref[0, :, CHANNELS : 2 * CHANNELS], gain))
    row_gain = gain * math.sqrt(CHANNELS)
    queries = qkv_ref[0, :, :CHANNELS].T * (row_gain * scale)
    values = qkv_ref[0, :, 2 * CHANNELS :].T * row_gain
    high, low = split(rows_of([queries, values]))
    qv3[...] = lanes_of([high, high, low])
    out3[...] = stack_rows(out_ref[0])


def prepare_feed(in_ref, mlp_ref, gain, in3, mlp_pair):
    in3[...] = stack_rows(gained(0.5 * in_ref[0], gain))
    mlp_pair[...] = deep_weight(mlp_ref[0])


PAIR = 2 * CELLS
PART = 512


def attend(pairs, k3, qv3, out3):
    left = lax.broadcasted_iota(jnp.int32, (HEAD_DIM, PAIR), 1) < CELLS
    left_all = lax.broadcasted_iota(jnp.int32, (CHANNELS, PAIR), 1) < CELLS
    zero = jnp.zeros((HEAD_DIM, PAIR), BF16)
    zero_block = jnp.zeros((2 * HEAD_DIM, PAIR), BF16)
    natural, turned = [], []
    for x in pairs:
        high, low = split(normed(x))
        natural.append(lanes_of([high, low, high]))
        high, low = high.T, low.T
        turned.append(rows_of([high, low, high]))
    yield
    keys = dot(rows_of(natural), k3[...])
    both = dot(qv3[...], lanes_of(turned))
    yield
    sides, value_sides = [], []

    def by_heads(straight, swapped):
        blocks = []
        for group in range(2):
            at = [slice(h * HEAD_DIM, (h + 1) * HEAD_DIM) for h in (2 * group, 2 * group + 1)]
            block = rows_of(
                [jnp.where(left, straight[at[0]], zero), jnp.where(left, zero, swapped[at[1]])]
            )
            blocks.append(lanes_of([zero_block, block] if group else [block, zero_block]))
        return rows_of(blocks)

    for p in range(len(pairs)):
        at = slice(p * PAIR, (p + 1) * PAIR)
        key3 = three(keys[at])
        high, low = split(both[:CHANNELS, at])
        high_swapped, low_swapped = pltpu.roll(high, CELLS, 1), pltpu.roll(low, CELLS, 1)
        for second in range(2):
            if second:
                h, l = by_heads(high_swapped, high), by_heads(low_swapped, low)
            else:
                h, l = by_heads(high, high_swapped), by_heads(low, low_swapped)
            sides.append((key3[second * CELLS : (second + 1) * CELLS], rows_of([h, h, l])))
        high, low = split(both[CHANNELS:, at])
        low = pltpu.roll(low, CELLS, 1)
        first, second = jnp.where(left_all, high, low), jnp.where(left_all, low, high)
        value_sides += [lanes_of([first, first]), lanes_of([second, second])]
    yield
    scores = [dot(key, query) for key, query in sides]
    yield
    weights, scales = [], []
    for score in scores:
        weight = jnp.exp2(score - jnp.max(score, axis=0, keepdims=True))
        scales.append(1.0 / jnp.sum(weight, axis=0, keepdims=True))
        high, low = split(weight)
        weights.append(rows_of([high, high, low, low]))
    yield
    mixed = [
        [dot(value[64 * g : 64 * g + 64], weight[:, 128 * g : 128 * g + 128]) for g in range(2)]
        for value, weight in zip(value_sides, weights)
    ]
    yield
    blended = []
    for p in range(len(pairs)):
        parts = []
        for h in range(HEADS):
            lanes = slice(128 * (h // 2), 128 * (h // 2) + 128)
            at = slice((h % 2) * HEAD_DIM, (h % 2 + 1) * HEAD_DIM)
            of_a, of_b = (
                mixed[2 * p + i][h // 2][at] * scales[2 * p + i][:, lanes] for i in range(2)
            )
            if h % 2:
                of_a = pltpu.roll(of_a, CELLS, 1)
            else:
                of_b = pltpu.roll(of_b, CELLS, 1)
            parts.append(jnp.where(left, of_a, of_b))
        blended.append(three(rows_of(parts).T))
    yield
    added = dot(rows_of(blended), out3[...])
    yield
    return [x + added[p * PAIR : (p + 1) * PAIR] for p, x in enumerate(pairs)]


def feed(pairs, in3, mlp_pair):
    parts = [three(normed(x)) for x in pairs]
    yield
    inner = dot(rows_of(parts), in3[...])
    yield
    high, low = split_blocks(inner, 64, gelu_of_half)
    yield
    wide = dot(high, mlp_pair[...])
    rest = dot(low, mlp_pair[:, :CHANNELS])
    yield
    out = []
    for p, x in enumerate(pairs):
        at = slice(p * PAIR, (p + 1) * PAIR)
        out.append(x + (wide[at, :CHANNELS] + (wide[at, CHANNELS:] + rest[at])))
    return out


def staggered(groups):
    waiting, running = list(groups), []
    while waiting or running:
        if waiting:
            running.append(waiting.pop(0))
        for group in list(running):
            try:
                next(group)
            except StopIteration:
                running.remove(group)


def split_blocks(x, rows, make):
    highs, lows = [], []
    for r in range(0, x.shape[0], rows):
        made = [split(make(x[r : r + rows, c : c + 128])) for c in range(0, x.shape[1], 128)]
        highs.append(lanes_of([m[0] for m in made]))
        lows.append(lanes_of([m[1] for m in made]))
    return rows_of(highs), rows_of(lows)


def column_weights():
    fine = np.zeros((WIDE, 40), np.float32)
    table = ((0.375, 0.625, 0.0), (0.125, 0.875, 0.0), (0.0, 0.875, 0.125), (0.0, 0.625, 0.375))

    def fill(at, column):
        k, o = column // 4, column % 4
        for step, weight in zip((-1, 0, 1), table[o]):
            if weight:
                fine[at, (k + step) % 40] = weight

    for column in range(129):
        fill(column, column)
    fill(135, -1)
    return np.concatenate([fine, fine], axis=1)


ROW_WEIGHTS = ((0.375, 0.625, -1), (0.125, 0.875, -1), (0.875, 0.125, 0), (0.625, 0.375, 0))


def lift_kernel(
    place_ref, field_ref, context_ref, rows_a_ref, rows_b_ref, cols_a_ref, cols_b_ref, up_ref,
    ctxw_ref, gains_ref, expand_ref, depth_ref, reduce_ref, lifted_ref, active_ref, sum_ref,
    lift, ctx, coarse, hid, expand3, total,
):
    step = pl.program_id(0)
    sublane = lax.broadcasted_iota(jnp.int32, (8, 128), 0)
    first_row, last_row = sublane == 0, sublane == 7

    @pl.when(step == 0)
    def _():
        expand3[...] = stack_rows(gained(0.5 * expand_ref[...], gains_ref[0:1]))
        total[...] = jnp.zeros_like(total)
        lift[1:33, :128] = field_ref[...]
        ctx[1:9, :32] = context_ref[...]

        def take_rows(above_ref, below_ref):
            lift[0, :128] = above_ref[:128]
            lift[33, :128] = below_ref[:128]
            ctx[0, :32] = above_ref[128:]
            ctx[9, :32] = below_ref[128:]

        def take_columns(before_ref, after_ref):
            zero = jnp.zeros((8, 128), F32)
            for e in range(44):
                after = jnp.broadcast_to(after_ref[e : e + 1], (8, 128))
                before = jnp.broadcast_to(before_ref[e : e + 1], (8, 128))
                group = jnp.where(first_row, after, jnp.where(last_row, before, zero))
                if e < 34:
                    lift[e, 128:] = group
                else:
                    ctx[e - 34, 32:] = group

        pl.when(place_ref[0] % 2 == 0)(lambda: take_rows(rows_b_ref, rows_a_ref))
        pl.when(place_ref[0] % 2 == 1)(lambda: take_rows(rows_a_ref, rows_b_ref))
        pl.when(place_ref[1] % 2 == 0)(lambda: take_columns(cols_b_ref, cols_a_ref))
        pl.when(place_ref[1] % 2 == 1)(lambda: take_columns(cols_a_ref, cols_b_ref))
        weight = stack_rows(ctxw_ref[...])
        projected = dot(three(ctx[...].reshape(400, CHANNELS)), weight)
        for k in range(10):
            high, low = split(projected[40 * k : 40 * k + 40])
            coarse[k] = dot(up_ref[...], rows_of([high, low]))

    has_after = jnp.where(place_ref[1] < 7, 1.0, 0.0)
    has_before = jnp.where(place_ref[1] > 0, 1.0, 0.0)
    inside = jnp.where(first_row, has_after, has_before)

    def hidden_rows(first, fine_first, k_first, count):
        parts = []
        for i in range(0, count, 2):
            two = []
            for j in (i, i + 1):
                k, o = (fine_first + j) // 4, (fine_first + j) % 4
                lower, upper, shift = ROW_WEIGHTS[o]
                at = k_first + k + shift
                x = lift[first + j] + (lower * coarse[at] + upper * coarse[at + 1])
                lift[first + j] = x
                two.append(x)
            parts.append(three(normed(rows_of(two))))
        made = dot(rows_of(parts), expand3[...])
        for i in range(count):
            for c in range(0, EXPANDED, 128):
                out = gelu_of_half(made[i * WIDE : (i + 1) * WIDE, c : c + 128])
                hid[first + i, :128, c : c + 128] = out[:128]
                hid[first + i, 128:, c : c + 128] = out[128:] * inside

    @pl.when(step == 0)
    def _():
        hidden_rows(0, -1, 1, 2)

        @pl.when(place_ref[0] == 0)
        def _():
            hid[0] = jnp.zeros((WIDE, EXPANDED), F32)

    hidden_rows(8 * step + 2, 1, 2 * step + 1, 4)
    hidden_rows(8 * step + 6, 5, 2 * step + 1, 4)

    @pl.when((step == 3) & (place_ref[0] == 15))
    def _():
        hid[33] = jnp.zeros((WIDE, EXPANDED), F32)

    lifted_ref[...] = lift[pl.ds(8 * step + 1, 8), :128]

    for part in range(EXPANDED // 128):
        lanes = slice(part * 128, (part + 1) * 128)
        taps = [
            [jnp.broadcast_to(0.5 * depth_ref[i, j : j + 1, lanes], (8, 128)) for j in range(3)]
            for i in range(3)
        ]

        def row(r, summed):
            def columns(g):
                seen = [hid[8 * step + r + i, 8 * g : 8 * g + 8, lanes] for i in range(3)]
                a, b, c = (
                    seen[0] * taps[0][j] + seen[1] * taps[1][j] + seen[2] * taps[2][j]
                    for j in range(3)
                )
                return pltpu.roll(a, 1, 0), b, pltpu.roll(c, 7, 0)

            halo = columns(16)
            held, here = halo[0], columns(0)
            for g in range(16):
                following = columns(g + 1) if g < 15 else halo
                out = gelu_of_half(
                    here[1]
                    + jnp.where(first_row, held, here[0])
                    + jnp.where(last_row, following[2], here[2])
                )
                active_ref[r, 8 * g : 8 * g + 8, lanes] = out
                summed = summed + out
                held, here = here[0], following
            return summed

        summed = total[:, lanes]
        for r in range(8):
            summed = row(r, summed)
        total[:, lanes] = summed

    @pl.when(step == 3)
    def _():
        squeezed = lax.dot_general(
            total[...], reduce_ref[...], (((1,), (1,)), ((), ())), precision=HIGHEST,
            preferred_element_type=F32,
        )
        squeezed = jnp.sum(squeezed, axis=0, keepdims=True)
        padded = lanes_of([squeezed, jnp.zeros((1, 128 - SQUEEZE), F32)])
        sum_ref[...] = jnp.broadcast_to(padded, sum_ref.shape)


def whole(shape):
    return pl.BlockSpec(shape, lambda *_: (0,) * len(shape))


def of_layer(array, layer):
    shape = (1,) + array.shape[1:]
    return pl.BlockSpec(shape, lambda *_: (layer,) + (0,) * (len(shape) - 1))


def lift_stage(place, args, copies):
    up = jnp.asarray(column_weights(), BF16)
    args = args[:6] + (up,) + args[6:]
    return pl.pallas_call(
        lift_kernel,
        grid=(4,),
        in_specs=[pl.BlockSpec(memory_space=pltpu.SMEM)] + [whole(a.shape) for a in args],
        out_specs=[
            pl.BlockSpec((8, 128, CHANNELS), lambda s: (s, 0, 0)),
            pl.BlockSpec((8, 128, EXPANDED), lambda s: (s, 0, 0)),
            whole((copies, 128)),
        ],
        out_shape=[
            jax.ShapeDtypeStruct((32, 128, CHANNELS), F32),
            jax.ShapeDtypeStruct((32, 128, EXPANDED), F32),
            jax.ShapeDtypeStruct((copies, 128), F32),
        ],
        scratch_shapes=[
            pltpu.VMEM((34, WIDE, CHANNELS), F32),
            pltpu.VMEM((10, 40, CHANNELS), F32),
            pltpu.VMEM((10, WIDE, CHANNELS), F32),
            pltpu.VMEM((34, WIDE, EXPANDED), F32),
            pltpu.VMEM((3 * CHANNELS, EXPANDED), BF16),
            pltpu.VMEM((8, EXPANDED), F32),
        ],
        compiler_params=pltpu.CompilerParams(vmem_limit_bytes=VMEM_LIMIT),
        cost_estimate=pl.CostEstimate(
            flops=8_000_000_000, bytes_accessed=14_000_000, transcendentals=0
        ),
    )(place, *args)


def block_kernel(
    cells_total, fed, lifted_ref, active_ref, sums_ref, sexp_ref, project_ref, gains_ref, qkv_ref,
    aout_ref, min_ref, mout_ref, out_ref, project, k3, qv3, out3, *feed_weights,
):
    @pl.when(pl.program_id(0) == 0)
    def _():
        pooled = jnp.sum(sums_ref[...], axis=0, keepdims=True) * (1.0 / cells_total)
        squeezed = pooled[:, :SQUEEZE]
        squeezed = squeezed * jax.nn.sigmoid(squeezed)
        wide = jnp.broadcast_to(squeezed, (CHANNELS, SQUEEZE))
        gate = jnp.dot(wide, sexp_ref[...], precision=HIGHEST, preferred_element_type=F32)
        project[...] = deep_weight(project_ref[...] * jax.nn.sigmoid(gate).T)
        prepare_attention(qkv_ref, aout_ref, gains_ref[1:2], k3, qv3, out3)
        if fed:
            prepare_feed(min_ref, mout_ref, gains_ref[2:3], *feed_weights)

    def projected(start):
        highs, lows = [], []
        for w in range(start, start + PART // CELLS):
            cells = active_ref[:, 8 * w : 8 * w + 8, :].reshape(CELLS, EXPANDED)
            high, low = split(cells)
            highs.append(high)
            lows.append(low)
        yield
        wide = dot(rows_of(highs), project[...])
        rest = dot(rows_of(lows), project[:, :CHANNELS])
        yield
        pairs = []
        for p in range(PART // PAIR):
            at = slice(p * PAIR, (p + 1) * PAIR)
            x = rows_of(
                [
                    lifted_ref[:, 8 * w : 8 * w + 8, :].reshape(CELLS, CHANNELS)
                    for w in (start + 2 * p, start + 2 * p + 1)
                ]
            )
            pairs.append(x + (wide[at, :CHANNELS] + (wide[at, CHANNELS:] + rest[at])))
        return pairs

    def group(part):
        pairs = yield from projected(part * PART // CELLS)
        pairs = yield from attend(pairs, k3, qv3, out3)
        if fed:
            pairs = yield from feed(pairs, *feed_weights)
        for p, x in enumerate(pairs):
            out_ref[part * PART + p * PAIR : part * PART + (p + 1) * PAIR] = x

    staggered(group(part) for part in range(BLOCK_STEP // PART))


ATTENTION_SCRATCH = [
    pltpu.VMEM((3 * CHANNELS, CHANNELS), BF16),
    pltpu.VMEM((2 * CHANNELS, 3 * CHANNELS), BF16),
    pltpu.VMEM((3 * CHANNELS, CHANNELS), BF16),
]
FEED_SCRATCH = [
    pltpu.VMEM((3 * CHANNELS, MLP_HIDDEN), BF16),
    pltpu.VMEM((MLP_HIDDEN, 2 * CHANNELS), BF16),
]


def block_stage(chunk, fed, lifted, active, sums, se_expand, project, gains, weights, cells_total):
    per_row = 128 // (BLOCK_STEP // 8)
    steps = 4 // CHUNKS * per_row
    row_base = chunk * (4 // CHUNKS)
    rest = (sums, se_expand, project, gains)

    def strip(channels):
        return pl.BlockSpec(
            (8, BLOCK_STEP // 8, channels), lambda s: (row_base + s // per_row, s % per_row, 0)
        )

    def body(*refs):
        block_kernel(cells_total, fed, *refs)

    return pl.pallas_call(
        body,
        grid=(steps,),
        in_specs=[strip(CHANNELS), strip(EXPANDED)]
        + [whole(a.shape) for a in rest]
        + [of_layer(w, 0) for w in weights],
        out_specs=pl.BlockSpec((BLOCK_STEP, CHANNELS), lambda s: (s, 0)),
        out_shape=jax.ShapeDtypeStruct((steps * BLOCK_STEP, CHANNELS), F32),
        scratch_shapes=[pltpu.VMEM((EXPANDED, 2 * CHANNELS), BF16)]
        + ATTENTION_SCRATCH
        + (FEED_SCRATCH if fed else []),
        compiler_params=pltpu.CompilerParams(vmem_limit_bytes=VMEM_LIMIT),
        cost_estimate=pl.CostEstimate(
            flops=14_000_000_000, bytes_accessed=8_000_000, transcendentals=0
        ),
    )(lifted, active, *rest, *weights)


def grid_kernel(fed, x_ref, gains_ref, *refs):
    scratch = 5 if fed else 7
    out_ref, k3, qv3, out3, *feeds = refs[-scratch - 1 :]
    qkv_ref, aout_ref, *feed_refs = refs[: 4 if fed else 6]

    @pl.when(pl.program_id(0) == 0)
    def _():
        prepare_attention(qkv_ref, aout_ref, gains_ref[3:4], k3, qv3, out3)
        prepare_feed(*feed_refs[:2], gains_ref[4:5], *feeds[:2])
        if not fed:
            prepare_feed(*feed_refs[2:], gains_ref[2:3], *feeds[2:])

    stride = GRID_STEP // GROUP
    flat_in = x_ref.reshape(GRID_STEP, CHANNELS)
    flat_out = out_ref.reshape(GRID_STEP, CHANNELS)

    def group(part):
        first = part * PART // GROUP
        windows = [flat_in[pl.ds(first + p, GROUP, stride=stride), :] for p in range(PART // GROUP)]
        pairs = [rows_of(windows[i : i + 2]) for i in range(0, len(windows), 2)]
        if not fed:
            pairs = yield from feed(pairs, *feeds[2:])
        pairs = yield from attend(pairs, k3, qv3, out3)
        pairs = yield from feed(pairs, *feeds[:2])
        for p, x in enumerate(pairs):
            for i in range(2):
                window = first + 2 * p + i
                flat_out[pl.ds(window, GROUP, stride=stride), :] = x[i * GROUP : (i + 1) * GROUP]

    staggered(group(part) for part in range(GRID_STEP // PART))


def grid_stage(received, fed, gains, weights, chunk, earlier):
    per_device = received.shape[1]
    steps = per_device * GROUP // GRID_STEP
    shape = (GROUP, GRID_STEP // GROUP, CHANNELS)
    in_specs = [pl.BlockSpec(shape, lambda s: (0, s, 0)), whole(gains.shape)]
    in_specs += [of_layer(w, 1) for w in weights]
    args = (received, gains) + weights
    if not fed:
        in_specs += [of_layer(w, 0) for w in weights[2:]]
        args += weights[2:]
    aliases = {}
    if earlier is not None:
        in_specs.append(pl.BlockSpec(memory_space=pl.ANY))
        aliases = {len(args): 0}
        args += (earlier,)

    def body(*refs):
        grid_kernel(fed, *refs)

    return pl.pallas_call(
        body,
        grid=(steps,),
        in_specs=in_specs,
        out_specs=pl.BlockSpec(shape, lambda s: (0, chunk * steps + s, 0)),
        out_shape=jax.ShapeDtypeStruct((GROUP, CHUNKS * per_device, CHANNELS), F32),
        scratch_shapes=ATTENTION_SCRATCH + FEED_SCRATCH + ([] if fed else FEED_SCRATCH),
        input_output_aliases=aliases,
        compiler_params=pltpu.CompilerParams(vmem_limit_bytes=VMEM_LIMIT),
        cost_estimate=pl.CostEstimate(
            flops=14_000_000_000, bytes_accessed=4_000_000, transcendentals=0
        ),
    )(*args)


def by_pairs(edge, at, axis, count):
    even = at % 2 == 0
    swaps = []
    for first, last in ((0, even), (1, jnp.logical_not(even))):
        lower = [(i, i + 1) for i in range(first, count - 1, 2)]
        pairs = lower + [(b, a) for a, b in lower]
        swaps.append(lax.ppermute(edge(last), axis, pairs))
    return swaps


def per_device(
    field, context, ctx_weight, norm_gains, expand_weight, depth_weight, se_reduce, se_expand,
    project_weight, attn_qkv, attn_out, mlp_in, mlp_out,
):
    row_axis = ("rg", "core")
    rows, cols = 16, 8
    row = lax.axis_index(row_axis)
    col = lax.axis_index("col")

    def row_edge(last):
        fine = lax.dynamic_index_in_dim(field, jnp.where(last, 31, 0), 0, keepdims=False)
        of_context = lax.dynamic_index_in_dim(context, jnp.where(last, 7, 0), 0, keepdims=False)
        return jnp.concatenate([fine, of_context], axis=0)

    rows_a, rows_b = by_pairs(row_edge, row, row_axis, rows)
    odd = row % 2 == 1

    def column_edge(last):
        fine_at, coarse_at = jnp.where(last, 127, 0), jnp.where(last, 31, 0)

        def one(x, at):
            return lax.dynamic_slice_in_dim(x, at, 1, axis=x.ndim - 2).reshape(-1, CHANNELS)

        parts = []
        for start, stop, tile, at in ((0, 128, field, fine_at), (128, 160, context, coarse_at)):
            of_a, of_b = one(rows_a[start:stop], at), one(rows_b[start:stop], at)
            parts += [jnp.where(odd, of_a, of_b), one(tile, at), jnp.where(odd, of_b, of_a)]
        return jnp.concatenate(parts, axis=0)

    cols_a, cols_b = by_pairs(column_edge, col, "col", cols)
    place = jnp.stack([row, col]).astype(jnp.int32)
    lifted, active, partial = lift_stage(
        place,
        (
            field, context, rows_a, rows_b, cols_a, cols_b, ctx_weight, norm_gains, expand_weight,
            depth_weight, se_reduce.T,
        ),
        rows * cols,
    )

    def exchange(x, axes):
        return lax.all_to_all(x, axes, split_axis=0, concat_axis=0, tiled=True)

    sums = exchange(partial[:, None, :], ("rg", "core", "col"))[:, 0, :]

    weights = (attn_qkv, attn_out, mlp_in, mlp_out)
    cells_total = rows * cols * field.shape[0] * field.shape[1]
    group = ("rg", "col")
    sent = []
    for chunk in range(CHUNKS):
        mine = block_stage(
            chunk, chunk > 0, lifted, active, sums, se_expand, project_weight, norm_gains, weights,
            cells_total,
        )
        sent.append(exchange(mine.reshape(GROUP, -1, CHANNELS), group))
    attended = None
    for chunk in range(CHUNKS):
        attended = grid_stage(sent[chunk], chunk > 0, norm_gains, weights, chunk, attended)
    back = exchange(attended, group)
    halves = back.reshape(4 // CHUNKS, 16, 2, CHUNKS, WINDOW // 2, WINDOW, CHANNELS)
    return halves.transpose(3, 0, 2, 4, 1, 5, 6).reshape(field.shape)


def solution(mesh):
    fine = Mesh(mesh.devices.reshape(8, 2, 8), ("rg", "core", "col"))
    tiled = P(("rg", "core"), "col", None)
    return jax.shard_map(
        per_device,
        mesh=fine,
        in_specs=(tiled, tiled) + (P(),) * 11,
        out_specs=tiled,
        check_vma=False,
    )
```

time: 226 us -> 162 us (0.72)
  Pallas kernels: 125 us -> 63.1 us
  starting transfers between devices: 22.6 us -> 12.8 us
  waiting for transfers between devices: 5.77 us -> 13.6 us
    pallas_call x2, Pallas kernels: 60 us -> 23.1 us  [grid_stage(): pl.pallas_call(body, grid=(steps,), in_specs=in_specs, out_specs=pl.Block...]
    pallas_call x2, Pallas kernels: 43.9 us -> 20.5 us  [block_stage(): pl.pallas_call(body, grid=(steps,), in_specs=[strip(CHANNELS), strip(EXPA...]
    all_to_all x2, waiting for transfers between devices: 0.01 us -> 12.8 us  [exchange(): return lax.all_to_all(x, axes, split_axis=0, concat_axis=0, tiled=True)]
    all_to_all x2, starting transfers between devices: 15.3 us -> 9.72 us  [exchange(): return lax.all_to_all(x, axes, split_axis=0, concat_axis=0, tiled=True)]
    ppermute x4, waiting for transfers between devices: 5.76 us -> 0.81 us  [by_pairs(): swaps.append(lax.ppermute(edge(last), axis, pairs))]
    ppermute x4, starting transfers between devices: 7.26 us -> 3.05 us  [by_pairs(): swaps.append(lax.ppermute(edge(last), axis, pairs))]
  transfers between devices with their start and end apart: 6 -> 6, of which waited for: 2 -> 3; matrix products, arithmetic and copies ran while one was open for 1% -> 2% of each run, Pallas kernels for 23% -> 16%
where the time goes in v3:
time: 162 us; the launch traced here: 161 us
  blocking collectives  63.5 us (39%)
  Pallas kernels  63.1 us (39%)
  waiting for transfers between devices  13.6 us (8%)
  starting transfers between devices  12.8 us (8%)
  local copies, waits for them, and re-layouts  7.05 us (4%)
    all_to_all x2, blocking collectives, exchange(): return lax.all_to_all(x, axes, split_axis=0, concat_axis=0, tiled=True)  63.5 us
    pallas_call x2, Pallas kernels, grid_stage(): pl.pallas_call(body, grid=(steps,), in_specs=in_specs, out_specs=pl.Block...  23.1 us
    pallas_call x2, Pallas kernels, block_stage(): pl.pallas_call(body, grid=(steps,), in_specs=[strip(CHANNELS), strip(EXPA...  20.5 us
    pallas_call x1, Pallas kernels, lift_stage(): pl.pallas_call(lift_kernel, grid=(4,), in_specs=[pl.BlockSpec(memory_spac...  19.5 us
    all_to_all x2, waiting for transfers between devices, exchange(): return lax.all_to_all(x, axes, split_axis=0, concat_axis=0, tiled=True)  12.8 us
    all_to_all x2, starting transfers between devices, exchange(): return lax.all_to_all(x, axes, split_axis=0, concat_axis=0, tiled=True)  9.72 us
  transfers between devices with their start and end apart: 6, of which 3 were waited for; matrix products, arithmetic and copies ran while one was open for 2% of the time, Pallas kernels for 16%

profile of v3, /device:TPU:0, one launch (start us, length us, event | category | flops | bytes accessed | tf_op | source)
XLA Modules:
  0.0 160.9 jit_solution(10708266885085007102)
XLA Ops:
  0.0 0.7 dynamic-slice_bitcast_fusion.2
  0.7 0.9 dynamic-slice_bitcast_fusion
  1.7 0.7 collective-permute-start.1
  2.4 1.0 constant_dynamic-slice_fusion.3
  3.5 0.8 constant_dynamic-slice_fusion
  4.4 0.3 concatenate.14
  4.6 1.6 %collective-permute-start.2 = (f32[44,128]{1,0:T(8,128)S(1)}, f32[44,128]{1,0:T(8,128)S(1)}, u32[]{:S(2)}, u32[]{:S(2)}) collective-permute-start(f32[44,128]{1,0:T(8,128)S(1)} %concatenate.14), channel_id=1, source_target_pairs={{0,1},{2,3},{4,5},{6,7},{1,0},{3,2},{5,4},{7,6},{8,9},{10,11},{12,... | collective-permute-start | bytes 67592 | tf_op jit(solution)/shard_map/ppermute | solution.py:572
  6.5 0.7 collective-permute-start.3
  7.1 0.6 pad_add_fusion.place_ref
  7.7 0.8 collective-permute-done.2.cols_a_ref
  8.5 0.6 copy-done.4
  9.1 19.5 %shard_map.136 = (f32[32,128,128]{2,1,0:T(8,128)}, f32[32,128,512]{2,1,0:T(8,128)}, f32[128,128]{1,0:T(8,128)}) custom-call(s32[2]{0:T(128)} %pad_add_fusion.place_ref, f32[32,128,128]{2,1,0:T(8,128)} %field_ref.1, f32[8,32,128]{2,1,0:T(8,128)} %context_ref.1, f32[160,128]{1,0:T(8,128)} %copy-done.2, f32[160,128]{1,0:T(8,128)} %copy-done.3, ...), custom_call_target="tpu_custom_call" | custom-call | flops 8000000000 | bytes 14000000 | tf_op jit(solution)/shard_map/pallas_call | solution.py:378
  28.6 29.5 %all_to_all.20 = f32[128,1,128]{2,1,0:T(1,128)} all-to-all(f32[128,1,128]{2,1,0:T(1,128)} %bitcast.30), channel_id=1, replica_groups=mesh['rg'=8,'core'=2,'col'=8] {'rg','core','col'}, dimensions={0} | all-to-all | bytes 131072 | tf_op jit(solution)/shard_map/all_to_all | solution.py:617
  58.1 8.6 %shard_map.138 = f32[2048,128]{1,0:T(8,128)} custom-call(f32[32,128,128]{2,1,0:T(8,128)} %get-tuple-element.8.refs_0_, f32[32,128,512]{2,1,0:T(8,128)} %get-tuple-element.9.refs_1_, f32[128,128]{1,0:T(8,128)} %bitcast.28, f32[32,512]{1,0:T(8,128)} %refs_3_.5, f32[512,128]{1,0:T(8,128)} %refs_4_.5, f32[5,128]{1,0:T(8,128)} %refs_1_.3, ...), custom_call_target="tpu_custom_call" | custom-call | flops 14000000000 | bytes 8000000 | tf_op jit(solution)/shard_map/pallas_call | solution.py:482
  66.7 5.1 %all-to-all-start.2 = ((f32[64,32,128]{2,1,0:T(8,128)}), f32[64,32,128]{2,1,0:T(8,128)S(1)}, u32[]{:S(2)}, u32[]{:S(2)}) async-start(f32[64,32,128]{2,1,0:T(8,128)} %bitcast.27), calls=%async_computation.2 | async-start | bytes 2097152 | tf_op jit(solution)/shard_map/all_to_all | solution.py:617
  71.8 12.0 %shard_map.137 = f32[2048,128]{1,0:T(8,128)} custom-call(f32[32,128,128]{2,1,0:T(8,128)} %get-tuple-element.8.refs_0_, f32[32,128,512]{2,1,0:T(8,128)} %get-tuple-element.9.refs_1_, f32[128,128]{1,0:T(8,128)} %bitcast.29, f32[32,512]{1,0:T(8,128)} %refs_3_.5, f32[512,128]{1,0:T(8,128)} %refs_4_.5, f32[5,128]{1,0:T(8,128)} %refs_1_.3, ...), custom_call_target="tpu_custom_call" | custom-call | flops 14000000000 | bytes 8000000 | tf_op jit(solution)/shard_map/pallas_call | solution.py:482
  83.7 7.4 %all-to-all-done.2.refs_0_ = f32[64,32,128]{2,1,0:T(8,128)S(1)} async-done(((f32[64,32,128]{2,1,0:T(8,128)}), f32[64,32,128]{2,1,0:T(8,128)S(1)}, u32[]{:S(2)}, u32[]{:S(2)}) %all-to-all-start.2) | async-done | bytes 1048608 | tf_op jit(solution)/shard_map/all_to_all | solution.py:617
  91.1 4.7 %all-to-all-start.1 = ((f32[64,32,128]{2,1,0:T(8,128)}), f32[64,32,128]{2,1,0:T(8,128)S(1)}, u32[]{:S(2)}, u32[]{:S(2)}) async-start(f32[64,32,128]{2,1,0:T(8,128)} %bitcast.26), calls=%async_computation.1 | async-start | bytes 2097152 | tf_op jit(solution)/shard_map/all_to_all | solution.py:617
  95.8 13.0 %shard_map.139.refs_6_ = f32[64,64,128]{2,1,0:T(8,128)} custom-call(f32[64,32,128]{2,1,0:T(8,128)} %copy-done, f32[5,128]{1,0:T(8,128)} %refs_1_.3, f32[2,128,384]{2,1,0:T(8,128)} %refs_2_.3, f32[2,128,128]{2,1,0:T(8,128)} %refs_3_.7, f32[2,128,512]{2,1,0:T(8,128)} %refs_4_.7, f32[2,512,128]{2,1,0:T(8,128)} %refs_5_.7, f32[2,128,512]{2,1,0:T(8,128)} %refs_4_.7, ...), custom_call_target="tpu_custom_call" | custom-call | flops 14000000000 | bytes 4000000 | tf_op jit(solution)/shard_map/pallas_call | solution.py:551
  108.8 5.5 %all-to-all-done.1.refs_0_ = f32[64,32,128]{2,1,0:T(8,128)S(1)} async-done(((f32[64,32,128]{2,1,0:T(8,128)}), f32[64,32,128]{2,1,0:T(8,128)S(1)}, u32[]{:S(2)}, u32[]{:S(2)}) %all-to-all-start.1) | async-done | bytes 1048608 | tf_op jit(solution)/shard_map/all_to_all | solution.py:617
  114.2 1.0 copy-done.1
  115.2 10.1 %shard_map.140 = f32[64,64,128]{2,1,0:T(8,128)} custom-call(f32[64,32,128]{2,1,0:T(8,128)} %copy-done.1, f32[5,128]{1,0:T(8,128)} %refs_1_.3, f32[2,128,384]{2,1,0:T(8,128)} %refs_2_.3, f32[2,128,128]{2,1,0:T(8,128)} %refs_3_.7, f32[2,128,512]{2,1,0:T(8,128)} %refs_4_.7, f32[2,512,128]{2,1,0:T(8,128)} %refs_5_.7, ...), custom_call_target="tpu_custom_call", output_to_operand_aliasing={{}: (6, {})} | custom-call | flops 14000000000 | bytes 4000000 | tf_op jit(solution)/shard_map/pallas_call | solution.py:551
  125.3 34.0 %all_to_all.21 = f32[64,64,128]{2,1,0:T(8,128)S(1)} all-to-all(f32[64,64,128]{2,1,0:T(8,128)} %shard_map.140), channel_id=1, replica_groups=mesh['rg'=8,'core'=2,'col'=8] {'rg','col'}, dimensions={0} | all-to-all | bytes 4194304 | tf_op jit(solution)/shard_map/all_to_all | solution.py:617
  159.3 1.6 copy.18
  (22 shorter events, 0.4 us)
Async XLA Ops:
  1.6 2.6 %collective-permute-start = (f32[160,128]{1,0:T(8,128)S(1)}, f32[160,128]{1,0:T(8,128)S(1)}, u32[]{:S(2)}, u32[]{:S(2)}) collective-permute-start(f32[160,128]{1,0:T(8,128)S(1)} %pad_maximum_fusion), channel_id=1, source_target_pairs={{0,8},{16,24},{32,40},{48,56},{64,72},{80,88},{96,104},{112,120},{... | collective-permute-start | bytes 245768 | tf_op jit(solution)/shard_map/ppermute | solution.py:572
  1.7 2.6 %collective-permute-start.1 = (f32[160,128]{1,0:T(8,128)S(1)}, f32[160,128]{1,0:T(8,128)S(1)}, u32[]{:S(2)}, u32[]{:S(2)}) collective-permute-start(f32[160,128]{1,0:T(8,128)S(1)} %pad_maximum_fusion.1), channel_id=1, source_target_pairs={{8,16},{24,32},{40,48},{56,64},{72,80},{88,96},{104,112},{16,8},{3... | collective-permute-start | bytes 245768 | tf_op jit(solution)/shard_map/ppermute | solution.py:572
  4.3 4.3 %copy-start.2 = (f32[160,128]{1,0:T(8,128)}, f32[160,128]{1,0:T(8,128)S(1)}, u32[]{:S(2)}) copy-start(f32[160,128]{1,0:T(8,128)S(1)} %collective-permute-done.rows_a_ref) | copy-start | bytes 245764
  4.3 4.2 %copy-start.3 = (f32[160,128]{1,0:T(8,128)}, f32[160,128]{1,0:T(8,128)S(1)}, u32[]{:S(2)}) copy-start(f32[160,128]{1,0:T(8,128)S(1)} %collective-permute-done.1.rows_b_ref) | copy-start | bytes 245764
  4.6 3.9 %collective-permute-start.2 = (f32[44,128]{1,0:T(8,128)S(1)}, f32[44,128]{1,0:T(8,128)S(1)}, u32[]{:S(2)}, u32[]{:S(2)}) collective-permute-start(f32[44,128]{1,0:T(8,128)S(1)} %concatenate.14), channel_id=1, source_target_pairs={{0,1},{2,3},{4,5},{6,7},{1,0},{3,2},{5,4},{7,6},{8,9},{10,11},{12,... | collective-permute-start | bytes 67592 | tf_op jit(solution)/shard_map/ppermute | solution.py:572
  6.5 2.1 %collective-permute-start.3 = (f32[44,128]{1,0:T(8,128)S(1)}, f32[44,128]{1,0:T(8,128)S(1)}, u32[]{:S(2)}, u32[]{:S(2)}) collective-permute-start(f32[44,128]{1,0:T(8,128)S(1)} %concatenate.15), channel_id=1, source_target_pairs={{1,2},{3,4},{5,6},{2,1},{4,3},{6,5},{9,10},{11,12},{13,14},{10,9},... | collective-permute-start | bytes 67592 | tf_op jit(solution)/shard_map/ppermute | solution.py:572
  8.5 0.6 copy-start.4
  8.5 0.6 copy-start.5
  66.7 24.4 %all-to-all-start.2 = ((f32[64,32,128]{2,1,0:T(8,128)}), f32[64,32,128]{2,1,0:T(8,128)S(1)}, u32[]{:S(2)}, u32[]{:S(2)}) async-start(f32[64,32,128]{2,1,0:T(8,128)} %bitcast.27), calls=%async_computation.2 | async-start | bytes 2097152 | tf_op jit(solution)/shard_map/all_to_all | solution.py:617
  91.1 4.7 %copy-start = (f32[64,32,128]{2,1,0:T(8,128)}, f32[64,32,128]{2,1,0:T(8,128)S(1)}, u32[]{:S(2)}) copy-start(f32[64,32,128]{2,1,0:T(8,128)S(1)} %all-to-all-done.2.refs_0_) | copy-start | bytes 3145732
  91.1 23.1 %all-to-all-start.1 = ((f32[64,32,128]{2,1,0:T(8,128)}), f32[64,32,128]{2,1,0:T(8,128)S(1)}, u32[]{:S(2)}, u32[]{:S(2)}) async-start(f32[64,32,128]{2,1,0:T(8,128)} %bitcast.26), calls=%async_computation.1 | async-start | bytes 2097152 | tf_op jit(solution)/shard_map/all_to_all | solution.py:617
  114.2 1.0 copy-start.1

commit v4 on v3

--- a/solution.py
+++ b/solution.py
@@ -26,7 +26,8 @@
 CHUNKS = 2
 BLOCK_STEP = 1024
 GRID_STEP = 2048
-VMEM_LIMIT = 56 * 1024 * 1024
+LIFT_VMEM = 32 * 1024 * 1024
+VMEM_LIMIT = 24 * 1024 * 1024
 
 GELU_A = 2.0 * math.sqrt(2.0 / math.pi)
 GELU_B = 4.0 * GELU_A * 0.044715
@@ -225,9 +226,10 @@
             if weight:
                 fine[at, (k + step) % 40] = weight
 
-    for column in range(129):
-        fill(column, column)
-    fill(135, -1)
+    for column in range(128):
+        fill(8 * (column % 16) + column // 16, column)
+    fill(128, -1)
+    fill(135, 128)
     return np.concatenate([fine, fine], axis=1)
 
 
@@ -247,12 +249,14 @@
     def _():
         expand3[...] = stack_rows(gained(0.5 * expand_ref[...], gains_ref[0:1]))
         total[...] = jnp.zeros_like(total)
-        lift[1:33, :128] = field_ref[...]
+        for t in range(16):
+            lift[1:33, 8 * t : 8 * t + 8] = field_ref[:, pl.ds(t, 8, stride=16), :]
         ctx[1:9, :32] = context_ref[...]
 
         def take_rows(above_ref, below_ref):
-            lift[0, :128] = above_ref[:128]
-            lift[33, :128] = below_ref[:128]
+            for t in range(16):
+                lift[0, 8 * t : 8 * t + 8] = above_ref[pl.ds(t, 8, stride=16), :]
+                lift[33, 8 * t : 8 * t + 8] = below_ref[pl.ds(t, 8, stride=16), :]
             ctx[0, :32] = above_ref[128:]
             ctx[9, :32] = below_ref[128:]
 
@@ -261,11 +265,10 @@
             for e in range(44):
                 after = jnp.broadcast_to(after_ref[e : e + 1], (8, 128))
                 before = jnp.broadcast_to(before_ref[e : e + 1], (8, 128))
-                group = jnp.where(first_row, after, jnp.where(last_row, before, zero))
                 if e < 34:
-                    lift[e, 128:] = group
+                    lift[e, 128:] = jnp.where(first_row, before, jnp.where(last_row, after, zero))
                 else:
-                    ctx[e - 34, 32:] = group
+                    ctx[e - 34, 32:] = jnp.where(first_row, after, jnp.where(last_row, before, zero))
 
         pl.when(place_ref[0] % 2 == 0)(lambda: take_rows(rows_b_ref, rows_a_ref))
         pl.when(place_ref[0] % 2 == 1)(lambda: take_rows(rows_a_ref, rows_b_ref))
@@ -279,7 +282,7 @@
 
     has_after = jnp.where(place_ref[1] < 7, 1.0, 0.0)
     has_before = jnp.where(place_ref[1] > 0, 1.0, 0.0)
-    inside = jnp.where(first_row, has_after, has_before)
+    inside = jnp.where(first_row, has_before, has_after)
 
     def hidden_rows(first, fine_first, k_first, count):
         parts = []
@@ -315,7 +318,8 @@
     def _():
         hid[33] = jnp.zeros((WIDE, EXPANDED), F32)
 
-    lifted_ref[...] = lift[pl.ds(8 * step + 1, 8), :128]
+    for t in range(16):
+        lifted_ref[:, pl.ds(t, 8, stride=16), :] = lift[pl.ds(8 * step + 1, 8), 8 * t : 8 * t + 8]
 
     for part in range(EXPANDED // 128):
         lanes = slice(part * 128, (part + 1) * 128)
@@ -325,26 +329,23 @@
         ]
 
         def row(r, summed):
-            def columns(g):
-                seen = [hid[8 * step + r + i, 8 * g : 8 * g + 8, lanes] for i in range(3)]
-                a, b, c = (
+            def column(t):
+                seen = [hid[8 * step + r + i, 8 * t : 8 * t + 8, lanes] for i in range(3)]
+                return [
                     seen[0] * taps[0][j] + seen[1] * taps[1][j] + seen[2] * taps[2][j]
                     for j in range(3)
-                )
-                return pltpu.roll(a, 1, 0), b, pltpu.roll(c, 7, 0)
-
-            halo = columns(16)
-            held, here = halo[0], columns(0)
-            for g in range(16):
-                following = columns(g + 1) if g < 15 else halo
-                out = gelu_of_half(
-                    here[1]
-                    + jnp.where(first_row, held, here[0])
-                    + jnp.where(last_row, following[2], here[2])
-                )
-                active_ref[r, 8 * g : 8 * g + 8, lanes] = out
+                ]
+
+            first, last, halo = column(0), column(15), column(16)
+            before = jnp.where(first_row, halo[0], pltpu.roll(last[0], 1, 0))
+            end = jnp.where(last_row, halo[2], pltpu.roll(first[2], 7, 0))
+            here = first
+            for t in range(16):
+                following = column(t + 1) if t < 14 else last
+                out = gelu_of_half(here[1] + before + (following[2] if t < 15 else end))
+                active_ref[r, part, pl.ds(t, 8, stride=16), :] = out
                 summed = summed + out
-                held, here = here[0], following
+                before, here = here[0], following
             return summed
 
         summed = total[:, lanes]
@@ -381,12 +382,12 @@
         in_specs=[pl.BlockSpec(memory_space=pltpu.SMEM)] + [whole(a.shape) for a in args],
         out_specs=[
             pl.BlockSpec((8, 128, CHANNELS), lambda s: (s, 0, 0)),
-            pl.BlockSpec((8, 128, EXPANDED), lambda s: (s, 0, 0)),
+            pl.BlockSpec((8, EXPANDED // 128, 128, 128), lambda s: (s, 0, 0, 0)),
             whole((copies, 128)),
         ],
         out_shape=[
             jax.ShapeDtypeStruct((32, 128, CHANNELS), F32),
-            jax.ShapeDtypeStruct((32, 128, EXPANDED), F32),
+            jax.ShapeDtypeStruct((32, EXPANDED // 128, 128, 128), F32),
             jax.ShapeDtypeStruct((copies, 128), F32),
         ],
         scratch_shapes=[
@@ -397,7 +398,7 @@
             pltpu.VMEM((3 * CHANNELS, EXPANDED), BF16),
             pltpu.VMEM((8, EXPANDED), F32),
         ],
-        compiler_params=pltpu.CompilerParams(vmem_limit_bytes=VMEM_LIMIT),
+        compiler_params=pltpu.CompilerParams(vmem_limit_bytes=LIFT_VMEM),
         cost_estimate=pl.CostEstimate(
             flops=8_000_000_000, bytes_accessed=14_000_000, transcendentals=0
         ),
@@ -423,8 +424,11 @@
     def projected(start):
         highs, lows = [], []
         for w in range(start, start + PART // CELLS):
-            cells = active_ref[:, 8 * w : 8 * w + 8, :].reshape(CELLS, EXPANDED)
-            high, low = split(cells)
+            cells = [
+                active_ref[:, k, 8 * w : 8 * w + 8, :].reshape(CELLS, 128)
+                for k in range(EXPANDED // 128)
+            ]
+            high, low = split(lanes_of(cells))
             highs.append(high)
             lows.append(low)
         yield
@@ -471,10 +475,14 @@
     row_base = chunk * (4 // CHUNKS)
     rest = (sums, se_expand, project, gains)
 
-    def strip(channels):
-        return pl.BlockSpec(
-            (8, BLOCK_STEP // 8, channels), lambda s: (row_base + s // per_row, s % per_row, 0)
-        )
+    columns = BLOCK_STEP // 8
+    strips = [
+        pl.BlockSpec((8, columns, CHANNELS), lambda s: (row_base + s // per_row, s % per_row, 0)),
+        pl.BlockSpec(
+            (8, EXPANDED // 128, columns, 128),
+            lambda s: (row_base + s // per_row, 0, s % per_row, 0),
+        ),
+    ]
 
     def body(*refs):
         block_kernel(cells_total, fed, *refs)
@@ -482,7 +490,7 @@
     return pl.pallas_call(
         body,
         grid=(steps,),
-        in_specs=[strip(CHANNELS), strip(EXPANDED)]
+        in_specs=strips
         + [whole(a.shape) for a in rest]
         + [of_layer(w, 0) for w in weights],
         out_specs=pl.BlockSpec((BLOCK_STEP, CHANNELS), lambda s: (s, 0)),

time: 162 us -> 168 us (1.037)
  local copies, waits for them, and re-layouts: 7.05 us -> 23.7 us
  Pallas kernels: 63.1 us -> 53.7 us
  waiting for transfers between devices: 13.6 us -> 10.4 us
  starting transfers between devices: 12.8 us -> 14.6 us
    unnamed x12 -> x50, local copies, waits for them, and re-layouts: 1.59 us -> 18.3 us
    pallas_call x2, Pallas kernels: 20.5 us -> 16.4 us  [block_stage(): pl.pallas_call(body, grid=(steps,), in_specs=strips + [whole(a.shape) for...]
    all_to_all x2, waiting for transfers between devices: 12.8 us -> 9.12 us  [exchange(): return lax.all_to_all(x, axes, split_axis=0, concat_axis=0, tiled=True)]
    pallas_call x2, Pallas kernels: 23.1 us -> 19.7 us  [grid_stage(): pl.pallas_call(body, grid=(steps,), in_specs=in_specs, out_specs=pl.Block...]
    all_to_all x2, starting transfers between devices: 9.72 us -> 11.6 us  [exchange(): return lax.all_to_all(x, axes, split_axis=0, concat_axis=0, tiled=True)]
    pallas_call x1, Pallas kernels: 19.5 us -> 17.7 us  [lift_stage(): pl.pallas_call(lift_kernel, grid=(4,), in_specs=[pl.BlockSpec(memory_spac...]
  transfers between devices with their start and end apart: 6 -> 6, of which waited for: 3 -> 3; matrix products, arithmetic and copies ran while one was open for 2% -> 1% of each run, Pallas kernels for 16% -> 12%
where the time goes in v4:
time: 168 us; the launch traced here: 166 us
  blocking collectives  63.5 us (38%)
  Pallas kernels  53.7 us (32%)
  local copies, waits for them, and re-layouts  23.7 us (14%)
  starting transfers between devices  14.6 us (9%)
  waiting for transfers between devices  10.4 us (6%)
    all_to_all x2, blocking collectives, exchange(): return lax.all_to_all(x, axes, split_axis=0, concat_axis=0, tiled=True)  63.5 us
    pallas_call x2, Pallas kernels, grid_stage(): pl.pallas_call(body, grid=(steps,), in_specs=in_specs, out_specs=pl.Block...  19.7 us
    unnamed x50, local copies, waits for them, and re-layouts  18.3 us
    pallas_call x1, Pallas kernels, lift_stage(): pl.pallas_call(lift_kernel, grid=(4,), in_specs=[pl.BlockSpec(memory_spac...  17.7 us
    pallas_call x2, Pallas kernels, block_stage(): pl.pallas_call(body, grid=(steps,), in_specs=strips + [whole(a.shape) for...  16.4 us
    all_to_all x2, starting transfers between devices, exchange(): return lax.all_to_all(x, axes, split_axis=0, concat_axis=0, tiled=True)  11.6 us
    all_to_all x2, waiting for transfers between devices, exchange(): return lax.all_to_all(x, axes, split_axis=0, concat_axis=0, tiled=True)  9.12 us
  transfers between devices with their start and end apart: 6, of which 3 were waited for; matrix products, arithmetic and copies ran while one was open for 1% of the time, Pallas kernels for 12%

profile of v4, /device:TPU:0, one launch (start us, length us, event | category | flops | bytes accessed | tf_op | source)
XLA Modules:
  0.0 166.4 jit_solution(1951993289860183309)
XLA Ops:
  2.4 1.0 constant_dynamic-slice_fusion.3
  4.6 1.6 collective-permute-start.2
  7.2 1.3 collective-permute-done.2.cols_a_ref
  8.5 1.6 copy-done
  10.1 0.9 copy-done.1
  11.0 0.9 copy-done.9
  15.9 17.7 %shard_map.136 = (f32[32,128,128]{2,1,0:T(8,128)S(1)}, f32[32,4,128,128]{3,2,1,0:T(8,128)S(1)}, f32[128,128]{1,0:T(8,128)S(1)}) custom-call(s32[2]{0:T(128)S(1)} %pad_add_fusion.place_ref, f32[32,128,128]{2,1,0:T(8,128)S(1)} %copy-done, f32[8,32,128]{2,1,0:T(8,128)S(1)} %copy-done.1, f32[160,128]{1,0:T(8,128)S(1)} %collective-permute-done.rows_a_ref, ...), custom_call_target="tpu_custom_call" | custom-call | flops 8000000000 | bytes 14000000 | tf_op jit(solution)/shard_map/pallas_call | solution.py:379
  33.6 28.9 %all_to_all.20 = f32[128,1,128]{2,1,0:T(1,128)S(1)} all-to-all(f32[128,1,128]{2,1,0:T(1,128)S(1)} %bitcast.27), channel_id=1, replica_groups=mesh['rg'=8,'core'=2,'col'=8] {'rg','core','col'}, dimensions={0} | all-to-all | bytes 131072 | tf_op jit(solution)/shard_map/all_to_all | solution.py:625
  62.5 6.5 %shard_map.138 = f32[2048,128]{1,0:T(8,128)} custom-call(f32[32,128,128]{2,1,0:T(8,128)S(1)} %get-tuple-element.8.refs_0_, f32[32,4,128,128]{3,2,1,0:T(8,128)S(1)} %get-tuple-element.9.refs_1_, f32[128,128]{1,0:T(8,128)S(1)} %bitcast.25, f32[32,512]{1,0:T(8,128)S(1)} %copy-done.16, f32[512,128]{1,0:T(8,128)S(1)} %copy-done.10, f32[5,128]{1,0:T(8,128)S(1)} %copy-done.18, ...), custom_call_target="tpu_custom_call" | custom-call | flops 14000000000 | bytes 8000000 | tf_op jit(solution)/shard_map/pallas_call | solution.py:490
  69.1 5.3 %all-to-all-start.2 = ((f32[64,32,128]{2,1,0:T(8,128)}), f32[64,32,128]{2,1,0:T(8,128)S(1)}, u32[]{:S(2)}, u32[]{:S(2)}) async-start(f32[64,32,128]{2,1,0:T(8,128)} %bitcast.15), calls=%async_computation.2 | async-start | bytes 2097152 | tf_op jit(solution)/shard_map/all_to_all | solution.py:625
  74.4 3.4 %copy-done.22 = f32[32,4,128,128]{3,2,1,0:T(8,128)S(1)} copy-done((f32[32,4,128,128]{3,2,1,0:T(8,128)S(1)}, f32[32,4,128,128]{3,2,1,0:T(8,128)}, u32[]{:S(2)}) %copy-start.22) | copy-done | bytes 8388632
  77.8 1.6 copy-done.24
  79.4 9.9 %shard_map.137 = f32[2048,128]{1,0:T(8,128)} custom-call(f32[32,128,128]{2,1,0:T(8,128)S(1)} %copy-done.24, f32[32,4,128,128]{3,2,1,0:T(8,128)S(1)} %copy-done.22, f32[128,128]{1,0:T(8,128)S(1)} %bitcast.26, f32[32,512]{1,0:T(8,128)S(1)} %copy-done.16, f32[512,128]{1,0:T(8,128)S(1)} %copy-done.10, f32[5,128]{1,0:T(8,128)S(1)} %copy-done.19, ...), custom_call_target="tpu_custom_call" | custom-call | flops 14000000000 | bytes 8000000 | tf_op jit(solution)/shard_map/pallas_call | solution.py:490
  89.3 4.2 %all-to-all-done.2.refs_0_ = f32[64,32,128]{2,1,0:T(8,128)S(1)} async-done(((f32[64,32,128]{2,1,0:T(8,128)}), f32[64,32,128]{2,1,0:T(8,128)S(1)}, u32[]{:S(2)}, u32[]{:S(2)}) %all-to-all-start.2) | async-done | bytes 1048608 | tf_op jit(solution)/shard_map/all_to_all | solution.py:625
  93.5 6.2 %all-to-all-start.1 = ((f32[64,32,128]{2,1,0:T(8,128)}), f32[64,32,128]{2,1,0:T(8,128)}, u32[]{:S(2)}, u32[]{:S(2)}) async-start(f32[64,32,128]{2,1,0:T(8,128)} %bitcast.14), calls=%async_computation.1 | async-start | bytes 2097152 | tf_op jit(solution)/shard_map/all_to_all | solution.py:625
  99.7 1.0 copy-done.3
  100.8 1.0 copy-done.6
  102.7 10.6 %shard_map.139.refs_6_ = f32[64,64,128]{2,1,0:T(8,128)S(1)} custom-call(f32[64,32,128]{2,1,0:T(8,128)S(1)} %all-to-all-done.2.refs_0_, f32[5,128]{1,0:T(8,128)S(1)} %copy-done.19, f32[2,128,384]{2,1,0:T(8,128)S(1)} %copy-done.8, f32[2,128,128]{2,1,0:T(8,128)S(1)} %copy-done.12, f32[2,128,512]{2,1,0:T(8,128)S(1)} %copy-done.3, f32[2,512,128]{2,1,0:T(8,128)S(1)} %copy-done.6, ...), custom_call_target="tpu_custom_call" | custom-call | flops 14000000000 | bytes 4000000 | tf_op jit(solution)/shard_map/pallas_call | solution.py:559
  113.4 4.9 %all-to-all-done.1.refs_0_ = f32[64,32,128]{2,1,0:T(8,128)} async-done(((f32[64,32,128]{2,1,0:T(8,128)}), f32[64,32,128]{2,1,0:T(8,128)}, u32[]{:S(2)}, u32[]{:S(2)}) %all-to-all-start.1) | async-done | bytes 1048608 | tf_op jit(solution)/shard_map/all_to_all | solution.py:625
  118.3 1.0 copy-done.4
  119.3 1.0 copy-done.7
  121.3 9.0 %shard_map.140 = f32[64,64,128]{2,1,0:T(8,128)S(1)} custom-call(f32[64,32,128]{2,1,0:T(8,128)} %all-to-all-done.1.refs_0_, f32[5,128]{1,0:T(8,128)S(1)} %copy-done.19, f32[2,128,384]{2,1,0:T(8,128)S(1)} %copy-done.8, f32[2,128,128]{2,1,0:T(8,128)S(1)} %copy-done.13, f32[2,128,512]{2,1,0:T(8,128)S(1)} %copy-done.4, ...), custom_call_target="tpu_custom_call", output_to_operand_aliasing={{}: (6, {})} | custom-call | flops 14000000000 | bytes 4000000 | tf_op jit(solution)/shard_map/pallas_call | solution.py:559
  130.3 34.6 %all_to_all.21 = f32[64,64,128]{2,1,0:T(8,128)S(1)} all-to-all(f32[64,64,128]{2,1,0:T(8,128)S(1)} %shard_map.140), channel_id=1, replica_groups=mesh['rg'=8,'core'=2,'col'=8] {'rg','col'}, dimensions={0} | all-to-all | bytes 4194304 | tf_op jit(solution)/shard_map/all_to_all | solution.py:625
  164.9 1.6 copy.18
  (60 shorter events, 10.1 us)
Async XLA Ops:
  1.6 2.6 %collective-permute-start = (f32[160,128]{1,0:T(8,128)S(1)}, f32[160,128]{1,0:T(8,128)S(1)}, u32[]{:S(2)}, u32[]{:S(2)}) collective-permute-start(f32[160,128]{1,0:T(8,128)S(1)} %pad_maximum_fusion), channel_id=1, source_target_pairs={{0,8},{16,24},{32,40},{48,56},{64,72},{80,88},{96,104},{112,120},{... | collective-permute-start | bytes 245768 | tf_op jit(solution)/shard_map/ppermute | solution.py:580
  1.7 2.5 %collective-permute-start.1 = (f32[160,128]{1,0:T(8,128)S(1)}, f32[160,128]{1,0:T(8,128)S(1)}, u32[]{:S(2)}, u32[]{:S(2)}) collective-permute-start(f32[160,128]{1,0:T(8,128)S(1)} %pad_maximum_fusion.1), channel_id=1, source_target_pairs={{8,16},{24,32},{40,48},{56,64},{72,80},{88,96},{104,112},{16,8},{3... | collective-permute-start | bytes 245768 | tf_op jit(solution)/shard_map/ppermute | solution.py:580
  4.6 3.9 %collective-permute-start.2 = (f32[44,128]{1,0:T(8,128)S(1)}, f32[44,128]{1,0:T(8,128)S(1)}, u32[]{:S(2)}, u32[]{:S(2)}) collective-permute-start(f32[44,128]{1,0:T(8,128)S(1)} %concatenate.14), channel_id=1, source_target_pairs={{0,1},{2,3},{4,5},{6,7},{1,0},{3,2},{5,4},{7,6},{8,9},{10,11},{12,... | collective-permute-start | bytes 67592 | tf_op jit(solution)/shard_map/ppermute | solution.py:580
  6.5 2.1 %collective-permute-start.3 = (f32[44,128]{1,0:T(8,128)S(1)}, f32[44,128]{1,0:T(8,128)S(1)}, u32[]{:S(2)}, u32[]{:S(2)}) collective-permute-start(f32[44,128]{1,0:T(8,128)S(1)} %concatenate.15), channel_id=1, source_target_pairs={{1,2},{3,4},{5,6},{2,1},{4,3},{6,5},{9,10},{11,12},{13,14},{10,9},... | collective-permute-start | bytes 67592 | tf_op jit(solution)/shard_map/ppermute | solution.py:580
  8.5 1.6 copy-start
  10.1 0.9 copy-start.1
  11.0 0.9 copy-start.9
  15.8 46.7 %copy-start.2 = (f32[2,128,512]{2,1,0:T(8,128)S(1)}, f32[2,128,512]{2,1,0:T(8,128)}, u32[]{:S(2)}) copy-start(f32[2,128,512]{2,1,0:T(8,128)} %refs_4_.7) | copy-start | bytes 1572868
  15.8 46.7 %copy-start.5 = (f32[2,512,128]{2,1,0:T(8,128)S(1)}, f32[2,512,128]{2,1,0:T(8,128)}, u32[]{:S(2)}) copy-start(f32[2,512,128]{2,1,0:T(8,128)} %refs_5_.7) | copy-start | bytes 1572868
  15.8 46.7 %copy-start.8 = (f32[2,128,384]{2,1,0:T(8,128)S(1)}, f32[2,128,384]{2,1,0:T(8,128)}, u32[]{:S(2)}) copy-start(f32[2,128,384]{2,1,0:T(8,128)} %refs_2_.3) | copy-start | bytes 1179652
  15.8 46.7 %copy-start.10 = (f32[512,128]{1,0:T(8,128)S(1)}, f32[512,128]{1,0:T(8,128)}, u32[]{:S(2)}) copy-start(f32[512,128]{1,0:T(8,128)} %refs_4_.5) | copy-start | bytes 786436
  15.8 46.7 %copy-start.11 = (f32[2,128,128]{2,1,0:T(8,128)S(1)}, f32[2,128,128]{2,1,0:T(8,128)}, u32[]{:S(2)}) copy-start(f32[2,128,128]{2,1,0:T(8,128)} %refs_3_.7) | copy-start | bytes 393220
  15.8 46.7 %copy-start.16 = (f32[32,512]{1,0:T(8,128)S(1)}, f32[32,512]{1,0:T(8,128)}, u32[]{:S(2)}) copy-start(f32[32,512]{1,0:T(8,128)} %refs_3_.5) | copy-start | bytes 196612
  33.5 35.5 %copy-start.21 = (f32[32,4,128,128]{3,2,1,0:T(8,128)}, f32[32,4,128,128]{3,2,1,0:T(8,128)S(1)}, u32[]{:S(2)}) copy-start(f32[32,4,128,128]{3,2,1,0:T(8,128)S(1)} %get-tuple-element.9.refs_1_) | copy-start | bytes 25165828
  33.5 35.5 %copy-start.23 = (f32[32,128,128]{2,1,0:T(8,128)}, f32[32,128,128]{2,1,0:T(8,128)S(1)}, u32[]{:S(2)}) copy-start(f32[32,128,128]{2,1,0:T(8,128)S(1)} %get-tuple-element.8.refs_0_) | copy-start | bytes 6291460
  69.1 5.3 %copy-start.19 = (f32[5,128]{1,0:T(8,128)S(1)}, f32[5,128]{1,0:T(8,128)}, u32[]{:S(2)}) copy-start(f32[5,128]{1,0:T(8,128)} %refs_1_.3) | copy-start | bytes 7684
  69.1 24.4 %all-to-all-start.2 = ((f32[64,32,128]{2,1,0:T(8,128)}), f32[64,32,128]{2,1,0:T(8,128)S(1)}, u32[]{:S(2)}, u32[]{:S(2)}) async-start(f32[64,32,128]{2,1,0:T(8,128)} %bitcast.15), calls=%async_computation.2 | async-start | bytes 2097152 | tf_op jit(solution)/shard_map/all_to_all | solution.py:625
  74.4 3.4 %copy-start.22 = (f32[32,4,128,128]{3,2,1,0:T(8,128)S(1)}, f32[32,4,128,128]{3,2,1,0:T(8,128)}, u32[]{:S(2)}) copy-start(f32[32,4,128,128]{3,2,1,0:T(8,128)} %copy-done.21) | copy-start | bytes 25165828
  77.8 1.6 copy-start.24
  93.5 24.8 %all-to-all-start.1 = ((f32[64,32,128]{2,1,0:T(8,128)}), f32[64,32,128]{2,1,0:T(8,128)}, u32[]{:S(2)}, u32[]{:S(2)}) async-start(f32[64,32,128]{2,1,0:T(8,128)} %bitcast.14), calls=%async_computation.1 | async-start | bytes 2097152 | tf_op jit(solution)/shard_map/all_to_all | solution.py:625
  99.7 1.0 copy-start.3
  100.8 1.0 copy-start.6
  118.3 1.0 copy-start.4
  119.3 1.0 copy-start.7
  (7 other events, 5.7 us)

commit v5 on v4

--- a/solution.py
+++ b/solution.py
@@ -19,6 +19,7 @@
 CELLS = WINDOW * WINDOW
 GROUP = 64
 WIDE = 136
+COARSE_WIDE = 48
 EPSILON = 1e-05
 F32 = jnp.float32
 BF16 = jnp.bfloat16
@@ -26,15 +27,15 @@
 CHUNKS = 2
 BLOCK_STEP = 1024
 GRID_STEP = 2048
-LIFT_VMEM = 32 * 1024 * 1024
-VMEM_LIMIT = 24 * 1024 * 1024
-
-GELU_A = 2.0 * math.sqrt(2.0 / math.pi)
-GELU_B = 4.0 * GELU_A * 0.044715
-
-
-def gelu_of_half(half):
-    return half * jnp.tanh(half * (GELU_A + GELU_B * (half * half))) + half
+VMEM_LIMIT = 56 * 1024 * 1024
+
+GELU_IN = (math.sqrt(2.0 / math.pi) * 0.044715) ** (1.0 / 3.0)
+GELU_OUT = 0.5 / GELU_IN
+GELU_LINEAR = math.sqrt(2.0 / math.pi) / GELU_IN
+
+
+def bend(s):
+    return s * (1.0 + jnp.tanh(s * (GELU_LINEAR + s * s)))
 
 
 def split(x):
@@ -92,8 +93,8 @@
 
 
 def prepare_feed(in_ref, mlp_ref, gain, in3, mlp_pair):
-    in3[...] = stack_rows(gained(0.5 * in_ref[0], gain))
-    mlp_pair[...] = deep_weight(mlp_ref[0])
+    in3[...] = stack_rows(gained(GELU_IN * in_ref[0], gain))
+    mlp_pair[...] = deep_weight(GELU_OUT * mlp_ref[0])
 
 
 PAIR = 2 * CELLS
@@ -183,7 +184,7 @@
     yield
     inner = dot(rows_of(parts), in3[...])
     yield
-    high, low = split_blocks(inner, 64, gelu_of_half)
+    high, low = split_blocks(inner, 64, bend)
     yield
     wide = dot(high, mlp_pair[...])
     rest = dot(low, mlp_pair[:, :CHANNELS])
@@ -216,13 +217,15 @@
     return rows_of(highs), rows_of(lows)
 
 
-def column_weights():
-    fine = np.zeros((WIDE, 40), np.float32)
-    table = ((0.375, 0.625, 0.0), (0.125, 0.875, 0.0), (0.0, 0.875, 0.125), (0.0, 0.625, 0.375))
+PHASES = ((0.375, 0.625, 0.0), (0.125, 0.875, 0.0), (0.0, 0.875, 0.125), (0.0, 0.625, 0.375))
+
+
+def lifting():
+    fine = np.zeros((WIDE + 8, COARSE_WIDE), np.float32)
 
     def fill(at, column):
         k, o = column // 4, column % 4
-        for step, weight in zip((-1, 0, 1), table[o]):
+        for step, weight in zip((-1, 0, 1), PHASES[o]):
             if weight:
                 fine[at, (k + step) % 40] = weight
 
@@ -230,10 +233,9 @@
         fill(8 * (column % 16) + column // 16, column)
     fill(128, -1)
     fill(135, 128)
-    return np.concatenate([fine, fine], axis=1)
-
-
-ROW_WEIGHTS = ((0.375, 0.625, -1), (0.125, 0.875, -1), (0.875, 0.125, 0), (0.625, 0.375, 0))
+    both = np.concatenate([fine, fine], axis=1)
+    pairs = (weights[:2] if weights[0] else weights[1:] for weights in PHASES)
+    return np.stack([np.concatenate([a * both, b * both], axis=1) for a, b in pairs])
 
 
 def lift_kernel(
@@ -247,7 +249,7 @@
 
     @pl.when(step == 0)
     def _():
-        expand3[...] = stack_rows(gained(0.5 * expand_ref[...], gains_ref[0:1]))
+        expand3[...] = stack_rows(gained(GELU_IN * expand_ref[...], gains_ref[0:1]))
         total[...] = jnp.zeros_like(total)
         for t in range(16):
             lift[1:33, 8 * t : 8 * t + 8] = field_ref[:, pl.ds(t, 8, stride=16), :]
@@ -268,17 +270,20 @@
                 if e < 34:
                     lift[e, 128:] = jnp.where(first_row, before, jnp.where(last_row, after, zero))
                 else:
-                    ctx[e - 34, 32:] = jnp.where(first_row, after, jnp.where(last_row, before, zero))
+                    ctx[e - 34, 32:40] = jnp.where(
+                        first_row, after, jnp.where(last_row, before, zero)
+                    )
+                    ctx[e - 34, 40:] = zero
 
         pl.when(place_ref[0] % 2 == 0)(lambda: take_rows(rows_b_ref, rows_a_ref))
         pl.when(place_ref[0] % 2 == 1)(lambda: take_rows(rows_a_ref, rows_b_ref))
         pl.when(place_ref[1] % 2 == 0)(lambda: take_columns(cols_b_ref, cols_a_ref))
         pl.when(place_ref[1] % 2 == 1)(lambda: take_columns(cols_a_ref, cols_b_ref))
         weight = stack_rows(ctxw_ref[...])
-        projected = dot(three(ctx[...].reshape(400, CHANNELS)), weight)
+        projected = dot(three(ctx[...].reshape(10 * COARSE_WIDE, CHANNELS)), weight)
         for k in range(10):
-            high, low = split(projected[40 * k : 40 * k + 40])
-            coarse[k] = dot(up_ref[...], rows_of([high, low]))
+            high, low = split(projected[COARSE_WIDE * k : COARSE_WIDE * (k + 1)])
+            coarse[2 * COARSE_WIDE * k : 2 * COARSE_WIDE * (k + 1)] = rows_of([high, low])
 
     has_after = jnp.where(place_ref[1] < 7, 1.0, 0.0)
     has_before = jnp.where(place_ref[1] > 0, 1.0, 0.0)
@@ -290,16 +295,17 @@
             two = []
             for j in (i, i + 1):
                 k, o = (fine_first + j) // 4, (fine_first + j) % 4
-                lower, upper, shift = ROW_WEIGHTS[o]
-                at = k_first + k + shift
-                x = lift[first + j] + (lower * coarse[at] + upper * coarse[at + 1])
+                at = k_first + k - (1 if PHASES[o][0] else 0)
+                at = pl.multiple_of(at * (2 * COARSE_WIDE), 2 * COARSE_WIDE)
+                two_rows = coarse[pl.ds(at, 4 * COARSE_WIDE)]
+                x = lift[first + j] + dot(up_ref[o], two_rows)[:WIDE]
                 lift[first + j] = x
                 two.append(x)
             parts.append(three(normed(rows_of(two))))
         made = dot(rows_of(parts), expand3[...])
         for i in range(count):
             for c in range(0, EXPANDED, 128):
-                out = gelu_of_half(made[i * WIDE : (i + 1) * WIDE, c : c + 128])
+                out = bend(made[i * WIDE : (i + 1) * WIDE, c : c + 128])
                 hid[first + i, :128, c : c + 128] = out[:128]
                 hid[first + i, 128:, c : c + 128] = out[128:] * inside
 
@@ -318,13 +324,12 @@
     def _():
         hid[33] = jnp.zeros((WIDE, EXPANDED), F32)
 
-    for t in range(16):
-        lifted_ref[:, pl.ds(t, 8, stride=16), :] = lift[pl.ds(8 * step + 1, 8), 8 * t : 8 * t + 8]
+    lifted_ref[...] = lift[pl.ds(8 * step + 1, 8), :128]
 
     for part in range(EXPANDED // 128):
         lanes = slice(part * 128, (part + 1) * 128)
         taps = [
-            [jnp.broadcast_to(0.5 * depth_ref[i, j : j + 1, lanes], (8, 128)) for j in range(3)]
+            [jnp.broadcast_to((GELU_IN * GELU_OUT) * depth_ref[i, j : j + 1, lanes], (8, 128)) for j in range(3)]
             for i in range(3)
         ]
 
@@ -342,8 +347,8 @@
             here = first
             for t in range(16):
                 following = column(t + 1) if t < 14 else last
-                out = gelu_of_half(here[1] + before + (following[2] if t < 15 else end))
-                active_ref[r, part, pl.ds(t, 8, stride=16), :] = out
+                out = bend(here[1] + before + (following[2] if t < 15 else end))
+                active_ref[r, 8 * t : 8 * t + 8, lanes] = out
                 summed = summed + out
                 before, here = here[0], following
             return summed
@@ -374,7 +379,7 @@
 
 
 def lift_stage(place, args, copies):
-    up = jnp.asarray(column_weights(), BF16)
+    up = jnp.asarray(lifting(), BF16)
     args = args[:6] + (up,) + args[6:]
     return pl.pallas_call(
         lift_kernel,
@@ -382,23 +387,23 @@
         in_specs=[pl.BlockSpec(memory_space=pltpu.SMEM)] + [whole(a.shape) for a in args],
         out_specs=[
             pl.BlockSpec((8, 128, CHANNELS), lambda s: (s, 0, 0)),
-            pl.BlockSpec((8, EXPANDED // 128, 128, 128), lambda s: (s, 0, 0, 0)),
+            pl.BlockSpec((8, 128, EXPANDED), lambda s: (s, 0, 0)),
             whole((copies, 128)),
         ],
         out_shape=[
             jax.ShapeDtypeStruct((32, 128, CHANNELS), F32),
-            jax.ShapeDtypeStruct((32, EXPANDED // 128, 128, 128), F32),
+            jax.ShapeDtypeStruct((32, 128, EXPANDED), F32),
             jax.ShapeDtypeStruct((copies, 128), F32),
         ],
         scratch_shapes=[
             pltpu.VMEM((34, WIDE, CHANNELS), F32),
-            pltpu.VMEM((10, 40, CHANNELS), F32),
-            pltpu.VMEM((10, WIDE, CHANNELS), F32),
+            pltpu.VMEM((10, COARSE_WIDE, CHANNELS), F32),
+            pltpu.VMEM((20 * COARSE_WIDE, CHANNELS), BF16),
             pltpu.VMEM((34, WIDE, EXPANDED), F32),
             pltpu.VMEM((3 * CHANNELS, EXPANDED), BF16),
             pltpu.VMEM((8, EXPANDED), F32),
         ],
-        compiler_params=pltpu.CompilerParams(vmem_limit_bytes=LIFT_VMEM),
+        compiler_params=pltpu.CompilerParams(vmem_limit_bytes=VMEM_LIMIT),
         cost_estimate=pl.CostEstimate(
             flops=8_000_000_000, bytes_accessed=14_000_000, transcendentals=0
         ),
@@ -407,48 +412,35 @@
 
 def block_kernel(
     cells_total, fed, lifted_ref, active_ref, sums_ref, sexp_ref, project_ref, gains_ref, qkv_ref,
-    aout_ref, min_ref, mout_ref, out_ref, project, k3, qv3, out3, *feed_weights,
+    aout_ref, min_ref, mout_ref, out_ref, project, sums, k3, qv3, out3, *feed_weights,
 ):
     @pl.when(pl.program_id(0) == 0)
     def _():
-        pooled = jnp.sum(sums_ref[...], axis=0, keepdims=True) * (1.0 / cells_total)
+        pooled = jnp.sum(sums_ref[...], axis=0, keepdims=True) * (GELU_OUT / cells_total)
         squeezed = pooled[:, :SQUEEZE]
         squeezed = squeezed * jax.nn.sigmoid(squeezed)
         wide = jnp.broadcast_to(squeezed, (CHANNELS, SQUEEZE))
         gate = jnp.dot(wide, sexp_ref[...], precision=HIGHEST, preferred_element_type=F32)
-        project[...] = deep_weight(project_ref[...] * jax.nn.sigmoid(gate).T)
+        project[...] = deep_weight(project_ref[...] * (GELU_OUT * jax.nn.sigmoid(gate)).T)
         prepare_attention(qkv_ref, aout_ref, gains_ref[1:2], k3, qv3, out3)
         if fed:
             prepare_feed(min_ref, mout_ref, gains_ref[2:3], *feed_weights)
 
-    def projected(start):
-        highs, lows = [], []
-        for w in range(start, start + PART // CELLS):
-            cells = [
-                active_ref[:, k, 8 * w : 8 * w + 8, :].reshape(CELLS, 128)
-                for k in range(EXPANDED // 128)
-            ]
-            high, low = split(lanes_of(cells))
-            highs.append(high)
-            lows.append(low)
-        yield
-        wide = dot(rows_of(highs), project[...])
-        rest = dot(rows_of(lows), project[:, :CHANNELS])
-        yield
-        pairs = []
-        for p in range(PART // PAIR):
-            at = slice(p * PAIR, (p + 1) * PAIR)
-            x = rows_of(
-                [
-                    lifted_ref[:, 8 * w : 8 * w + 8, :].reshape(CELLS, CHANNELS)
-                    for w in (start + 2 * p, start + 2 * p + 1)
-                ]
-            )
-            pairs.append(x + (wide[at, :CHANNELS] + (wide[at, CHANNELS:] + rest[at])))
-        return pairs
+    for half in range(0, 8, PART // 128):
+        rows = slice(half, half + PART // 128)
+        halves = [split(active_ref[r]) for r in range(half, half + PART // 128)]
+        wide = dot(rows_of([h[0] for h in halves]), project[...])
+        rest = dot(rows_of([h[1] for h in halves]), project[:, :CHANNELS])
+        added = wide[:, :CHANNELS] + (wide[:, CHANNELS:] + rest)
+        sums[rows] = lifted_ref[rows] + added.reshape(PART // 128, 128, CHANNELS)
+
+    def window(w):
+        at = pl.ds(64 * (w % 2) + w // 2, WINDOW, stride=8)
+        return rows_of([sums[r, at, :] for r in range(WINDOW)])
 
     def group(part):
-        pairs = yield from projected(part * PART // CELLS)
+        start = part * PART // CELLS
+        pairs = [rows_of([window(w), window(w + 1)]) for w in range(start, start + 8, 2)]
         pairs = yield from attend(pairs, k3, qv3, out3)
         if fed:
             pairs = yield from feed(pairs, *feed_weights)
@@ -475,14 +467,10 @@
     row_base = chunk * (4 // CHUNKS)
     rest = (sums, se_expand, project, gains)
 
-    columns = BLOCK_STEP // 8
-    strips = [
-        pl.BlockSpec((8, columns, CHANNELS), lambda s: (row_base + s // per_row, s % per_row, 0)),
-        pl.BlockSpec(
-            (8, EXPANDED // 128, columns, 128),
-            lambda s: (row_base + s // per_row, 0, s % per_row, 0),
-        ),
-    ]
+    def strip(channels):
+        return pl.BlockSpec(
+            (8, BLOCK_STEP // 8, channels), lambda s: (row_base + s // per_row, s % per_row, 0)
+        )
 
     def body(*refs):
         block_kernel(cells_total, fed, *refs)
@@ -490,12 +478,15 @@
     return pl.pallas_call(
         body,
         grid=(steps,),
-        in_specs=strips
+        in_specs=[strip(CHANNELS), strip(EXPANDED)]
         + [whole(a.shape) for a in rest]
         + [of_layer(w, 0) for w in weights],
         out_specs=pl.BlockSpec((BLOCK_STEP, CHANNELS), lambda s: (s, 0)),
         out_shape=jax.ShapeDtypeStruct((steps * BLOCK_STEP, CHANNELS), F32),
-        scratch_shapes=[pltpu.VMEM((EXPANDED, 2 * CHANNELS), BF16)]
+        scratch_shapes=[
+            pltpu.VMEM((EXPANDED, 2 * CHANNELS), BF16),
+            pltpu.VMEM((8, 128, CHANNELS), F32),
+        ]
         + ATTENTION_SCRATCH
         + (FEED_SCRATCH if fed else []),
         compiler_params=pltpu.CompilerParams(vmem_limit_bytes=VMEM_LIMIT),

time: 168 us -> 162 us (0.964)
  local copies, waits for them, and re-layouts: 23.7 us -> 7.05 us
  Pallas kernels: 53.7 us -> 64.3 us
  waiting for transfers between devices: 10.4 us -> 13.4 us
  starting transfers between devices: 14.6 us -> 12.8 us
    unnamed x50 -> x12, local copies, waits for them, and re-layouts: 18.3 us -> 1.59 us
    pallas_call x2, Pallas kernels: 16.4 us -> 21.5 us  [block_stage(): pl.pallas_call(body, grid=(steps,), in_specs=[strip(CHANNELS), strip(EXPA...]
    all_to_all x2, waiting for transfers between devices: 9.12 us -> 12.6 us  [exchange(): return lax.all_to_all(x, axes, split_axis=0, concat_axis=0, tiled=True)]
    pallas_call x2, Pallas kernels: 19.7 us -> 22.5 us  [grid_stage(): pl.pallas_call(body, grid=(steps,), in_specs=in_specs, out_specs=pl.Block...]
    pallas_call x1, Pallas kernels: 17.7 us -> 20.3 us  [lift_stage(): pl.pallas_call(lift_kernel, grid=(4,), in_specs=[pl.BlockSpec(memory_spac...]
    all_to_all x2, starting transfers between devices: 11.6 us -> 9.73 us  [exchange(): return lax.all_to_all(x, axes, split_axis=0, concat_axis=0, tiled=True)]
  transfers between devices with their start and end apart: 6 -> 6, of which waited for: 3 -> 3; matrix products, arithmetic and copies ran while one was open for 1% -> 2% of each run, Pallas kernels for 12% -> 16%
where the time goes in v5:
time: 162 us
  Pallas kernels  64.3 us (40%)
  blocking collectives  63.2 us (39%)
  waiting for transfers between devices  13.4 us (8%)
  starting transfers between devices  12.8 us (8%)
  local copies, waits for them, and re-layouts  7.05 us (4%)
    all_to_all x2, blocking collectives, exchange(): return lax.all_to_all(x, axes, split_axis=0, concat_axis=0, tiled=True)  63.2 us
    pallas_call x2, Pallas kernels, grid_stage(): pl.pallas_call(body, grid=(steps,), in_specs=in_specs, out_specs=pl.Block...  22.5 us
    pallas_call x2, Pallas kernels, block_stage(): pl.pallas_call(body, grid=(steps,), in_specs=[strip(CHANNELS), strip(EXPA...  21.5 us
    pallas_call x1, Pallas kernels, lift_stage(): pl.pallas_call(lift_kernel, grid=(4,), in_specs=[pl.BlockSpec(memory_spac...  20.3 us
    all_to_all x2, waiting for transfers between devices, exchange(): return lax.all_to_all(x, axes, split_axis=0, concat_axis=0, tiled=True)  12.6 us
    all_to_all x2, starting transfers between devices, exchange(): return lax.all_to_all(x, axes, split_axis=0, concat_axis=0, tiled=True)  9.73 us
  transfers between devices with their start and end apart: 6, of which 3 were waited for; matrix products, arithmetic and copies ran while one was open for 2% of the time, Pallas kernels for 16%

profile of v5, /device:TPU:0, one launch (start us, length us, event | category | flops | bytes accessed | tf_op | source)
XLA Modules:
  0.0 161.6 jit_solution(15298260572504135576)
XLA Ops:
  0.0 0.7 dynamic-slice_bitcast_fusion.2
  0.7 0.9 dynamic-slice_bitcast_fusion
  1.7 0.7 collective-permute-start.1
  2.4 1.0 constant_dynamic-slice_fusion.3
  3.5 0.8 constant_dynamic-slice_fusion
  4.4 0.3 concatenate.14
  4.6 1.6 %collective-permute-start.2 = (f32[44,128]{1,0:T(8,128)S(1)}, f32[44,128]{1,0:T(8,128)S(1)}, u32[]{:S(2)}, u32[]{:S(2)}) collective-permute-start(f32[44,128]{1,0:T(8,128)S(1)} %concatenate.14), channel_id=1, source_target_pairs={{0,1},{2,3},{4,5},{6,7},{1,0},{3,2},{5,4},{7,6},{8,9},{10,11},{12,... | collective-permute-start | bytes 67592 | tf_op jit(solution)/shard_map/ppermute | solution.py:571
  6.5 0.7 collective-permute-start.3
  7.1 0.6 pad_add_fusion.place_ref
  7.7 0.8 collective-permute-done.2.cols_a_ref
  8.5 0.6 copy-done.4
  9.1 20.3 %shard_map.136 = (f32[32,128,128]{2,1,0:T(8,128)}, f32[32,128,512]{2,1,0:T(8,128)}, f32[128,128]{1,0:T(8,128)}) custom-call(s32[2]{0:T(128)} %pad_add_fusion.place_ref, f32[32,128,128]{2,1,0:T(8,128)} %field_ref.1, f32[8,32,128]{2,1,0:T(8,128)} %context_ref.1, f32[160,128]{1,0:T(8,128)} %copy-done.2, f32[160,128]{1,0:T(8,128)} %copy-done.3, ...), custom_call_target="tpu_custom_call" | custom-call | flops 8000000000 | bytes 14000000 | tf_op jit(solution)/shard_map/pallas_call | solution.py:384
  29.5 29.5 %all_to_all.20 = f32[128,1,128]{2,1,0:T(1,128)} all-to-all(f32[128,1,128]{2,1,0:T(1,128)} %bitcast.30), channel_id=1, replica_groups=mesh['rg'=8,'core'=2,'col'=8] {'rg','core','col'}, dimensions={0} | all-to-all | bytes 131072 | tf_op jit(solution)/shard_map/all_to_all | solution.py:616
  59.0 9.1 %shard_map.138 = f32[2048,128]{1,0:T(8,128)} custom-call(f32[32,128,128]{2,1,0:T(8,128)} %get-tuple-element.8.refs_0_, f32[32,128,512]{2,1,0:T(8,128)} %get-tuple-element.9.refs_1_, f32[128,128]{1,0:T(8,128)} %bitcast.28, f32[32,512]{1,0:T(8,128)} %refs_3_.5, f32[512,128]{1,0:T(8,128)} %refs_4_.5, f32[5,128]{1,0:T(8,128)} %refs_1_.3, ...), custom_call_target="tpu_custom_call" | custom-call | flops 14000000000 | bytes 8000000 | tf_op jit(solution)/shard_map/pallas_call | solution.py:478
  68.0 5.1 %all-to-all-start.2 = ((f32[64,32,128]{2,1,0:T(8,128)}), f32[64,32,128]{2,1,0:T(8,128)S(1)}, u32[]{:S(2)}, u32[]{:S(2)}) async-start(f32[64,32,128]{2,1,0:T(8,128)} %bitcast.27), calls=%async_computation.2 | async-start | bytes 2097152 | tf_op jit(solution)/shard_map/all_to_all | solution.py:616
  73.1 12.5 %shard_map.137 = f32[2048,128]{1,0:T(8,128)} custom-call(f32[32,128,128]{2,1,0:T(8,128)} %get-tuple-element.8.refs_0_, f32[32,128,512]{2,1,0:T(8,128)} %get-tuple-element.9.refs_1_, f32[128,128]{1,0:T(8,128)} %bitcast.29, f32[32,512]{1,0:T(8,128)} %refs_3_.5, f32[512,128]{1,0:T(8,128)} %refs_4_.5, f32[5,128]{1,0:T(8,128)} %refs_1_.3, ...), custom_call_target="tpu_custom_call" | custom-call | flops 14000000000 | bytes 8000000 | tf_op jit(solution)/shard_map/pallas_call | solution.py:478
  85.6 6.8 %all-to-all-done.2.refs_0_ = f32[64,32,128]{2,1,0:T(8,128)S(1)} async-done(((f32[64,32,128]{2,1,0:T(8,128)}), f32[64,32,128]{2,1,0:T(8,128)S(1)}, u32[]{:S(2)}, u32[]{:S(2)}) %all-to-all-start.2) | async-done | bytes 1048608 | tf_op jit(solution)/shard_map/all_to_all | solution.py:616
  92.4 4.7 %all-to-all-start.1 = ((f32[64,32,128]{2,1,0:T(8,128)}), f32[64,32,128]{2,1,0:T(8,128)S(1)}, u32[]{:S(2)}, u32[]{:S(2)}) async-start(f32[64,32,128]{2,1,0:T(8,128)} %bitcast.26), calls=%async_computation.1 | async-start | bytes 2097152 | tf_op jit(solution)/shard_map/all_to_all | solution.py:616
  97.1 12.7 %shard_map.139.refs_6_ = f32[64,64,128]{2,1,0:T(8,128)} custom-call(f32[64,32,128]{2,1,0:T(8,128)} %copy-done, f32[5,128]{1,0:T(8,128)} %refs_1_.3, f32[2,128,384]{2,1,0:T(8,128)} %refs_2_.3, f32[2,128,128]{2,1,0:T(8,128)} %refs_3_.7, f32[2,128,512]{2,1,0:T(8,128)} %refs_4_.7, f32[2,512,128]{2,1,0:T(8,128)} %refs_5_.7, f32[2,128,512]{2,1,0:T(8,128)} %refs_4_.7, ...), custom_call_target="tpu_custom_call" | custom-call | flops 14000000000 | bytes 4000000 | tf_op jit(solution)/shard_map/pallas_call | solution.py:550
  109.8 5.8 %all-to-all-done.1.refs_0_ = f32[64,32,128]{2,1,0:T(8,128)S(1)} async-done(((f32[64,32,128]{2,1,0:T(8,128)}), f32[64,32,128]{2,1,0:T(8,128)S(1)}, u32[]{:S(2)}, u32[]{:S(2)}) %all-to-all-start.1) | async-done | bytes 1048608 | tf_op jit(solution)/shard_map/all_to_all | solution.py:616
  115.5 1.0 copy-done.1
  116.5 9.8 %shard_map.140 = f32[64,64,128]{2,1,0:T(8,128)} custom-call(f32[64,32,128]{2,1,0:T(8,128)} %copy-done.1, f32[5,128]{1,0:T(8,128)} %refs_1_.3, f32[2,128,384]{2,1,0:T(8,128)} %refs_2_.3, f32[2,128,128]{2,1,0:T(8,128)} %refs_3_.7, f32[2,128,512]{2,1,0:T(8,128)} %refs_4_.7, f32[2,512,128]{2,1,0:T(8,128)} %refs_5_.7, ...), custom_call_target="tpu_custom_call", output_to_operand_aliasing={{}: (6, {})} | custom-call | flops 14000000000 | bytes 4000000 | tf_op jit(solution)/shard_map/pallas_call | solution.py:550
  126.3 33.7 %all_to_all.21 = f32[64,64,128]{2,1,0:T(8,128)S(1)} all-to-all(f32[64,64,128]{2,1,0:T(8,128)} %shard_map.140), channel_id=1, replica_groups=mesh['rg'=8,'core'=2,'col'=8] {'rg','col'}, dimensions={0} | all-to-all | bytes 4194304 | tf_op jit(solution)/shard_map/all_to_all | solution.py:616
  160.0 1.6 copy.18
  (22 shorter events, 0.4 us)
Async XLA Ops:
  1.6 2.6 %collective-permute-start = (f32[160,128]{1,0:T(8,128)S(1)}, f32[160,128]{1,0:T(8,128)S(1)}, u32[]{:S(2)}, u32[]{:S(2)}) collective-permute-start(f32[160,128]{1,0:T(8,128)S(1)} %pad_maximum_fusion), channel_id=1, source_target_pairs={{0,8},{16,24},{32,40},{48,56},{64,72},{80,88},{96,104},{112,120},{... | collective-permute-start | bytes 245768 | tf_op jit(solution)/shard_map/ppermute | solution.py:571
  1.7 2.6 %collective-permute-start.1 = (f32[160,128]{1,0:T(8,128)S(1)}, f32[160,128]{1,0:T(8,128)S(1)}, u32[]{:S(2)}, u32[]{:S(2)}) collective-permute-start(f32[160,128]{1,0:T(8,128)S(1)} %pad_maximum_fusion.1), channel_id=1, source_target_pairs={{8,16},{24,32},{40,48},{56,64},{72,80},{88,96},{104,112},{16,8},{3... | collective-permute-start | bytes 245768 | tf_op jit(solution)/shard_map/ppermute | solution.py:571
  4.3 4.3 %copy-start.2 = (f32[160,128]{1,0:T(8,128)}, f32[160,128]{1,0:T(8,128)S(1)}, u32[]{:S(2)}) copy-start(f32[160,128]{1,0:T(8,128)S(1)} %collective-permute-done.rows_a_ref) | copy-start | bytes 245764
  4.3 4.2 %copy-start.3 = (f32[160,128]{1,0:T(8,128)}, f32[160,128]{1,0:T(8,128)S(1)}, u32[]{:S(2)}) copy-start(f32[160,128]{1,0:T(8,128)S(1)} %collective-permute-done.1.rows_b_ref) | copy-start | bytes 245764
  4.6 3.9 %collective-permute-start.2 = (f32[44,128]{1,0:T(8,128)S(1)}, f32[44,128]{1,0:T(8,128)S(1)}, u32[]{:S(2)}, u32[]{:S(2)}) collective-permute-start(f32[44,128]{1,0:T(8,128)S(1)} %concatenate.14), channel_id=1, source_target_pairs={{0,1},{2,3},{4,5},{6,7},{1,0},{3,2},{5,4},{7,6},{8,9},{10,11},{12,... | collective-permute-start | bytes 67592 | tf_op jit(solution)/shard_map/ppermute | solution.py:571
  6.5 2.1 %collective-permute-start.3 = (f32[44,128]{1,0:T(8,128)S(1)}, f32[44,128]{1,0:T(8,128)S(1)}, u32[]{:S(2)}, u32[]{:S(2)}) collective-permute-start(f32[44,128]{1,0:T(8,128)S(1)} %concatenate.15), channel_id=1, source_target_pairs={{1,2},{3,4},{5,6},{2,1},{4,3},{6,5},{9,10},{11,12},{13,14},{10,9},... | collective-permute-start | bytes 67592 | tf_op jit(solution)/shard_map/ppermute | solution.py:571
  8.5 0.6 copy-start.4
  8.5 0.6 copy-start.5
  68.0 24.4 %all-to-all-start.2 = ((f32[64,32,128]{2,1,0:T(8,128)}), f32[64,32,128]{2,1,0:T(8,128)S(1)}, u32[]{:S(2)}, u32[]{:S(2)}) async-start(f32[64,32,128]{2,1,0:T(8,128)} %bitcast.27), calls=%async_computation.2 | async-start | bytes 2097152 | tf_op jit(solution)/shard_map/all_to_all | solution.py:616
  92.4 4.7 %copy-start = (f32[64,32,128]{2,1,0:T(8,128)}, f32[64,32,128]{2,1,0:T(8,128)S(1)}, u32[]{:S(2)}) copy-start(f32[64,32,128]{2,1,0:T(8,128)S(1)} %all-to-all-done.2.refs_0_) | copy-start | bytes 3145732
  92.4 23.1 %all-to-all-start.1 = ((f32[64,32,128]{2,1,0:T(8,128)}), f32[64,32,128]{2,1,0:T(8,128)S(1)}, u32[]{:S(2)}, u32[]{:S(2)}) async-start(f32[64,32,128]{2,1,0:T(8,128)} %bitcast.26), calls=%async_computation.1 | async-start | bytes 2097152 | tf_op jit(solution)/shard_map/all_to_all | solution.py:616
  115.5 1.0 copy-start.1

commit v6 on v5

--- a/solution.py
+++ b/solution.py
@@ -217,15 +217,13 @@
     return rows_of(highs), rows_of(lows)
 
 
-PHASES = ((0.375, 0.625, 0.0), (0.125, 0.875, 0.0), (0.0, 0.875, 0.125), (0.0, 0.625, 0.375))
-
-
-def lifting():
-    fine = np.zeros((WIDE + 8, COARSE_WIDE), np.float32)
+def column_weights():
+    fine = np.zeros((WIDE, COARSE_WIDE), np.float32)
+    table = ((0.375, 0.625, 0.0), (0.125, 0.875, 0.0), (0.0, 0.875, 0.125), (0.0, 0.625, 0.375))
 
     def fill(at, column):
         k, o = column // 4, column % 4
-        for step, weight in zip((-1, 0, 1), PHASES[o]):
+        for step, weight in zip((-1, 0, 1), table[o]):
             if weight:
                 fine[at, (k + step) % 40] = weight
 
@@ -233,9 +231,10 @@
         fill(8 * (column % 16) + column // 16, column)
     fill(128, -1)
     fill(135, 128)
-    both = np.concatenate([fine, fine], axis=1)
-    pairs = (weights[:2] if weights[0] else weights[1:] for weights in PHASES)
-    return np.stack([np.concatenate([a * both, b * both], axis=1) for a, b in pairs])
+    return np.concatenate([fine, fine], axis=1)
+
+
+ROW_WEIGHTS = ((0.375, 0.625, -1), (0.125, 0.875, -1), (0.875, 0.125, 0), (0.625, 0.375, 0))
 
 
 def lift_kernel(
@@ -283,7 +282,7 @@
         projected = dot(three(ctx[...].reshape(10 * COARSE_WIDE, CHANNELS)), weight)
         for k in range(10):
             high, low = split(projected[COARSE_WIDE * k : COARSE_WIDE * (k + 1)])
-            coarse[2 * COARSE_WIDE * k : 2 * COARSE_WIDE * (k + 1)] = rows_of([high, low])
+            coarse[k] = dot(up_ref[...], rows_of([high, low]))
 
     has_after = jnp.where(place_ref[1] < 7, 1.0, 0.0)
     has_before = jnp.where(place_ref[1] > 0, 1.0, 0.0)
@@ -295,10 +294,9 @@
             two = []
             for j in (i, i + 1):
                 k, o = (fine_first + j) // 4, (fine_first + j) % 4
-                at = k_first + k - (1 if PHASES[o][0] else 0)
-                at = pl.multiple_of(at * (2 * COARSE_WIDE), 2 * COARSE_WIDE)
-                two_rows = coarse[pl.ds(at, 4 * COARSE_WIDE)]
-                x = lift[first + j] + dot(up_ref[o], two_rows)[:WIDE]
+                lower, upper, shift = ROW_WEIGHTS[o]
+                at = k_first + k + shift
+                x = lift[first + j] + (lower * coarse[at] + upper * coarse[at + 1])
                 lift[first + j] = x
                 two.append(x)
             parts.append(three(normed(rows_of(two))))
@@ -348,7 +346,7 @@
             for t in range(16):
                 following = column(t + 1) if t < 14 else last
                 out = bend(here[1] + before + (following[2] if t < 15 else end))
-                active_ref[r, 8 * t : 8 * t + 8, lanes] = out
+                active_ref[r, part, 8 * t : 8 * t + 8] = out
                 summed = summed + out
                 before, here = here[0], following
             return summed
@@ -379,7 +377,7 @@
 
 
 def lift_stage(place, args, copies):
-    up = jnp.asarray(lifting(), BF16)
+    up = jnp.asarray(column_weights(), BF16)
     args = args[:6] + (up,) + args[6:]
     return pl.pallas_call(
         lift_kernel,
@@ -387,18 +385,18 @@
         in_specs=[pl.BlockSpec(memory_space=pltpu.SMEM)] + [whole(a.shape) for a in args],
         out_specs=[
             pl.BlockSpec((8, 128, CHANNELS), lambda s: (s, 0, 0)),
-            pl.BlockSpec((8, 128, EXPANDED), lambda s: (s, 0, 0)),
+            pl.BlockSpec((8, EXPANDED // 128, 128, 128), lambda s: (s, 0, 0, 0)),
             whole((copies, 128)),
         ],
         out_shape=[
             jax.ShapeDtypeStruct((32, 128, CHANNELS), F32),
-            jax.ShapeDtypeStruct((32, 128, EXPANDED), F32),
+            jax.ShapeDtypeStruct((32, EXPANDED // 128, 128, 128), F32),
             jax.ShapeDtypeStruct((copies, 128), F32),
         ],
         scratch_shapes=[
             pltpu.VMEM((34, WIDE, CHANNELS), F32),
             pltpu.VMEM((10, COARSE_WIDE, CHANNELS), F32),
-            pltpu.VMEM((20 * COARSE_WIDE, CHANNELS), BF16),
+            pltpu.VMEM((10, WIDE, CHANNELS), F32),
             pltpu.VMEM((34, WIDE, EXPANDED), F32),
             pltpu.VMEM((3 * CHANNELS, EXPANDED), BF16),
             pltpu.VMEM((8, EXPANDED), F32),
@@ -412,7 +410,7 @@
 
 def block_kernel(
     cells_total, fed, lifted_ref, active_ref, sums_ref, sexp_ref, project_ref, gains_ref, qkv_ref,
-    aout_ref, min_ref, mout_ref, out_ref, project, sums, k3, qv3, out3, *feed_weights,
+    aout_ref, min_ref, mout_ref, out_ref, project, k3, qv3, out3, *feed_weights,
 ):
     @pl.when(pl.program_id(0) == 0)
     def _():
@@ -426,21 +424,30 @@
         if fed:
             prepare_feed(min_ref, mout_ref, gains_ref[2:3], *feed_weights)
 
-    for half in range(0, 8, PART // 128):
-        rows = slice(half, half + PART // 128)
-        halves = [split(active_ref[r]) for r in range(half, half + PART // 128)]
+    def window(w, load):
+        at = pl.ds(64 * (w % 2) + w // 2, WINDOW, stride=8)
+        return rows_of([load(r, at) for r in range(WINDOW)])
+
+    def expanded(r, at):
+        return lanes_of([active_ref[r, k, at, :] for k in range(EXPANDED // 128)])
+
+    def projected(start):
+        halves = [split(window(w, expanded)) for w in range(start, start + PART // CELLS)]
+        yield
         wide = dot(rows_of([h[0] for h in halves]), project[...])
         rest = dot(rows_of([h[1] for h in halves]), project[:, :CHANNELS])
-        added = wide[:, :CHANNELS] + (wide[:, CHANNELS:] + rest)
-        sums[rows] = lifted_ref[rows] + added.reshape(PART // 128, 128, CHANNELS)
-
-    def window(w):
-        at = pl.ds(64 * (w % 2) + w // 2, WINDOW, stride=8)
-        return rows_of([sums[r, at, :] for r in range(WINDOW)])
+        yield
+        pairs = []
+        for p in range(PART // PAIR):
+            at = slice(p * PAIR, (p + 1) * PAIR)
+            x = rows_of(
+                [window(start + 2 * p + i, lambda r, at: lifted_ref[r, at, :]) for i in range(2)]
+            )
+            pairs.append(x + (wide[at, :CHANNELS] + (wide[at, CHANNELS:] + rest[at])))
+        return pairs
 
     def group(part):
-        start = part * PART // CELLS
-        pairs = [rows_of([window(w), window(w + 1)]) for w in range(start, start + 8, 2)]
+        pairs = yield from projected(part * PART // CELLS)
         pairs = yield from attend(pairs, k3, qv3, out3)
         if fed:
             pairs = yield from feed(pairs, *feed_weights)
@@ -462,15 +469,15 @@
 
 
 def block_stage(chunk, fed, lifted, active, sums, se_expand, project, gains, weights, cells_total):
-    per_row = 128 // (BLOCK_STEP // 8)
-    steps = 4 // CHUNKS * per_row
+    steps = 4 // CHUNKS
     row_base = chunk * (4 // CHUNKS)
     rest = (sums, se_expand, project, gains)
 
-    def strip(channels):
-        return pl.BlockSpec(
-            (8, BLOCK_STEP // 8, channels), lambda s: (row_base + s // per_row, s % per_row, 0)
-        )
+    columns = BLOCK_STEP // 8
+    strips = [
+        pl.BlockSpec((8, columns, CHANNELS), lambda s: (row_base + s, 0, 0)),
+        pl.BlockSpec((8, EXPANDED // 128, columns, 128), lambda s: (row_base + s, 0, 0, 0)),
+    ]
 
     def body(*refs):
         block_kernel(cells_total, fed, *refs)
@@ -478,14 +485,13 @@
     return pl.pallas_call(
         body,
         grid=(steps,),
-        in_specs=[strip(CHANNELS), strip(EXPANDED)]
+        in_specs=strips
         + [whole(a.shape) for a in rest]
         + [of_layer(w, 0) for w in weights],
         out_specs=pl.BlockSpec((BLOCK_STEP, CHANNELS), lambda s: (s, 0)),
         out_shape=jax.ShapeDtypeStruct((steps * BLOCK_STEP, CHANNELS), F32),
         scratch_shapes=[
             pltpu.VMEM((EXPANDED, 2 * CHANNELS), BF16),
-            pltpu.VMEM((8, 128, CHANNELS), F32),
         ]
         + ATTENTION_SCRATCH
         + (FEED_SCRATCH if fed else []),
@@ -609,17 +615,18 @@
             field, context, rows_a, rows_b, cols_a, cols_b, ctx_weight, norm_gains, expand_weight,
             depth_weight, se_reduce.T,
         ),
-        rows * cols,
+        8,
     )
 
     def exchange(x, axes):
         return lax.all_to_all(x, axes, split_axis=0, concat_axis=0, tiled=True)
 
-    sums = exchange(partial[:, None, :], ("rg", "core", "col"))[:, 0, :]
+    group = ("rg", "col")
+    chip = partial[:1] + lax.ppermute(partial[:1], "core", [(0, 1), (1, 0)])
+    sums = exchange(jnp.broadcast_to(chip, (GROUP, 1, 128)), group)[:, 0, :]
 
     weights = (attn_qkv, attn_out, mlp_in, mlp_out)
     cells_total = rows * cols * field.shape[0] * field.shape[1]
-    group = ("rg", "col")
     sent = []
     for chunk in range(CHUNKS):
         mine = block_stage(

time: 162 us -> 160 us (0.988)
  Pallas kernels: 64.3 us -> 61.4 us
  starting transfers between devices: 12.8 us -> 15.2 us
  blocking collectives: 63.2 us -> 61.2 us
    ppermute x0 -> x1, starting transfers between devices: none -> 2.6 us  [per_device(): chip = partial[:1] + lax.ppermute(partial[:1], 'core', [(0, 1), (1, 0)])]
    all_to_all x2, blocking collectives: 63.2 us -> 61.2 us  [exchange(): return lax.all_to_all(x, axes, split_axis=0, concat_axis=0, tiled=True)]
    pallas_call x1, Pallas kernels: 20.3 us -> 18.5 us  [lift_stage(): pl.pallas_call(lift_kernel, grid=(4,), in_specs=[pl.BlockSpec(memory_spac...]
    all_to_all x2, waiting for transfers between devices: 12.6 us -> 10.9 us  [exchange(): return lax.all_to_all(x, axes, split_axis=0, concat_axis=0, tiled=True)]
  transfers between devices with their start and end apart: 6 -> 7, of which waited for: 3 -> 4; matrix products, arithmetic and copies ran while one was open for 2% -> 2% of each run, Pallas kernels for 16% -> 15%
where the time goes in v6:
time: 160 us
  Pallas kernels  61.4 us (38%)
  blocking collectives  61.2 us (38%)
  starting transfers between devices  15.2 us (10%)
  waiting for transfers between devices  12.5 us (8%)
  local copies, waits for them, and re-layouts  7.77 us (5%)
    all_to_all x2, blocking collectives, exchange(): return lax.all_to_all(x, axes, split_axis=0, concat_axis=0, tiled=True)  61.2 us
    pallas_call x2, Pallas kernels, grid_stage(): pl.pallas_call(body, grid=(steps,), in_specs=in_specs, out_specs=pl.Block...  22.5 us
    pallas_call x2, Pallas kernels, block_stage(): pl.pallas_call(body, grid=(steps,), in_specs=strips + [whole(a.shape) for...  20.4 us
    pallas_call x1, Pallas kernels, lift_stage(): pl.pallas_call(lift_kernel, grid=(4,), in_specs=[pl.BlockSpec(memory_spac...  18.5 us
    all_to_all x2, waiting for transfers between devices, exchange(): return lax.all_to_all(x, axes, split_axis=0, concat_axis=0, tiled=True)  10.9 us
    all_to_all x2, starting transfers between devices, exchange(): return lax.all_to_all(x, axes, split_axis=0, concat_axis=0, tiled=True)  9.54 us
  transfers between devices with their start and end apart: 7, of which 4 were waited for; matrix products, arithmetic and copies ran while one was open for 2% of the time, Pallas kernels for 15%

profile of v6, /device:TPU:0, one launch (start us, length us, event | category | flops | bytes accessed | tf_op | source)
XLA Modules:
  0.0 159.6 jit_solution(554311464246905387)
XLA Ops:
  0.0 0.7 dynamic-slice_bitcast_fusion.2
  0.7 0.9 dynamic-slice_bitcast_fusion
  1.7 0.7 collective-permute-start.1
  2.4 1.0 constant_dynamic-slice_fusion.3
  3.5 0.8 constant_dynamic-slice_fusion
  4.6 1.6 %collective-permute-start.2 = (f32[44,128]{1,0:T(8,128)S(1)}, f32[44,128]{1,0:T(8,128)S(1)}, u32[]{:S(2)}, u32[]{:S(2)}) collective-permute-start(f32[44,128]{1,0:T(8,128)S(1)} %concatenate.14), channel_id=1, source_target_pairs={{0,1},{2,3},{4,5},{6,7},{1,0},{3,2},{5,4},{7,6},{8,9},{10,11},{12,... | collective-permute-start | bytes 67592 | tf_op jit(solution)/shard_map/ppermute | solution.py:577
  7.7 0.8 collective-permute-done.2.cols_a_ref
  9.2 18.5 %shard_map.136 = (f32[32,128,128]{2,1,0:T(8,128)}, f32[32,4,128,128]{3,2,1,0:T(8,128)}, f32[8,128]{1,0:T(8,128)}) custom-call(s32[2]{0:T(128)} %pad_add_fusion.place_ref, f32[32,128,128]{2,1,0:T(8,128)} %field_ref.1, f32[8,32,128]{2,1,0:T(8,128)} %context_ref.1, f32[160,128]{1,0:T(8,128)} %copy-done.2, f32[160,128]{1,0:T(8,128)} %copy-done.3, ...), custom_call_target="tpu_custom_call" | custom-call | flops 8000000000 | bytes 14000000 | tf_op jit(solution)/shard_map/pallas_call | solution.py:382
  27.7 0.7 slice.24
  28.3 2.6 %collective-permute-start.4 = (f32[1,128]{1,0:T(1,128)S(1)}, f32[1,128]{1,0:T(1,128)S(1)}, u32[]{:S(2)}, u32[]{:S(2)}) collective-permute-start(f32[1,128]{1,0:T(1,128)S(1)} %slice.24), channel_id=1, source_target_pairs={{0,8},{8,0},{1,9},{9,1},{2,10},{10,2},{3,11},{11,3},{4,12},{12,4},... | collective-permute-start | bytes 1544 | tf_op jit(solution)/shard_map/ppermute | solution.py:625
  30.9 0.8 collective-permute-done.4
  31.8 0.7 add_bitcast_fusion
  32.4 27.5 %all_to_all.20 = f32[64,1,128]{2,1,0:T(1,128)} all-to-all(f32[64,1,128]{2,1,0:T(1,128)S(1)} %broadcast_in_dim.3), channel_id=1, replica_groups=mesh['rg'=8,'core'=2,'col'=8] {'rg','col'}, dimensions={0} | all-to-all | bytes 65536 | tf_op jit(solution)/shard_map/all_to_all | solution.py:622
  59.9 8.6 %shard_map.138 = f32[2048,128]{1,0:T(8,128)} custom-call(f32[32,128,128]{2,1,0:T(8,128)} %get-tuple-element.8.refs_0_, f32[32,4,128,128]{3,2,1,0:T(8,128)} %get-tuple-element.9.refs_1_, f32[64,128]{1,0:T(8,128)} %bitcast.29, f32[32,512]{1,0:T(8,128)} %refs_3_.5, f32[512,128]{1,0:T(8,128)} %refs_4_.5, f32[5,128]{1,0:T(8,128)} %refs_1_.3, ...), custom_call_target="tpu_custom_call" | custom-call | flops 14000000000 | bytes 8000000 | tf_op jit(solution)/shard_map/pallas_call | solution.py:485
  68.5 4.9 %all-to-all-start.2 = ((f32[64,32,128]{2,1,0:T(8,128)}), f32[64,32,128]{2,1,0:T(8,128)S(1)}, u32[]{:S(2)}, u32[]{:S(2)}) async-start(f32[64,32,128]{2,1,0:T(8,128)} %bitcast.26), calls=%async_computation.2 | async-start | bytes 2097152 | tf_op jit(solution)/shard_map/all_to_all | solution.py:622
  73.4 11.8 %shard_map.137 = f32[2048,128]{1,0:T(8,128)} custom-call(f32[32,128,128]{2,1,0:T(8,128)} %get-tuple-element.8.refs_0_, f32[32,4,128,128]{3,2,1,0:T(8,128)} %get-tuple-element.9.refs_1_, f32[64,128]{1,0:T(8,128)} %bitcast.30, f32[32,512]{1,0:T(8,128)} %refs_3_.5, f32[512,128]{1,0:T(8,128)} %refs_4_.5, f32[5,128]{1,0:T(8,128)} %refs_1_.3, ...), custom_call_target="tpu_custom_call" | custom-call | flops 14000000000 | bytes 8000000 | tf_op jit(solution)/shard_map/pallas_call | solution.py:485
  85.3 6.2 %all-to-all-done.2.refs_0_ = f32[64,32,128]{2,1,0:T(8,128)S(1)} async-done(((f32[64,32,128]{2,1,0:T(8,128)}), f32[64,32,128]{2,1,0:T(8,128)S(1)}, u32[]{:S(2)}, u32[]{:S(2)}) %all-to-all-start.2) | async-done | bytes 1048608 | tf_op jit(solution)/shard_map/all_to_all | solution.py:622
  91.4 4.7 %all-to-all-start.1 = ((f32[64,32,128]{2,1,0:T(8,128)}), f32[64,32,128]{2,1,0:T(8,128)S(1)}, u32[]{:S(2)}, u32[]{:S(2)}) async-start(f32[64,32,128]{2,1,0:T(8,128)} %bitcast.25), calls=%async_computation.1 | async-start | bytes 2097152 | tf_op jit(solution)/shard_map/all_to_all | solution.py:622
  96.1 12.7 %shard_map.139.refs_6_ = f32[64,64,128]{2,1,0:T(8,128)} custom-call(f32[64,32,128]{2,1,0:T(8,128)} %copy-done, f32[5,128]{1,0:T(8,128)} %refs_1_.3, f32[2,128,384]{2,1,0:T(8,128)} %refs_2_.3, f32[2,128,128]{2,1,0:T(8,128)} %refs_3_.7, f32[2,128,512]{2,1,0:T(8,128)} %refs_4_.7, f32[2,512,128]{2,1,0:T(8,128)} %refs_5_.7, f32[2,128,512]{2,1,0:T(8,128)} %refs_4_.7, ...), custom_call_target="tpu_custom_call" | custom-call | flops 14000000000 | bytes 4000000 | tf_op jit(solution)/shard_map/pallas_call | solution.py:556
  108.8 4.7 %all-to-all-done.1.refs_0_ = f32[64,32,128]{2,1,0:T(8,128)S(1)} async-done(((f32[64,32,128]{2,1,0:T(8,128)}), f32[64,32,128]{2,1,0:T(8,128)S(1)}, u32[]{:S(2)}, u32[]{:S(2)}) %all-to-all-start.1) | async-done | bytes 1048608 | tf_op jit(solution)/shard_map/all_to_all | solution.py:622
  113.5 1.0 copy-done.1
  114.5 9.8 %shard_map.140 = f32[64,64,128]{2,1,0:T(8,128)} custom-call(f32[64,32,128]{2,1,0:T(8,128)} %copy-done.1, f32[5,128]{1,0:T(8,128)} %refs_1_.3, f32[2,128,384]{2,1,0:T(8,128)} %refs_2_.3, f32[2,128,128]{2,1,0:T(8,128)} %refs_3_.7, f32[2,128,512]{2,1,0:T(8,128)} %refs_4_.7, f32[2,512,128]{2,1,0:T(8,128)} %refs_5_.7, ...), custom_call_target="tpu_custom_call", output_to_operand_aliasing={{}: (6, {})} | custom-call | flops 14000000000 | bytes 4000000 | tf_op jit(solution)/shard_map/pallas_call | solution.py:556
  124.3 33.7 %all_to_all.21 = f32[64,64,128]{2,1,0:T(8,128)S(1)} all-to-all(f32[64,64,128]{2,1,0:T(8,128)} %shard_map.140), channel_id=1, replica_groups=mesh['rg'=8,'core'=2,'col'=8] {'rg','col'}, dimensions={0} | all-to-all | bytes 4194304 | tf_op jit(solution)/shard_map/all_to_all | solution.py:622
  158.0 1.6 copy.17
  (27 shorter events, 2.5 us)
Async XLA Ops:
  1.6 2.6 %collective-permute-start = (f32[160,128]{1,0:T(8,128)S(1)}, f32[160,128]{1,0:T(8,128)S(1)}, u32[]{:S(2)}, u32[]{:S(2)}) collective-permute-start(f32[160,128]{1,0:T(8,128)S(1)} %pad_maximum_fusion), channel_id=1, source_target_pairs={{0,8},{16,24},{32,40},{48,56},{64,72},{80,88},{96,104},{112,120},{... | collective-permute-start | bytes 245768 | tf_op jit(solution)/shard_map/ppermute | solution.py:577
  1.7 2.6 %collective-permute-start.1 = (f32[160,128]{1,0:T(8,128)S(1)}, f32[160,128]{1,0:T(8,128)S(1)}, u32[]{:S(2)}, u32[]{:S(2)}) collective-permute-start(f32[160,128]{1,0:T(8,128)S(1)} %pad_maximum_fusion.1), channel_id=1, source_target_pairs={{8,16},{24,32},{40,48},{56,64},{72,80},{88,96},{104,112},{16,8},{3... | collective-permute-start | bytes 245768 | tf_op jit(solution)/shard_map/ppermute | solution.py:577
  4.3 4.3 %copy-start.2 = (f32[160,128]{1,0:T(8,128)}, f32[160,128]{1,0:T(8,128)S(1)}, u32[]{:S(2)}) copy-start(f32[160,128]{1,0:T(8,128)S(1)} %collective-permute-done.rows_a_ref) | copy-start | bytes 245764
  4.3 4.2 %copy-start.3 = (f32[160,128]{1,0:T(8,128)}, f32[160,128]{1,0:T(8,128)S(1)}, u32[]{:S(2)}) copy-start(f32[160,128]{1,0:T(8,128)S(1)} %collective-permute-done.1.rows_b_ref) | copy-start | bytes 245764
  4.6 3.9 %collective-permute-start.2 = (f32[44,128]{1,0:T(8,128)S(1)}, f32[44,128]{1,0:T(8,128)S(1)}, u32[]{:S(2)}, u32[]{:S(2)}) collective-permute-start(f32[44,128]{1,0:T(8,128)S(1)} %concatenate.14), channel_id=1, source_target_pairs={{0,1},{2,3},{4,5},{6,7},{1,0},{3,2},{5,4},{7,6},{8,9},{10,11},{12,... | collective-permute-start | bytes 67592 | tf_op jit(solution)/shard_map/ppermute | solution.py:577
  6.5 2.1 %collective-permute-start.3 = (f32[44,128]{1,0:T(8,128)S(1)}, f32[44,128]{1,0:T(8,128)S(1)}, u32[]{:S(2)}, u32[]{:S(2)}) collective-permute-start(f32[44,128]{1,0:T(8,128)S(1)} %concatenate.15), channel_id=1, source_target_pairs={{1,2},{3,4},{5,6},{2,1},{4,3},{6,5},{9,10},{11,12},{13,14},{10,9},... | collective-permute-start | bytes 67592 | tf_op jit(solution)/shard_map/ppermute | solution.py:577
  8.5 0.6 copy-start.4
  8.5 0.6 copy-start.5
  28.3 3.4 %collective-permute-start.4 = (f32[1,128]{1,0:T(1,128)S(1)}, f32[1,128]{1,0:T(1,128)S(1)}, u32[]{:S(2)}, u32[]{:S(2)}) collective-permute-start(f32[1,128]{1,0:T(1,128)S(1)} %slice.24), channel_id=1, source_target_pairs={{0,8},{8,0},{1,9},{9,1},{2,10},{10,2},{3,11},{11,3},{4,12},{12,4},... | collective-permute-start | bytes 1544 | tf_op jit(solution)/shard_map/ppermute | solution.py:625
  68.5 22.9 %all-to-all-start.2 = ((f32[64,32,128]{2,1,0:T(8,128)}), f32[64,32,128]{2,1,0:T(8,128)S(1)}, u32[]{:S(2)}, u32[]{:S(2)}) async-start(f32[64,32,128]{2,1,0:T(8,128)} %bitcast.26), calls=%async_computation.2 | async-start | bytes 2097152 | tf_op jit(solution)/shard_map/all_to_all | solution.py:622
  91.4 4.7 %copy-start = (f32[64,32,128]{2,1,0:T(8,128)}, f32[64,32,128]{2,1,0:T(8,128)S(1)}, u32[]{:S(2)}) copy-start(f32[64,32,128]{2,1,0:T(8,128)S(1)} %all-to-all-done.2.refs_0_) | copy-start | bytes 3145732
  91.4 22.1 %all-to-all-start.1 = ((f32[64,32,128]{2,1,0:T(8,128)}), f32[64,32,128]{2,1,0:T(8,128)S(1)}, u32[]{:S(2)}, u32[]{:S(2)}) async-start(f32[64,32,128]{2,1,0:T(8,128)} %bitcast.25), calls=%async_computation.1 | async-start | bytes 2097152 | tf_op jit(solution)/shard_map/all_to_all | solution.py:622
  113.5 1.0 copy-start.1

commit v7 on v6

--- a/solution.py
+++ b/solution.py
@@ -240,24 +240,29 @@
 def lift_kernel(
     place_ref, field_ref, context_ref, rows_a_ref, rows_b_ref, cols_a_ref, cols_b_ref, up_ref,
     ctxw_ref, gains_ref, expand_ref, depth_ref, reduce_ref, lifted_ref, active_ref, sum_ref,
-    lift, ctx, coarse, hid, expand3, total,
+    field, ends, sides, lift, ctx, coarse, hid, expand3, total, sems,
 ):
     step = pl.program_id(0)
+
+    def arrival(k):
+        at = pl.ds(0, 9) if k == 0 else pl.ds(8 * k + 1, 8 if k < 3 else 7)
+        return pltpu.make_async_copy(field_ref.at[at], field.at[at], sems.at[k])
+
     sublane = lax.broadcasted_iota(jnp.int32, (8, 128), 0)
     first_row, last_row = sublane == 0, sublane == 7
 
     @pl.when(step == 0)
     def _():
+        for k in range(4):
+            arrival(k).start()
         expand3[...] = stack_rows(gained(GELU_IN * expand_ref[...], gains_ref[0:1]))
         total[...] = jnp.zeros_like(total)
-        for t in range(16):
-            lift[1:33, 8 * t : 8 * t + 8] = field_ref[:, pl.ds(t, 8, stride=16), :]
         ctx[1:9, :32] = context_ref[...]
 
         def take_rows(above_ref, below_ref):
             for t in range(16):
-                lift[0, 8 * t : 8 * t + 8] = above_ref[pl.ds(t, 8, stride=16), :]
-                lift[33, 8 * t : 8 * t + 8] = below_ref[pl.ds(t, 8, stride=16), :]
+                ends[0, 8 * t : 8 * t + 8] = above_ref[pl.ds(t, 8, stride=16), :]
+                ends[1, 8 * t : 8 * t + 8] = below_ref[pl.ds(t, 8, stride=16), :]
             ctx[0, :32] = above_ref[128:]
             ctx[9, :32] = below_ref[128:]
 
@@ -267,7 +272,7 @@
                 after = jnp.broadcast_to(after_ref[e : e + 1], (8, 128))
                 before = jnp.broadcast_to(before_ref[e : e + 1], (8, 128))
                 if e < 34:
-                    lift[e, 128:] = jnp.where(first_row, before, jnp.where(last_row, after, zero))
+                    sides[e] = jnp.where(first_row, before, jnp.where(last_row, after, zero))
                 else:
                     ctx[e - 34, 32:40] = jnp.where(
                         first_row, after, jnp.where(last_row, before, zero)
@@ -288,6 +293,9 @@
     has_before = jnp.where(place_ref[1] > 0, 1.0, 0.0)
     inside = jnp.where(first_row, has_before, has_after)
 
+    for k in range(4):
+        pl.when(step == k)(lambda k=k: arrival(k).wait())
+
     def hidden_rows(first, fine_first, k_first, count):
         parts = []
         for i in range(0, count, 2):
@@ -296,8 +304,16 @@
                 k, o = (fine_first + j) // 4, (fine_first + j) % 4
                 lower, upper, shift = ROW_WEIGHTS[o]
                 at = k_first + k + shift
-                x = lift[first + j] + (lower * coarse[at] + upper * coarse[at + 1])
-                lift[first + j] = x
+                up = lower * coarse[at] + upper * coarse[at + 1]
+                if fine_first + j < 0:
+                    own = ends[0]
+                else:
+                    f = jnp.minimum(first + j - 1, 31)
+                    own = rows_of([field[f, pl.ds(t, 8, stride=16), :] for t in range(16)])
+                    if fine_first + j == 8:
+                        own = jnp.where(step == 3, ends[1], own)
+                x = rows_of([own, sides[first + j]]) + up
+                lift[first + j] = x[:128]
                 two.append(x)
             parts.append(three(normed(rows_of(two))))
         made = dot(rows_of(parts), expand3[...])
@@ -322,7 +338,7 @@
     def _():
         hid[33] = jnp.zeros((WIDE, EXPANDED), F32)
 
-    lifted_ref[...] = lift[pl.ds(8 * step + 1, 8), :128]
+    lifted_ref[...] = lift[pl.ds(8 * step + 1, 8)]
 
     for part in range(EXPANDED // 128):
         lanes = slice(part * 128, (part + 1) * 128)
@@ -382,7 +398,8 @@
     return pl.pallas_call(
         lift_kernel,
         grid=(4,),
-        in_specs=[pl.BlockSpec(memory_space=pltpu.SMEM)] + [whole(a.shape) for a in args],
+        in_specs=[pl.BlockSpec(memory_space=pltpu.SMEM), pl.BlockSpec(memory_space=pl.ANY)]
+        + [whole(a.shape) for a in args[1:]],
         out_specs=[
             pl.BlockSpec((8, 128, CHANNELS), lambda s: (s, 0, 0)),
             pl.BlockSpec((8, EXPANDED // 128, 128, 128), lambda s: (s, 0, 0, 0)),
@@ -394,12 +411,16 @@
             jax.ShapeDtypeStruct((copies, 128), F32),
         ],
         scratch_shapes=[
-            pltpu.VMEM((34, WIDE, CHANNELS), F32),
+            pltpu.VMEM((32, 128, CHANNELS), F32),
+            pltpu.VMEM((2, 128, CHANNELS), F32),
+            pltpu.VMEM((34, 8, CHANNELS), F32),
+            pltpu.VMEM((34, 128, CHANNELS), F32),
             pltpu.VMEM((10, COARSE_WIDE, CHANNELS), F32),
             pltpu.VMEM((10, WIDE, CHANNELS), F32),
             pltpu.VMEM((34, WIDE, EXPANDED), F32),
             pltpu.VMEM((3 * CHANNELS, EXPANDED), BF16),
             pltpu.VMEM((8, EXPANDED), F32),
+            pltpu.SemaphoreType.DMA((4,)),
         ],
         compiler_params=pltpu.CompilerParams(vmem_limit_bytes=VMEM_LIMIT),
         cost_estimate=pl.CostEstimate(
@@ -571,11 +592,11 @@
 def by_pairs(edge, at, axis, count):
     even = at % 2 == 0
     swaps = []
-    for first, last in ((0, even), (1, jnp.logical_not(even))):
+    for first, last in ((1, jnp.logical_not(even)), (0, even)):
         lower = [(i, i + 1) for i in range(first, count - 1, 2)]
         pairs = lower + [(b, a) for a, b in lower]
         swaps.append(lax.ppermute(edge(last), axis, pairs))
-    return swaps
+    return swaps[::-1]
 
 
 def per_device(
@@ -615,15 +636,14 @@
             field, context, rows_a, rows_b, cols_a, cols_b, ctx_weight, norm_gains, expand_weight,
             depth_weight, se_reduce.T,
         ),
-        8,
+        rows * cols,
     )
 
     def exchange(x, axes):
         return lax.all_to_all(x, axes, split_axis=0, concat_axis=0, tiled=True)
 
     group = ("rg", "col")
-    chip = partial[:1] + lax.ppermute(partial[:1], "core", [(0, 1), (1, 0)])
-    sums = exchange(jnp.broadcast_to(chip, (GROUP, 1, 128)), group)[:, 0, :]
+    sums = exchange(partial[:, None, :], ("rg", "core", "col"))[:, 0, :]
 
     weights = (attn_qkv, attn_out, mlp_in, mlp_out)
     cells_total = rows * cols * field.shape[0] * field.shape[1]

time: 160 us -> 159 us (level)
  starting transfers between devices: 15.2 us -> 12.8 us
  blocking collectives: 61.2 us -> 63.2 us
    ppermute x1 -> x0, starting transfers between devices: 2.6 us -> none  [per_device(): chip = partial[:1] + lax.ppermute(partial[:1], 'core', [(0, 1), (1, 0)])]
    all_to_all x2, waiting for transfers between devices: 10.9 us -> 13.3 us  [exchange(): return lax.all_to_all(x, axes, split_axis=0, concat_axis=0, tiled=True)]
    all_to_all x2, blocking collectives: 61.2 us -> 63.2 us  [exchange(): return lax.all_to_all(x, axes, split_axis=0, concat_axis=0, tiled=True)]
  transfers between devices with their start and end apart: 7 -> 6, of which waited for: 4 -> 3; matrix products, arithmetic and copies ran while one was open for 2% -> 2% of each run, Pallas kernels for 15% -> 15%
where the time goes in v7:
time: 159 us; the launch traced here: 158 us
  blocking collectives  63.2 us (40%)
  Pallas kernels  60.3 us (38%)
  waiting for transfers between devices  14.1 us (9%)
  starting transfers between devices  12.8 us (8%)
  local copies, waits for them, and re-layouts  7.05 us (4%)
    all_to_all x2, blocking collectives, exchange(): return lax.all_to_all(x, axes, split_axis=0, concat_axis=0, tiled=True)  63.2 us
    pallas_call x2, Pallas kernels, grid_stage(): pl.pallas_call(body, grid=(steps,), in_specs=in_specs, out_specs=pl.Block...  22.5 us
    pallas_call x2, Pallas kernels, block_stage(): pl.pallas_call(body, grid=(steps,), in_specs=strips + [whole(a.shape) for...  20.4 us
    pallas_call x1, Pallas kernels, lift_stage(): pl.pallas_call(lift_kernel, grid=(4,), in_specs=[pl.BlockSpec(memory_spac...  17.5 us
    all_to_all x2, waiting for transfers between devices, exchange(): return lax.all_to_all(x, axes, split_axis=0, concat_axis=0, tiled=True)  13.3 us
    all_to_all x2, starting transfers between devices, exchange(): return lax.all_to_all(x, axes, split_axis=0, concat_axis=0, tiled=True)  9.73 us
  transfers between devices with their start and end apart: 6, of which 3 were waited for; matrix products, arithmetic and copies ran while one was open for 2% of the time, Pallas kernels for 15%

profile of v7, /device:TPU:0, one launch (start us, length us, event | category | flops | bytes accessed | tf_op | source)
XLA Modules:
  0.0 158.3 jit_solution(14691524871956763925)
XLA Ops:
  0.0 0.7 dynamic-slice_bitcast_fusion.2
  0.7 0.9 dynamic-slice_bitcast_fusion
  1.7 0.7 collective-permute-start.1
  2.4 1.0 constant_dynamic-slice_fusion.3
  3.5 0.8 constant_dynamic-slice_fusion
  4.4 0.3 concatenate.14
  4.6 1.6 %collective-permute-start.2 = (f32[44,128]{1,0:T(8,128)S(1)}, f32[44,128]{1,0:T(8,128)S(1)}, u32[]{:S(2)}, u32[]{:S(2)}) collective-permute-start(f32[44,128]{1,0:T(8,128)S(1)} %concatenate.14), channel_id=1, source_target_pairs={{0,1},{2,3},{4,5},{6,7},{1,0},{3,2},{5,4},{7,6},{8,9},{10,11},{12,... | collective-permute-start | bytes 67592 | tf_op jit(solution)/shard_map/ppermute | solution.py:598
  6.5 0.7 collective-permute-start.3
  7.1 0.6 pad_add_fusion.place_ref
  7.7 0.8 collective-permute-done.2.cols_a_ref
  8.5 0.6 copy-done.4
  9.1 17.5 %shard_map.136 = (f32[32,128,128]{2,1,0:T(8,128)}, f32[32,4,128,128]{3,2,1,0:T(8,128)}, f32[128,128]{1,0:T(8,128)}) custom-call(s32[2]{0:T(128)} %pad_add_fusion.place_ref, f32[32,128,128]{2,1,0:T(8,128)} %field_ref.1, f32[8,32,128]{2,1,0:T(8,128)} %context_ref.1, f32[160,128]{1,0:T(8,128)} %copy-done.2, f32[160,128]{1,0:T(8,128)} %copy-done.3, ...), custom_call_target="tpu_custom_call" | custom-call | flops 8000000000 | bytes 14000000 | tf_op jit(solution)/shard_map/pallas_call | solution.py:398
  26.6 29.5 %all_to_all.20 = f32[128,1,128]{2,1,0:T(1,128)} all-to-all(f32[128,1,128]{2,1,0:T(1,128)} %bitcast.30), channel_id=1, replica_groups=mesh['rg'=8,'core'=2,'col'=8] {'rg','core','col'}, dimensions={0} | all-to-all | bytes 131072 | tf_op jit(solution)/shard_map/all_to_all | solution.py:643
  56.1 8.6 %shard_map.138 = f32[2048,128]{1,0:T(8,128)} custom-call(f32[32,128,128]{2,1,0:T(8,128)} %get-tuple-element.8.refs_0_, f32[32,4,128,128]{3,2,1,0:T(8,128)} %get-tuple-element.9.refs_1_, f32[128,128]{1,0:T(8,128)} %bitcast.28, f32[32,512]{1,0:T(8,128)} %refs_3_.5, f32[512,128]{1,0:T(8,128)} %refs_4_.5, f32[5,128]{1,0:T(8,128)} %refs_1_.3, ...), custom_call_target="tpu_custom_call" | custom-call | flops 14000000000 | bytes 8000000 | tf_op jit(solution)/shard_map/pallas_call | solution.py:506
  64.7 5.1 %all-to-all-start.2 = ((f32[64,32,128]{2,1,0:T(8,128)}), f32[64,32,128]{2,1,0:T(8,128)S(1)}, u32[]{:S(2)}, u32[]{:S(2)}) async-start(f32[64,32,128]{2,1,0:T(8,128)} %bitcast.27), calls=%async_computation.2 | async-start | bytes 2097152 | tf_op jit(solution)/shard_map/all_to_all | solution.py:643
  69.8 11.8 %shard_map.137 = f32[2048,128]{1,0:T(8,128)} custom-call(f32[32,128,128]{2,1,0:T(8,128)} %get-tuple-element.8.refs_0_, f32[32,4,128,128]{3,2,1,0:T(8,128)} %get-tuple-element.9.refs_1_, f32[128,128]{1,0:T(8,128)} %bitcast.29, f32[32,512]{1,0:T(8,128)} %refs_3_.5, f32[512,128]{1,0:T(8,128)} %refs_4_.5, f32[5,128]{1,0:T(8,128)} %refs_1_.3, ...), custom_call_target="tpu_custom_call" | custom-call | flops 14000000000 | bytes 8000000 | tf_op jit(solution)/shard_map/pallas_call | solution.py:506
  81.6 7.5 %all-to-all-done.2.refs_0_ = f32[64,32,128]{2,1,0:T(8,128)S(1)} async-done(((f32[64,32,128]{2,1,0:T(8,128)}), f32[64,32,128]{2,1,0:T(8,128)S(1)}, u32[]{:S(2)}, u32[]{:S(2)}) %all-to-all-start.2) | async-done | bytes 1048608 | tf_op jit(solution)/shard_map/all_to_all | solution.py:643
  89.1 4.7 %all-to-all-start.1 = ((f32[64,32,128]{2,1,0:T(8,128)}), f32[64,32,128]{2,1,0:T(8,128)S(1)}, u32[]{:S(2)}, u32[]{:S(2)}) async-start(f32[64,32,128]{2,1,0:T(8,128)} %bitcast.26), calls=%async_computation.1 | async-start | bytes 2097152 | tf_op jit(solution)/shard_map/all_to_all | solution.py:643
  93.8 12.7 %shard_map.139.refs_6_ = f32[64,64,128]{2,1,0:T(8,128)} custom-call(f32[64,32,128]{2,1,0:T(8,128)} %copy-done, f32[5,128]{1,0:T(8,128)} %refs_1_.3, f32[2,128,384]{2,1,0:T(8,128)} %refs_2_.3, f32[2,128,128]{2,1,0:T(8,128)} %refs_3_.7, f32[2,128,512]{2,1,0:T(8,128)} %refs_4_.7, f32[2,512,128]{2,1,0:T(8,128)} %refs_5_.7, f32[2,128,512]{2,1,0:T(8,128)} %refs_4_.7, ...), custom_call_target="tpu_custom_call" | custom-call | flops 14000000000 | bytes 4000000 | tf_op jit(solution)/shard_map/pallas_call | solution.py:577
  106.5 5.8 %all-to-all-done.1.refs_0_ = f32[64,32,128]{2,1,0:T(8,128)S(1)} async-done(((f32[64,32,128]{2,1,0:T(8,128)}), f32[64,32,128]{2,1,0:T(8,128)S(1)}, u32[]{:S(2)}, u32[]{:S(2)}) %all-to-all-start.1) | async-done | bytes 1048608 | tf_op jit(solution)/shard_map/all_to_all | solution.py:643
  112.3 1.0 copy-done.1
  113.2 9.8 %shard_map.140 = f32[64,64,128]{2,1,0:T(8,128)} custom-call(f32[64,32,128]{2,1,0:T(8,128)} %copy-done.1, f32[5,128]{1,0:T(8,128)} %refs_1_.3, f32[2,128,384]{2,1,0:T(8,128)} %refs_2_.3, f32[2,128,128]{2,1,0:T(8,128)} %refs_3_.7, f32[2,128,512]{2,1,0:T(8,128)} %refs_4_.7, f32[2,512,128]{2,1,0:T(8,128)} %refs_5_.7, ...), custom_call_target="tpu_custom_call", output_to_operand_aliasing={{}: (6, {})} | custom-call | flops 14000000000 | bytes 4000000 | tf_op jit(solution)/shard_map/pallas_call | solution.py:577
  123.0 33.7 %all_to_all.21 = f32[64,64,128]{2,1,0:T(8,128)S(1)} all-to-all(f32[64,64,128]{2,1,0:T(8,128)} %shard_map.140), channel_id=1, replica_groups=mesh['rg'=8,'core'=2,'col'=8] {'rg','col'}, dimensions={0} | all-to-all | bytes 4194304 | tf_op jit(solution)/shard_map/all_to_all | solution.py:643
  156.7 1.6 copy.18
  (22 shorter events, 0.4 us)
Async XLA Ops:
  1.6 2.6 %collective-permute-start = (f32[160,128]{1,0:T(8,128)S(1)}, f32[160,128]{1,0:T(8,128)S(1)}, u32[]{:S(2)}, u32[]{:S(2)}) collective-permute-start(f32[160,128]{1,0:T(8,128)S(1)} %pad_maximum_fusion), channel_id=1, source_target_pairs={{0,8},{16,24},{32,40},{48,56},{64,72},{80,88},{96,104},{112,120},{... | collective-permute-start | bytes 245768 | tf_op jit(solution)/shard_map/ppermute | solution.py:598
  1.7 2.6 %collective-permute-start.1 = (f32[160,128]{1,0:T(8,128)S(1)}, f32[160,128]{1,0:T(8,128)S(1)}, u32[]{:S(2)}, u32[]{:S(2)}) collective-permute-start(f32[160,128]{1,0:T(8,128)S(1)} %pad_maximum_fusion.1), channel_id=1, source_target_pairs={{8,16},{24,32},{40,48},{56,64},{72,80},{88,96},{104,112},{16,8},{3... | collective-permute-start | bytes 245768 | tf_op jit(solution)/shard_map/ppermute | solution.py:598
  4.3 4.3 %copy-start.2 = (f32[160,128]{1,0:T(8,128)}, f32[160,128]{1,0:T(8,128)S(1)}, u32[]{:S(2)}) copy-start(f32[160,128]{1,0:T(8,128)S(1)} %collective-permute-done.rows_a_ref) | copy-start | bytes 245764
  4.3 4.2 %copy-start.3 = (f32[160,128]{1,0:T(8,128)}, f32[160,128]{1,0:T(8,128)S(1)}, u32[]{:S(2)}) copy-start(f32[160,128]{1,0:T(8,128)S(1)} %collective-permute-done.1.rows_b_ref) | copy-start | bytes 245764
  4.6 3.9 %collective-permute-start.2 = (f32[44,128]{1,0:T(8,128)S(1)}, f32[44,128]{1,0:T(8,128)S(1)}, u32[]{:S(2)}, u32[]{:S(2)}) collective-permute-start(f32[44,128]{1,0:T(8,128)S(1)} %concatenate.14), channel_id=1, source_target_pairs={{0,1},{2,3},{4,5},{6,7},{1,0},{3,2},{5,4},{7,6},{8,9},{10,11},{12,... | collective-permute-start | bytes 67592 | tf_op jit(solution)/shard_map/ppermute | solution.py:598
  6.5 2.1 %collective-permute-start.3 = (f32[44,128]{1,0:T(8,128)S(1)}, f32[44,128]{1,0:T(8,128)S(1)}, u32[]{:S(2)}, u32[]{:S(2)}) collective-permute-start(f32[44,128]{1,0:T(8,128)S(1)} %concatenate.15), channel_id=1, source_target_pairs={{1,2},{3,4},{5,6},{2,1},{4,3},{6,5},{9,10},{11,12},{13,14},{10,9},... | collective-permute-start | bytes 67592 | tf_op jit(solution)/shard_map/ppermute | solution.py:598
  8.5 0.6 copy-start.4
  8.5 0.6 copy-start.5
  64.7 24.4 %all-to-all-start.2 = ((f32[64,32,128]{2,1,0:T(8,128)}), f32[64,32,128]{2,1,0:T(8,128)S(1)}, u32[]{:S(2)}, u32[]{:S(2)}) async-start(f32[64,32,128]{2,1,0:T(8,128)} %bitcast.27), calls=%async_computation.2 | async-start | bytes 2097152 | tf_op jit(solution)/shard_map/all_to_all | solution.py:643
  89.1 4.7 %copy-start = (f32[64,32,128]{2,1,0:T(8,128)}, f32[64,32,128]{2,1,0:T(8,128)S(1)}, u32[]{:S(2)}) copy-start(f32[64,32,128]{2,1,0:T(8,128)S(1)} %all-to-all-done.2.refs_0_) | copy-start | bytes 3145732
  89.1 23.1 %all-to-all-start.1 = ((f32[64,32,128]{2,1,0:T(8,128)}), f32[64,32,128]{2,1,0:T(8,128)S(1)}, u32[]{:S(2)}, u32[]{:S(2)}) async-start(f32[64,32,128]{2,1,0:T(8,128)} %bitcast.26), calls=%async_computation.1 | async-start | bytes 2097152 | tf_op jit(solution)/shard_map/all_to_all | solution.py:643
  112.3 1.0 copy-start.1

commit v8 on v7

--- a/solution.py
+++ b/solution.py
@@ -239,14 +239,18 @@
 
 def lift_kernel(
     place_ref, field_ref, context_ref, rows_a_ref, rows_b_ref, cols_a_ref, cols_b_ref, up_ref,
-    ctxw_ref, gains_ref, expand_ref, depth_ref, reduce_ref, lifted_ref, active_ref, sum_ref,
-    field, ends, sides, lift, ctx, coarse, hid, expand3, total, sems,
+    ctxw_ref, gains_ref, expand_ref, depth_ref, reduce_ref, lifted_ref, active_hbm, sum_ref,
+    active, field, ends, sides, lift, ctx, coarse, hid, expand3, total, sems, leave_sems,
 ):
     step = pl.program_id(0)
 
     def arrival(k):
         at = pl.ds(0, 9) if k == 0 else pl.ds(8 * k + 1, 8 if k < 3 else 7)
         return pltpu.make_async_copy(field_ref.at[at], field.at[at], sems.at[k])
+
+    def leaving(k, part):
+        at = (pl.ds(8 * k, 8), part)
+        return pltpu.make_async_copy(active.at[at], active_hbm.at[at], leave_sems.at[k, part])
 
     sublane = lax.broadcasted_iota(jnp.int32, (8, 128), 0)
     first_row, last_row = sublane == 0, sublane == 7
@@ -362,7 +366,7 @@
             for t in range(16):
                 following = column(t + 1) if t < 14 else last
                 out = bend(here[1] + before + (following[2] if t < 15 else end))
-                active_ref[r, part, 8 * t : 8 * t + 8] = out
+                active[8 * step + r, part, 8 * t : 8 * t + 8] = out
                 summed = summed + out
                 before, here = here[0], following
             return summed
@@ -371,6 +375,7 @@
         for r in range(8):
             summed = row(r, summed)
         total[:, lanes] = summed
+        leaving(step, part).start()
 
     @pl.when(step == 3)
     def _():
@@ -381,6 +386,9 @@
         squeezed = jnp.sum(squeezed, axis=0, keepdims=True)
         padded = lanes_of([squeezed, jnp.zeros((1, 128 - SQUEEZE), F32)])
         sum_ref[...] = jnp.broadcast_to(padded, sum_ref.shape)
+        for k in range(4):
+            for part in range(4):
+                leaving(k, part).wait()
 
 
 def whole(shape):
@@ -402,7 +410,7 @@
         + [whole(a.shape) for a in args[1:]],
         out_specs=[
             pl.BlockSpec((8, 128, CHANNELS), lambda s: (s, 0, 0)),
-            pl.BlockSpec((8, EXPANDED // 128, 128, 128), lambda s: (s, 0, 0, 0)),
+            pl.BlockSpec(memory_space=pl.ANY),
             whole((copies, 128)),
         ],
         out_shape=[
@@ -411,6 +419,7 @@
             jax.ShapeDtypeStruct((copies, 128), F32),
         ],
         scratch_shapes=[
+            pltpu.VMEM((32, EXPANDED // 128, 128, 128), F32),
             pltpu.VMEM((32, 128, CHANNELS), F32),
             pltpu.VMEM((2, 128, CHANNELS), F32),
             pltpu.VMEM((34, 8, CHANNELS), F32),
@@ -421,6 +430,7 @@
             pltpu.VMEM((3 * CHANNELS, EXPANDED), BF16),
             pltpu.VMEM((8, EXPANDED), F32),
             pltpu.SemaphoreType.DMA((4,)),
+            pltpu.SemaphoreType.DMA((4, 4)),
         ],
         compiler_params=pltpu.CompilerParams(vmem_limit_bytes=VMEM_LIMIT),
         cost_estimate=pl.CostEstimate(
@@ -523,25 +533,37 @@
     )(lifted, active, *rest, *weights)
 
 
-def grid_kernel(fed, x_ref, gains_ref, *refs):
-    scratch = 5 if fed else 7
-    out_ref, k3, qv3, out3, *feeds = refs[-scratch - 1 :]
+def grid_kernel(fed, chunk, x_hbm, gains_ref, *refs):
+    scratch = 8 if fed else 10
+    out_hbm, x_all, out_all, sems, k3, qv3, out3, *feeds = refs[-scratch - 1 :]
     qkv_ref, aout_ref, *feed_refs = refs[: 4 if fed else 6]
-
-    @pl.when(pl.program_id(0) == 0)
-    def _():
-        prepare_attention(qkv_ref, aout_ref, gains_ref[3:4], k3, qv3, out3)
-        prepare_feed(*feed_refs[:2], gains_ref[4:5], *feeds[:2])
-        if not fed:
-            prepare_feed(*feed_refs[2:], gains_ref[2:3], *feeds[2:])
-
-    stride = GRID_STEP // GROUP
-    flat_in = x_ref.reshape(GRID_STEP, CHANNELS)
-    flat_out = out_ref.reshape(GRID_STEP, CHANNELS)
+    stride = x_all.shape[1]
+    per_part = PART // GROUP
+    parts = GRID_STEP // PART
+
+    def arrival(part):
+        at = (slice(None), pl.ds(part * per_part, per_part))
+        return pltpu.make_async_copy(x_hbm.at[at], x_all.at[at], sems.at[0, part])
+
+    def leaving(part):
+        here = (slice(None), pl.ds(part * per_part, per_part))
+        there = (slice(None), pl.ds(chunk * stride + part * per_part, per_part))
+        return pltpu.make_async_copy(out_all.at[here], out_hbm.at[there], sems.at[1, part])
+
+    for part in range(parts):
+        arrival(part).start()
+    prepare_attention(qkv_ref, aout_ref, gains_ref[3:4], k3, qv3, out3)
+    prepare_feed(*feed_refs[:2], gains_ref[4:5], *feeds[:2])
+    if not fed:
+        prepare_feed(*feed_refs[2:], gains_ref[2:3], *feeds[2:])
+
+    flat_in = x_all.reshape(GRID_STEP, CHANNELS)
+    flat_out = out_all.reshape(GRID_STEP, CHANNELS)
 
     def group(part):
-        first = part * PART // GROUP
-        windows = [flat_in[pl.ds(first + p, GROUP, stride=stride), :] for p in range(PART // GROUP)]
+        first = part * per_part
+        arrival(part).wait()
+        windows = [flat_in[pl.ds(first + p, GROUP, stride=stride), :] for p in range(per_part)]
         pairs = [rows_of(windows[i : i + 2]) for i in range(0, len(windows), 2)]
         if not fed:
             pairs = yield from feed(pairs, *feeds[2:])
@@ -551,36 +573,41 @@
             for i in range(2):
                 window = first + 2 * p + i
                 flat_out[pl.ds(window, GROUP, stride=stride), :] = x[i * GROUP : (i + 1) * GROUP]
-
-    staggered(group(part) for part in range(GRID_STEP // PART))
+        leaving(part).start()
+
+    staggered(group(part) for part in range(parts))
+    for part in range(parts):
+        leaving(part).wait()
 
 
 def grid_stage(received, fed, gains, weights, chunk, earlier):
     per_device = received.shape[1]
-    steps = per_device * GROUP // GRID_STEP
-    shape = (GROUP, GRID_STEP // GROUP, CHANNELS)
-    in_specs = [pl.BlockSpec(shape, lambda s: (0, s, 0)), whole(gains.shape)]
-    in_specs += [of_layer(w, 1) for w in weights]
+    in_hbm = pl.BlockSpec(memory_space=pl.ANY)
+    in_specs = [in_hbm, whole(gains.shape)] + [of_layer(w, 1) for w in weights]
     args = (received, gains) + weights
     if not fed:
         in_specs += [of_layer(w, 0) for w in weights[2:]]
         args += weights[2:]
     aliases = {}
     if earlier is not None:
-        in_specs.append(pl.BlockSpec(memory_space=pl.ANY))
+        in_specs.append(in_hbm)
         aliases = {len(args): 0}
         args += (earlier,)
 
     def body(*refs):
-        grid_kernel(fed, *refs)
+        grid_kernel(fed, chunk, *refs)
 
     return pl.pallas_call(
         body,
-        grid=(steps,),
+        grid=(1,),
         in_specs=in_specs,
-        out_specs=pl.BlockSpec(shape, lambda s: (0, chunk * steps + s, 0)),
+        out_specs=in_hbm,
         out_shape=jax.ShapeDtypeStruct((GROUP, CHUNKS * per_device, CHANNELS), F32),
-        scratch_shapes=ATTENTION_SCRATCH + FEED_SCRATCH + ([] if fed else FEED_SCRATCH),
+        scratch_shapes=[pltpu.VMEM(received.shape, F32)] * 2
+        + [pltpu.SemaphoreType.DMA((2, GRID_STEP // PART))]
+        + ATTENTION_SCRATCH
+        + FEED_SCRATCH
+        + ([] if fed else FEED_SCRATCH),
         input_output_aliases=aliases,
         compiler_params=pltpu.CompilerParams(vmem_limit_bytes=VMEM_LIMIT),
         cost_estimate=pl.CostEstimate(

time: 159 us -> 161 us (1.013)
  Pallas kernels: 60.3 us -> 62.4 us
    pallas_call x2, Pallas kernels: 22.5 us -> 24.7 us  [grid_stage(): pl.pallas_call(body, grid=(1,), in_specs=in_specs, out_specs=in_hbm, out_...]
  transfers between devices with their start and end apart: 6 -> 6, of which waited for: 3 -> 3; matrix products, arithmetic and copies ran while one was open for 2% -> 2% of each run, Pallas kernels for 15% -> 16%
where the time goes in v8:
time: 161 us; the launch traced here: 160 us
  blocking collectives  64.3 us (40%)
  Pallas kernels  62.4 us (39%)
  waiting for transfers between devices  13.1 us (8%)
  starting transfers between devices  12.7 us (8%)
  local copies, waits for them, and re-layouts  7.05 us (4%)
    all_to_all x2, blocking collectives, exchange(): return lax.all_to_all(x, axes, split_axis=0, concat_axis=0, tiled=True)  64.3 us
    pallas_call x2, Pallas kernels, grid_stage(): pl.pallas_call(body, grid=(1,), in_specs=in_specs, out_specs=in_hbm, out_...  24.7 us
    pallas_call x2, Pallas kernels, block_stage(): pl.pallas_call(body, grid=(steps,), in_specs=strips + [whole(a.shape) for...  20.4 us
    pallas_call x1, Pallas kernels, lift_stage(): pl.pallas_call(lift_kernel, grid=(4,), in_specs=[pl.BlockSpec(memory_spac...  17.3 us
    all_to_all x2, waiting for transfers between devices, exchange(): return lax.all_to_all(x, axes, split_axis=0, concat_axis=0, tiled=True)  12.2 us
    all_to_all x2, starting transfers between devices, exchange(): return lax.all_to_all(x, axes, split_axis=0, concat_axis=0, tiled=True)  9.69 us
  transfers between devices with their start and end apart: 6, of which 3 were waited for; matrix products, arithmetic and copies ran while one was open for 2% of the time, Pallas kernels for 16%

profile of v8, /device:TPU:0, one launch (start us, length us, event | category | flops | bytes accessed | tf_op | source)
XLA Modules:
  0.0 160.5 jit_solution(3488013965305330373)
XLA Ops:
  0.0 0.7 dynamic-slice_bitcast_fusion.2
  0.7 0.9 dynamic-slice_bitcast_fusion
  1.7 0.7 collective-permute-start.1
  2.4 1.0 constant_dynamic-slice_fusion.3
  3.5 0.8 constant_dynamic-slice_fusion
  4.4 0.3 concatenate.14
  4.6 1.6 %collective-permute-start.2 = (f32[44,128]{1,0:T(8,128)S(1)}, f32[44,128]{1,0:T(8,128)S(1)}, u32[]{:S(2)}, u32[]{:S(2)}) collective-permute-start(f32[44,128]{1,0:T(8,128)S(1)} %concatenate.14), channel_id=1, source_target_pairs={{0,1},{2,3},{4,5},{6,7},{1,0},{3,2},{5,4},{7,6},{8,9},{10,11},{12,... | collective-permute-start | bytes 67592 | tf_op jit(solution)/shard_map/ppermute | solution.py:625
  6.5 0.7 collective-permute-start.3
  7.1 0.6 pad_add_fusion.place_ref
  7.7 0.8 collective-permute-done.2.cols_a_ref
  8.5 0.6 copy-done.4
  9.1 17.3 %shard_map.136 = (f32[32,128,128]{2,1,0:T(8,128)}, f32[32,4,128,128]{3,2,1,0:T(8,128)}, f32[128,128]{1,0:T(8,128)}) custom-call(s32[2]{0:T(128)} %pad_add_fusion.place_ref, f32[32,128,128]{2,1,0:T(8,128)} %field_ref.1, f32[8,32,128]{2,1,0:T(8,128)} %context_ref.1, f32[160,128]{1,0:T(8,128)} %copy-done.2, f32[160,128]{1,0:T(8,128)} %copy-done.3, ...), custom_call_target="tpu_custom_call" | custom-call | flops 8000000000 | bytes 14000000 | tf_op jit(solution)/shard_map/pallas_call | solution.py:406
  26.4 29.5 %all_to_all.20 = f32[128,1,128]{2,1,0:T(1,128)} all-to-all(f32[128,1,128]{2,1,0:T(1,128)} %bitcast.30), channel_id=1, replica_groups=mesh['rg'=8,'core'=2,'col'=8] {'rg','core','col'}, dimensions={0} | all-to-all | bytes 131072 | tf_op jit(solution)/shard_map/all_to_all | solution.py:670
  56.0 8.6 %shard_map.138 = f32[2048,128]{1,0:T(8,128)} custom-call(f32[32,128,128]{2,1,0:T(8,128)} %get-tuple-element.8.refs_0_, f32[32,4,128,128]{3,2,1,0:T(8,128)} %get-tuple-element.9.refs_1_, f32[128,128]{1,0:T(8,128)} %bitcast.28, f32[32,512]{1,0:T(8,128)} %refs_3_.5, f32[512,128]{1,0:T(8,128)} %refs_4_.5, f32[5,128]{1,0:T(8,128)} %refs_1_.3, ...), custom_call_target="tpu_custom_call" | custom-call | flops 14000000000 | bytes 8000000 | tf_op jit(solution)/shard_map/pallas_call | solution.py:516
  64.6 5.0 %all-to-all-start.2 = ((f32[64,32,128]{2,1,0:T(8,128)}), f32[64,32,128]{2,1,0:T(8,128)S(1)}, u32[]{:S(2)}, u32[]{:S(2)}) async-start(f32[64,32,128]{2,1,0:T(8,128)} %bitcast.27), calls=%async_computation.2 | async-start | bytes 2097152 | tf_op jit(solution)/shard_map/all_to_all | solution.py:670
  69.6 11.8 %shard_map.137 = f32[2048,128]{1,0:T(8,128)} custom-call(f32[32,128,128]{2,1,0:T(8,128)} %get-tuple-element.8.refs_0_, f32[32,4,128,128]{3,2,1,0:T(8,128)} %get-tuple-element.9.refs_1_, f32[128,128]{1,0:T(8,128)} %bitcast.29, f32[32,512]{1,0:T(8,128)} %refs_3_.5, f32[512,128]{1,0:T(8,128)} %refs_4_.5, f32[5,128]{1,0:T(8,128)} %refs_1_.3, ...), custom_call_target="tpu_custom_call" | custom-call | flops 14000000000 | bytes 8000000 | tf_op jit(solution)/shard_map/pallas_call | solution.py:516
  81.5 7.5 %all-to-all-done.2.refs_0_ = f32[64,32,128]{2,1,0:T(8,128)S(1)} async-done(((f32[64,32,128]{2,1,0:T(8,128)}), f32[64,32,128]{2,1,0:T(8,128)S(1)}, u32[]{:S(2)}, u32[]{:S(2)}) %all-to-all-start.2) | async-done | bytes 1048608 | tf_op jit(solution)/shard_map/all_to_all | solution.py:670
  89.0 4.7 %all-to-all-start.1 = ((f32[64,32,128]{2,1,0:T(8,128)}), f32[64,32,128]{2,1,0:T(8,128)S(1)}, u32[]{:S(2)}, u32[]{:S(2)}) async-start(f32[64,32,128]{2,1,0:T(8,128)} %bitcast.26), calls=%async_computation.1 | async-start | bytes 2097152 | tf_op jit(solution)/shard_map/all_to_all | solution.py:670
  93.7 13.8 %shard_map.139.refs_6_ = f32[64,64,128]{2,1,0:T(8,128)} custom-call(f32[64,32,128]{2,1,0:T(8,128)} %copy-done, f32[5,128]{1,0:T(8,128)} %refs_1_.3, f32[2,128,384]{2,1,0:T(8,128)} %refs_2_.3, f32[2,128,128]{2,1,0:T(8,128)} %refs_3_.7, f32[2,128,512]{2,1,0:T(8,128)} %refs_4_.7, f32[2,512,128]{2,1,0:T(8,128)} %refs_5_.7, f32[2,128,512]{2,1,0:T(8,128)} %refs_4_.7, ...), custom_call_target="tpu_custom_call" | custom-call | flops 14000000000 | bytes 4000000 | tf_op jit(solution)/shard_map/pallas_call | solution.py:600
  107.4 4.7 %all-to-all-done.1.refs_0_ = f32[64,32,128]{2,1,0:T(8,128)S(1)} async-done(((f32[64,32,128]{2,1,0:T(8,128)}), f32[64,32,128]{2,1,0:T(8,128)S(1)}, u32[]{:S(2)}, u32[]{:S(2)}) %all-to-all-start.1) | async-done | bytes 1048608 | tf_op jit(solution)/shard_map/all_to_all | solution.py:670
  112.1 1.0 copy-done.1
  113.1 10.9 %shard_map.140 = f32[64,64,128]{2,1,0:T(8,128)} custom-call(f32[64,32,128]{2,1,0:T(8,128)} %copy-done.1, f32[5,128]{1,0:T(8,128)} %refs_1_.3, f32[2,128,384]{2,1,0:T(8,128)} %refs_2_.3, f32[2,128,128]{2,1,0:T(8,128)} %refs_3_.7, f32[2,128,512]{2,1,0:T(8,128)} %refs_4_.7, f32[2,512,128]{2,1,0:T(8,128)} %refs_5_.7, ...), custom_call_target="tpu_custom_call", output_to_operand_aliasing={{}: (6, {})} | custom-call | flops 14000000000 | bytes 4000000 | tf_op jit(solution)/shard_map/pallas_call | solution.py:600
  124.1 34.8 %all_to_all.21 = f32[64,64,128]{2,1,0:T(8,128)S(1)} all-to-all(f32[64,64,128]{2,1,0:T(8,128)} %shard_map.140), channel_id=1, replica_groups=mesh['rg'=8,'core'=2,'col'=8] {'rg','col'}, dimensions={0} | all-to-all | bytes 4194304 | tf_op jit(solution)/shard_map/all_to_all | solution.py:670
  158.9 1.6 copy.18
  (22 shorter events, 0.4 us)
Async XLA Ops:
  1.6 2.6 %collective-permute-start = (f32[160,128]{1,0:T(8,128)S(1)}, f32[160,128]{1,0:T(8,128)S(1)}, u32[]{:S(2)}, u32[]{:S(2)}) collective-permute-start(f32[160,128]{1,0:T(8,128)S(1)} %pad_maximum_fusion), channel_id=1, source_target_pairs={{0,8},{16,24},{32,40},{48,56},{64,72},{80,88},{96,104},{112,120},{... | collective-permute-start | bytes 245768 | tf_op jit(solution)/shard_map/ppermute | solution.py:625
  1.7 2.6 %collective-permute-start.1 = (f32[160,128]{1,0:T(8,128)S(1)}, f32[160,128]{1,0:T(8,128)S(1)}, u32[]{:S(2)}, u32[]{:S(2)}) collective-permute-start(f32[160,128]{1,0:T(8,128)S(1)} %pad_maximum_fusion.1), channel_id=1, source_target_pairs={{8,16},{24,32},{40,48},{56,64},{72,80},{88,96},{104,112},{16,8},{3... | collective-permute-start | bytes 245768 | tf_op jit(solution)/shard_map/ppermute | solution.py:625
  4.3 4.3 %copy-start.2 = (f32[160,128]{1,0:T(8,128)}, f32[160,128]{1,0:T(8,128)S(1)}, u32[]{:S(2)}) copy-start(f32[160,128]{1,0:T(8,128)S(1)} %collective-permute-done.rows_a_ref) | copy-start | bytes 245764
  4.3 4.2 %copy-start.3 = (f32[160,128]{1,0:T(8,128)}, f32[160,128]{1,0:T(8,128)S(1)}, u32[]{:S(2)}) copy-start(f32[160,128]{1,0:T(8,128)S(1)} %collective-permute-done.1.rows_b_ref) | copy-start | bytes 245764
  4.6 3.9 %collective-permute-start.2 = (f32[44,128]{1,0:T(8,128)S(1)}, f32[44,128]{1,0:T(8,128)S(1)}, u32[]{:S(2)}, u32[]{:S(2)}) collective-permute-start(f32[44,128]{1,0:T(8,128)S(1)} %concatenate.14), channel_id=1, source_target_pairs={{0,1},{2,3},{4,5},{6,7},{1,0},{3,2},{5,4},{7,6},{8,9},{10,11},{12,... | collective-permute-start | bytes 67592 | tf_op jit(solution)/shard_map/ppermute | solution.py:625
  6.5 2.1 %collective-permute-start.3 = (f32[44,128]{1,0:T(8,128)S(1)}, f32[44,128]{1,0:T(8,128)S(1)}, u32[]{:S(2)}, u32[]{:S(2)}) collective-permute-start(f32[44,128]{1,0:T(8,128)S(1)} %concatenate.15), channel_id=1, source_target_pairs={{1,2},{3,4},{5,6},{2,1},{4,3},{6,5},{9,10},{11,12},{13,14},{10,9},... | collective-permute-start | bytes 67592 | tf_op jit(solution)/shard_map/ppermute | solution.py:625
  8.5 0.6 copy-start.4
  8.5 0.6 copy-start.5
  64.6 24.4 %all-to-all-start.2 = ((f32[64,32,128]{2,1,0:T(8,128)}), f32[64,32,128]{2,1,0:T(8,128)S(1)}, u32[]{:S(2)}, u32[]{:S(2)}) async-start(f32[64,32,128]{2,1,0:T(8,128)} %bitcast.27), calls=%async_computation.2 | async-start | bytes 2097152 | tf_op jit(solution)/shard_map/all_to_all | solution.py:670
  89.0 4.7 %copy-start = (f32[64,32,128]{2,1,0:T(8,128)}, f32[64,32,128]{2,1,0:T(8,128)S(1)}, u32[]{:S(2)}) copy-start(f32[64,32,128]{2,1,0:T(8,128)S(1)} %all-to-all-done.2.refs_0_) | copy-start | bytes 3145732
  89.0 23.2 %all-to-all-start.1 = ((f32[64,32,128]{2,1,0:T(8,128)}), f32[64,32,128]{2,1,0:T(8,128)S(1)}, u32[]{:S(2)}, u32[]{:S(2)}) async-start(f32[64,32,128]{2,1,0:T(8,128)} %bitcast.26), calls=%async_computation.1 | async-start | bytes 2097152 | tf_op jit(solution)/shard_map/all_to_all | solution.py:670
  112.1 1.0 copy-start.1

commit v9 on v7

--- a/solution.py
+++ b/solution.py
@@ -98,7 +98,7 @@
 
 
 PAIR = 2 * CELLS
-PART = 512
+PART = 1024
 
 
 def attend(pairs, k3, qv3, out3):
@@ -239,14 +239,18 @@
 
 def lift_kernel(
     place_ref, field_ref, context_ref, rows_a_ref, rows_b_ref, cols_a_ref, cols_b_ref, up_ref,
-    ctxw_ref, gains_ref, expand_ref, depth_ref, reduce_ref, lifted_ref, active_ref, sum_ref,
-    field, ends, sides, lift, ctx, coarse, hid, expand3, total, sems,
+    ctxw_ref, gains_ref, expand_ref, depth_ref, reduce_ref, lifted_ref, active_hbm, sum_ref,
+    active, field, ends, sides, lift, ctx, coarse, hid, expand3, total, sems, leave_sems,
 ):
     step = pl.program_id(0)
 
     def arrival(k):
         at = pl.ds(0, 9) if k == 0 else pl.ds(8 * k + 1, 8 if k < 3 else 7)
         return pltpu.make_async_copy(field_ref.at[at], field.at[at], sems.at[k])
+
+    def leaving(k, part):
+        at = (pl.ds(8 * k, 8), part)
+        return pltpu.make_async_copy(active.at[at], active_hbm.at[at], leave_sems.at[k, part])
 
     sublane = lax.broadcasted_iota(jnp.int32, (8, 128), 0)
     first_row, last_row = sublane == 0, sublane == 7
@@ -331,8 +335,7 @@
         def _():
             hid[0] = jnp.zeros((WIDE, EXPANDED), F32)
 
-    hidden_rows(8 * step + 2, 1, 2 * step + 1, 4)
-    hidden_rows(8 * step + 6, 5, 2 * step + 1, 4)
+    hidden_rows(8 * step + 2, 1, 2 * step + 1, 8)
 
     @pl.when((step == 3) & (place_ref[0] == 15))
     def _():
@@ -362,7 +365,7 @@
             for t in range(16):
                 following = column(t + 1) if t < 14 else last
                 out = bend(here[1] + before + (following[2] if t < 15 else end))
-                active_ref[r, part, 8 * t : 8 * t + 8] = out
+                active[8 * step + r, part, 8 * t : 8 * t + 8] = out
                 summed = summed + out
                 before, here = here[0], following
             return summed
@@ -371,6 +374,7 @@
         for r in range(8):
             summed = row(r, summed)
         total[:, lanes] = summed
+        leaving(step, part).start()
 
     @pl.when(step == 3)
     def _():
@@ -381,6 +385,9 @@
         squeezed = jnp.sum(squeezed, axis=0, keepdims=True)
         padded = lanes_of([squeezed, jnp.zeros((1, 128 - SQUEEZE), F32)])
         sum_ref[...] = jnp.broadcast_to(padded, sum_ref.shape)
+        for k in range(4):
+            for part in range(4):
+                leaving(k, part).wait()
 
 
 def whole(shape):
@@ -402,7 +409,7 @@
         + [whole(a.shape) for a in args[1:]],
         out_specs=[
             pl.BlockSpec((8, 128, CHANNELS), lambda s: (s, 0, 0)),
-            pl.BlockSpec((8, EXPANDED // 128, 128, 128), lambda s: (s, 0, 0, 0)),
+            pl.BlockSpec(memory_space=pl.ANY),
             whole((copies, 128)),
         ],
         out_shape=[
@@ -411,6 +418,7 @@
             jax.ShapeDtypeStruct((copies, 128), F32),
         ],
         scratch_shapes=[
+            pltpu.VMEM((32, EXPANDED // 128, 128, 128), F32),
             pltpu.VMEM((32, 128, CHANNELS), F32),
             pltpu.VMEM((2, 128, CHANNELS), F32),
             pltpu.VMEM((34, 8, CHANNELS), F32),
@@ -421,6 +429,7 @@
             pltpu.VMEM((3 * CHANNELS, EXPANDED), BF16),
             pltpu.VMEM((8, EXPANDED), F32),
             pltpu.SemaphoreType.DMA((4,)),
+            pltpu.SemaphoreType.DMA((4, 4)),
         ],
         compiler_params=pltpu.CompilerParams(vmem_limit_bytes=VMEM_LIMIT),
         cost_estimate=pl.CostEstimate(

time: 159 us -> 160 us (level)
  transfers between devices with their start and end apart: 6 -> 6, of which waited for: 3 -> 3; matrix products, arithmetic and copies ran while one was open for 2% -> 2% of each run, Pallas kernels for 15% -> 16%
where the time goes in v9:
time: 160 us; the launch traced here: 159 us
  blocking collectives  63.6 us (40%)
  Pallas kernels  61.8 us (39%)
  waiting for transfers between devices  13.4 us (8%)
  starting transfers between devices  12.8 us (8%)
  local copies, waits for them, and re-layouts  7.05 us (4%)
    all_to_all x2, blocking collectives, exchange(): return lax.all_to_all(x, axes, split_axis=0, concat_axis=0, tiled=True)  63.6 us
    pallas_call x2, Pallas kernels, grid_stage(): pl.pallas_call(body, grid=(steps,), in_specs=in_specs, out_specs=pl.Block...  23.5 us
    pallas_call x2, Pallas kernels, block_stage(): pl.pallas_call(body, grid=(steps,), in_specs=strips + [whole(a.shape) for...  20.9 us
    pallas_call x1, Pallas kernels, lift_stage(): pl.pallas_call(lift_kernel, grid=(4,), in_specs=[pl.BlockSpec(memory_spac...  17.4 us
    all_to_all x2, waiting for transfers between devices, exchange(): return lax.all_to_all(x, axes, split_axis=0, concat_axis=0, tiled=True)  12.6 us
    all_to_all x2, starting transfers between devices, exchange(): return lax.all_to_all(x, axes, split_axis=0, concat_axis=0, tiled=True)  9.7 us
  transfers between devices with their start and end apart: 6, of which 3 were waited for; matrix products, arithmetic and copies ran while one was open for 2% of the time, Pallas kernels for 16%

profile of v9, /device:TPU:0, one launch (start us, length us, event | category | flops | bytes accessed | tf_op | source)
XLA Modules:
  0.0 159.4 jit_solution(9151208871692598055)
XLA Ops:
  0.0 0.7 dynamic-slice_bitcast_fusion.2
  0.7 0.9 dynamic-slice_bitcast_fusion
  1.7 0.7 collective-permute-start.1
  2.4 1.0 constant_dynamic-slice_fusion.3
  3.5 0.8 constant_dynamic-slice_fusion
  4.4 0.3 concatenate.14
  4.6 1.6 %collective-permute-start.2 = (f32[44,128]{1,0:T(8,128)S(1)}, f32[44,128]{1,0:T(8,128)S(1)}, u32[]{:S(2)}, u32[]{:S(2)}) collective-permute-start(f32[44,128]{1,0:T(8,128)S(1)} %concatenate.14), channel_id=1, source_target_pairs={{0,1},{2,3},{4,5},{6,7},{1,0},{3,2},{5,4},{7,6},{8,9},{10,11},{12,... | collective-permute-start | bytes 67592 | tf_op jit(solution)/shard_map/ppermute | solution.py:607
  6.5 0.7 collective-permute-start.3
  7.1 0.6 pad_add_fusion.place_ref
  7.7 0.8 collective-permute-done.2.cols_a_ref
  8.5 0.6 copy-done.4
  9.1 17.4 %shard_map.136 = (f32[32,128,128]{2,1,0:T(8,128)}, f32[32,4,128,128]{3,2,1,0:T(8,128)}, f32[128,128]{1,0:T(8,128)}) custom-call(s32[2]{0:T(128)} %pad_add_fusion.place_ref, f32[32,128,128]{2,1,0:T(8,128)} %field_ref.1, f32[8,32,128]{2,1,0:T(8,128)} %context_ref.1, f32[160,128]{1,0:T(8,128)} %copy-done.2, f32[160,128]{1,0:T(8,128)} %copy-done.3, ...), custom_call_target="tpu_custom_call" | custom-call | flops 8000000000 | bytes 14000000 | tf_op jit(solution)/shard_map/pallas_call | solution.py:405
  26.6 29.5 %all_to_all.20 = f32[128,1,128]{2,1,0:T(1,128)} all-to-all(f32[128,1,128]{2,1,0:T(1,128)} %bitcast.30), channel_id=1, replica_groups=mesh['rg'=8,'core'=2,'col'=8] {'rg','core','col'}, dimensions={0} | all-to-all | bytes 131072 | tf_op jit(solution)/shard_map/all_to_all | solution.py:652
  56.1 8.8 %shard_map.138 = f32[2048,128]{1,0:T(8,128)} custom-call(f32[32,128,128]{2,1,0:T(8,128)} %get-tuple-element.8.refs_0_, f32[32,4,128,128]{3,2,1,0:T(8,128)} %get-tuple-element.9.refs_1_, f32[128,128]{1,0:T(8,128)} %bitcast.28, f32[32,512]{1,0:T(8,128)} %refs_3_.5, f32[512,128]{1,0:T(8,128)} %refs_4_.5, f32[5,128]{1,0:T(8,128)} %refs_1_.3, ...), custom_call_target="tpu_custom_call" | custom-call | flops 14000000000 | bytes 8000000 | tf_op jit(solution)/shard_map/pallas_call | solution.py:515
  64.8 5.1 %all-to-all-start.2 = ((f32[64,32,128]{2,1,0:T(8,128)}), f32[64,32,128]{2,1,0:T(8,128)S(1)}, u32[]{:S(2)}, u32[]{:S(2)}) async-start(f32[64,32,128]{2,1,0:T(8,128)} %bitcast.27), calls=%async_computation.2 | async-start | bytes 2097152 | tf_op jit(solution)/shard_map/all_to_all | solution.py:652
  69.9 12.1 %shard_map.137 = f32[2048,128]{1,0:T(8,128)} custom-call(f32[32,128,128]{2,1,0:T(8,128)} %get-tuple-element.8.refs_0_, f32[32,4,128,128]{3,2,1,0:T(8,128)} %get-tuple-element.9.refs_1_, f32[128,128]{1,0:T(8,128)} %bitcast.29, f32[32,512]{1,0:T(8,128)} %refs_3_.5, f32[512,128]{1,0:T(8,128)} %refs_4_.5, f32[5,128]{1,0:T(8,128)} %refs_1_.3, ...), custom_call_target="tpu_custom_call" | custom-call | flops 14000000000 | bytes 8000000 | tf_op jit(solution)/shard_map/pallas_call | solution.py:515
  82.0 7.2 %all-to-all-done.2.refs_0_ = f32[64,32,128]{2,1,0:T(8,128)S(1)} async-done(((f32[64,32,128]{2,1,0:T(8,128)}), f32[64,32,128]{2,1,0:T(8,128)S(1)}, u32[]{:S(2)}, u32[]{:S(2)}) %all-to-all-start.2) | async-done | bytes 1048608 | tf_op jit(solution)/shard_map/all_to_all | solution.py:652
  89.2 4.7 %all-to-all-start.1 = ((f32[64,32,128]{2,1,0:T(8,128)}), f32[64,32,128]{2,1,0:T(8,128)S(1)}, u32[]{:S(2)}, u32[]{:S(2)}) async-start(f32[64,32,128]{2,1,0:T(8,128)} %bitcast.26), calls=%async_computation.1 | async-start | bytes 2097152 | tf_op jit(solution)/shard_map/all_to_all | solution.py:652
  93.9 13.1 %shard_map.139.refs_6_ = f32[64,64,128]{2,1,0:T(8,128)} custom-call(f32[64,32,128]{2,1,0:T(8,128)} %copy-done, f32[5,128]{1,0:T(8,128)} %refs_1_.3, f32[2,128,384]{2,1,0:T(8,128)} %refs_2_.3, f32[2,128,128]{2,1,0:T(8,128)} %refs_3_.7, f32[2,128,512]{2,1,0:T(8,128)} %refs_4_.7, f32[2,512,128]{2,1,0:T(8,128)} %refs_5_.7, f32[2,128,512]{2,1,0:T(8,128)} %refs_4_.7, ...), custom_call_target="tpu_custom_call" | custom-call | flops 14000000000 | bytes 4000000 | tf_op jit(solution)/shard_map/pallas_call | solution.py:586
  107.0 5.3 %all-to-all-done.1.refs_0_ = f32[64,32,128]{2,1,0:T(8,128)S(1)} async-done(((f32[64,32,128]{2,1,0:T(8,128)}), f32[64,32,128]{2,1,0:T(8,128)S(1)}, u32[]{:S(2)}, u32[]{:S(2)}) %all-to-all-start.1) | async-done | bytes 1048608 | tf_op jit(solution)/shard_map/all_to_all | solution.py:652
  112.4 1.0 copy-done.1
  113.3 10.4 %shard_map.140 = f32[64,64,128]{2,1,0:T(8,128)} custom-call(f32[64,32,128]{2,1,0:T(8,128)} %copy-done.1, f32[5,128]{1,0:T(8,128)} %refs_1_.3, f32[2,128,384]{2,1,0:T(8,128)} %refs_2_.3, f32[2,128,128]{2,1,0:T(8,128)} %refs_3_.7, f32[2,128,512]{2,1,0:T(8,128)} %refs_4_.7, f32[2,512,128]{2,1,0:T(8,128)} %refs_5_.7, ...), custom_call_target="tpu_custom_call", output_to_operand_aliasing={{}: (6, {})} | custom-call | flops 14000000000 | bytes 4000000 | tf_op jit(solution)/shard_map/pallas_call | solution.py:586
  123.7 34.1 %all_to_all.21 = f32[64,64,128]{2,1,0:T(8,128)S(1)} all-to-all(f32[64,64,128]{2,1,0:T(8,128)} %shard_map.140), channel_id=1, replica_groups=mesh['rg'=8,'core'=2,'col'=8] {'rg','col'}, dimensions={0} | all-to-all | bytes 4194304 | tf_op jit(solution)/shard_map/all_to_all | solution.py:652
  157.9 1.6 copy.18
  (22 shorter events, 0.4 us)
Async XLA Ops:
  1.6 2.6 %collective-permute-start = (f32[160,128]{1,0:T(8,128)S(1)}, f32[160,128]{1,0:T(8,128)S(1)}, u32[]{:S(2)}, u32[]{:S(2)}) collective-permute-start(f32[160,128]{1,0:T(8,128)S(1)} %pad_maximum_fusion), channel_id=1, source_target_pairs={{0,8},{16,24},{32,40},{48,56},{64,72},{80,88},{96,104},{112,120},{... | collective-permute-start | bytes 245768 | tf_op jit(solution)/shard_map/ppermute | solution.py:607
  1.7 2.6 %collective-permute-start.1 = (f32[160,128]{1,0:T(8,128)S(1)}, f32[160,128]{1,0:T(8,128)S(1)}, u32[]{:S(2)}, u32[]{:S(2)}) collective-permute-start(f32[160,128]{1,0:T(8,128)S(1)} %pad_maximum_fusion.1), channel_id=1, source_target_pairs={{8,16},{24,32},{40,48},{56,64},{72,80},{88,96},{104,112},{16,8},{3... | collective-permute-start | bytes 245768 | tf_op jit(solution)/shard_map/ppermute | solution.py:607
  4.3 4.3 %copy-start.2 = (f32[160,128]{1,0:T(8,128)}, f32[160,128]{1,0:T(8,128)S(1)}, u32[]{:S(2)}) copy-start(f32[160,128]{1,0:T(8,128)S(1)} %collective-permute-done.rows_a_ref) | copy-start | bytes 245764
  4.3 4.2 %copy-start.3 = (f32[160,128]{1,0:T(8,128)}, f32[160,128]{1,0:T(8,128)S(1)}, u32[]{:S(2)}) copy-start(f32[160,128]{1,0:T(8,128)S(1)} %collective-permute-done.1.rows_b_ref) | copy-start | bytes 245764
  4.6 3.9 %collective-permute-start.2 = (f32[44,128]{1,0:T(8,128)S(1)}, f32[44,128]{1,0:T(8,128)S(1)}, u32[]{:S(2)}, u32[]{:S(2)}) collective-permute-start(f32[44,128]{1,0:T(8,128)S(1)} %concatenate.14), channel_id=1, source_target_pairs={{0,1},{2,3},{4,5},{6,7},{1,0},{3,2},{5,4},{7,6},{8,9},{10,11},{12,... | collective-permute-start | bytes 67592 | tf_op jit(solution)/shard_map/ppermute | solution.py:607
  6.5 2.1 %collective-permute-start.3 = (f32[44,128]{1,0:T(8,128)S(1)}, f32[44,128]{1,0:T(8,128)S(1)}, u32[]{:S(2)}, u32[]{:S(2)}) collective-permute-start(f32[44,128]{1,0:T(8,128)S(1)} %concatenate.15), channel_id=1, source_target_pairs={{1,2},{3,4},{5,6},{2,1},{4,3},{6,5},{9,10},{11,12},{13,14},{10,9},... | collective-permute-start | bytes 67592 | tf_op jit(solution)/shard_map/ppermute | solution.py:607
  8.5 0.6 copy-start.4
  8.5 0.6 copy-start.5
  64.8 24.4 %all-to-all-start.2 = ((f32[64,32,128]{2,1,0:T(8,128)}), f32[64,32,128]{2,1,0:T(8,128)S(1)}, u32[]{:S(2)}, u32[]{:S(2)}) async-start(f32[64,32,128]{2,1,0:T(8,128)} %bitcast.27), calls=%async_computation.2 | async-start | bytes 2097152 | tf_op jit(solution)/shard_map/all_to_all | solution.py:652
  89.2 4.7 %copy-start = (f32[64,32,128]{2,1,0:T(8,128)}, f32[64,32,128]{2,1,0:T(8,128)S(1)}, u32[]{:S(2)}) copy-start(f32[64,32,128]{2,1,0:T(8,128)S(1)} %all-to-all-done.2.refs_0_) | copy-start | bytes 3145732
  89.2 23.1 %all-to-all-start.1 = ((f32[64,32,128]{2,1,0:T(8,128)}), f32[64,32,128]{2,1,0:T(8,128)S(1)}, u32[]{:S(2)}, u32[]{:S(2)}) async-start(f32[64,32,128]{2,1,0:T(8,128)} %bitcast.26), calls=%async_computation.1 | async-start | bytes 2097152 | tf_op jit(solution)/shard_map/all_to_all | solution.py:652
  112.4 1.0 copy-start.1

commit v10 on v9

--- a/solution.py
+++ b/solution.py
@@ -98,7 +98,7 @@
 
 
 PAIR = 2 * CELLS
-PART = 1024
+PART = 256
 
 
 def attend(pairs, k3, qv3, out3):
@@ -335,7 +335,8 @@
         def _():
             hid[0] = jnp.zeros((WIDE, EXPANDED), F32)
 
-    hidden_rows(8 * step + 2, 1, 2 * step + 1, 8)
+    hidden_rows(8 * step + 2, 1, 2 * step + 1, 4)
+    hidden_rows(8 * step + 6, 5, 2 * step + 1, 4)
 
     @pl.when((step == 3) & (place_ref[0] == 15))
     def _():

time: 160 us -> 159 us (level)
  transfers between devices with their start and end apart: 6 -> 6, of which waited for: 3 -> 3; matrix products, arithmetic and copies ran while one was open for 2% -> 2% of each run, Pallas kernels for 16% -> 15%
where the time goes in v10:
time: 159 us
  blocking collectives  62.8 us (39%)
  Pallas kernels  60.7 us (38%)
  waiting for transfers between devices  14.5 us (9%)
  starting transfers between devices  12.8 us (8%)
  local copies, waits for them, and re-layouts  7.05 us (4%)
    all_to_all x2, blocking collectives, exchange(): return lax.all_to_all(x, axes, split_axis=0, concat_axis=0, tiled=True)  62.8 us
    pallas_call x2, Pallas kernels, grid_stage(): pl.pallas_call(body, grid=(steps,), in_specs=in_specs, out_specs=pl.Block...  22.7 us
    pallas_call x2, Pallas kernels, block_stage(): pl.pallas_call(body, grid=(steps,), in_specs=strips + [whole(a.shape) for...  20.8 us
    pallas_call x1, Pallas kernels, lift_stage(): pl.pallas_call(lift_kernel, grid=(4,), in_specs=[pl.BlockSpec(memory_spac...  17.3 us
    all_to_all x2, waiting for transfers between devices, exchange(): return lax.all_to_all(x, axes, split_axis=0, concat_axis=0, tiled=True)  13.7 us
    all_to_all x2, starting transfers between devices, exchange(): return lax.all_to_all(x, axes, split_axis=0, concat_axis=0, tiled=True)  9.71 us
  transfers between devices with their start and end apart: 6, of which 3 were waited for; matrix products, arithmetic and copies ran while one was open for 2% of the time, Pallas kernels for 15%

profile of v10, /device:TPU:0, one launch (start us, length us, event | category | flops | bytes accessed | tf_op | source)
XLA Modules:
  0.0 158.7 jit_solution(13877028081760560333)
XLA Ops:
  0.0 0.7 dynamic-slice_bitcast_fusion.2
  0.7 0.9 dynamic-slice_bitcast_fusion
  1.7 0.7 collective-permute-start.1
  2.4 1.0 constant_dynamic-slice_fusion.3
  3.5 0.8 constant_dynamic-slice_fusion
  4.4 0.3 concatenate.14
  4.6 1.6 %collective-permute-start.2 = (f32[44,128]{1,0:T(8,128)S(1)}, f32[44,128]{1,0:T(8,128)S(1)}, u32[]{:S(2)}, u32[]{:S(2)}) collective-permute-start(f32[44,128]{1,0:T(8,128)S(1)} %concatenate.14), channel_id=1, source_target_pairs={{0,1},{2,3},{4,5},{6,7},{1,0},{3,2},{5,4},{7,6},{8,9},{10,11},{12,... | collective-permute-start | bytes 67592 | tf_op jit(solution)/shard_map/ppermute | solution.py:608
  6.5 0.7 collective-permute-start.3
  7.1 0.6 pad_add_fusion.place_ref
  7.7 0.8 collective-permute-done.2.cols_a_ref
  8.5 0.6 copy-done.4
  9.1 17.3 %shard_map.136 = (f32[32,128,128]{2,1,0:T(8,128)}, f32[32,4,128,128]{3,2,1,0:T(8,128)}, f32[128,128]{1,0:T(8,128)}) custom-call(s32[2]{0:T(128)} %pad_add_fusion.place_ref, f32[32,128,128]{2,1,0:T(8,128)} %field_ref.1, f32[8,32,128]{2,1,0:T(8,128)} %context_ref.1, f32[160,128]{1,0:T(8,128)} %copy-done.2, f32[160,128]{1,0:T(8,128)} %copy-done.3, ...), custom_call_target="tpu_custom_call" | custom-call | flops 8000000000 | bytes 14000000 | tf_op jit(solution)/shard_map/pallas_call | solution.py:406
  26.4 29.5 %all_to_all.20 = f32[128,1,128]{2,1,0:T(1,128)} all-to-all(f32[128,1,128]{2,1,0:T(1,128)} %bitcast.30), channel_id=1, replica_groups=mesh['rg'=8,'core'=2,'col'=8] {'rg','core','col'}, dimensions={0} | all-to-all | bytes 131072 | tf_op jit(solution)/shard_map/all_to_all | solution.py:653
  56.0 8.9 %shard_map.138 = f32[2048,128]{1,0:T(8,128)} custom-call(f32[32,128,128]{2,1,0:T(8,128)} %get-tuple-element.8.refs_0_, f32[32,4,128,128]{3,2,1,0:T(8,128)} %get-tuple-element.9.refs_1_, f32[128,128]{1,0:T(8,128)} %bitcast.28, f32[32,512]{1,0:T(8,128)} %refs_3_.5, f32[512,128]{1,0:T(8,128)} %refs_4_.5, f32[5,128]{1,0:T(8,128)} %refs_1_.3, ...), custom_call_target="tpu_custom_call" | custom-call | flops 14000000000 | bytes 8000000 | tf_op jit(solution)/shard_map/pallas_call | solution.py:516
  64.9 5.1 %all-to-all-start.2 = ((f32[64,32,128]{2,1,0:T(8,128)}), f32[64,32,128]{2,1,0:T(8,128)S(1)}, u32[]{:S(2)}, u32[]{:S(2)}) async-start(f32[64,32,128]{2,1,0:T(8,128)} %bitcast.27), calls=%async_computation.2 | async-start | bytes 2097152 | tf_op jit(solution)/shard_map/all_to_all | solution.py:653
  70.0 11.8 %shard_map.137 = f32[2048,128]{1,0:T(8,128)} custom-call(f32[32,128,128]{2,1,0:T(8,128)} %get-tuple-element.8.refs_0_, f32[32,4,128,128]{3,2,1,0:T(8,128)} %get-tuple-element.9.refs_1_, f32[128,128]{1,0:T(8,128)} %bitcast.29, f32[32,512]{1,0:T(8,128)} %refs_3_.5, f32[512,128]{1,0:T(8,128)} %refs_4_.5, f32[5,128]{1,0:T(8,128)} %refs_1_.3, ...), custom_call_target="tpu_custom_call" | custom-call | flops 14000000000 | bytes 8000000 | tf_op jit(solution)/shard_map/pallas_call | solution.py:516
  81.8 7.5 %all-to-all-done.2.refs_0_ = f32[64,32,128]{2,1,0:T(8,128)S(1)} async-done(((f32[64,32,128]{2,1,0:T(8,128)}), f32[64,32,128]{2,1,0:T(8,128)S(1)}, u32[]{:S(2)}, u32[]{:S(2)}) %all-to-all-start.2) | async-done | bytes 1048608 | tf_op jit(solution)/shard_map/all_to_all | solution.py:653
  89.3 4.7 %all-to-all-start.1 = ((f32[64,32,128]{2,1,0:T(8,128)}), f32[64,32,128]{2,1,0:T(8,128)S(1)}, u32[]{:S(2)}, u32[]{:S(2)}) async-start(f32[64,32,128]{2,1,0:T(8,128)} %bitcast.26), calls=%async_computation.1 | async-start | bytes 2097152 | tf_op jit(solution)/shard_map/all_to_all | solution.py:653
  94.0 12.2 %shard_map.139.refs_6_ = f32[64,64,128]{2,1,0:T(8,128)} custom-call(f32[64,32,128]{2,1,0:T(8,128)} %copy-done, f32[5,128]{1,0:T(8,128)} %refs_1_.3, f32[2,128,384]{2,1,0:T(8,128)} %refs_2_.3, f32[2,128,128]{2,1,0:T(8,128)} %refs_3_.7, f32[2,128,512]{2,1,0:T(8,128)} %refs_4_.7, f32[2,512,128]{2,1,0:T(8,128)} %refs_5_.7, f32[2,128,512]{2,1,0:T(8,128)} %refs_4_.7, ...), custom_call_target="tpu_custom_call" | custom-call | flops 14000000000 | bytes 4000000 | tf_op jit(solution)/shard_map/pallas_call | solution.py:587
  106.2 6.2 %all-to-all-done.1.refs_0_ = f32[64,32,128]{2,1,0:T(8,128)S(1)} async-done(((f32[64,32,128]{2,1,0:T(8,128)}), f32[64,32,128]{2,1,0:T(8,128)S(1)}, u32[]{:S(2)}, u32[]{:S(2)}) %all-to-all-start.1) | async-done | bytes 1048608 | tf_op jit(solution)/shard_map/all_to_all | solution.py:653
  112.4 1.0 copy-done.1
  113.4 10.5 %shard_map.140 = f32[64,64,128]{2,1,0:T(8,128)} custom-call(f32[64,32,128]{2,1,0:T(8,128)} %copy-done.1, f32[5,128]{1,0:T(8,128)} %refs_1_.3, f32[2,128,384]{2,1,0:T(8,128)} %refs_2_.3, f32[2,128,128]{2,1,0:T(8,128)} %refs_3_.7, f32[2,128,512]{2,1,0:T(8,128)} %refs_4_.7, f32[2,512,128]{2,1,0:T(8,128)} %refs_5_.7, ...), custom_call_target="tpu_custom_call", output_to_operand_aliasing={{}: (6, {})} | custom-call | flops 14000000000 | bytes 4000000 | tf_op jit(solution)/shard_map/pallas_call | solution.py:587
  123.9 33.3 %all_to_all.21 = f32[64,64,128]{2,1,0:T(8,128)S(1)} all-to-all(f32[64,64,128]{2,1,0:T(8,128)} %shard_map.140), channel_id=1, replica_groups=mesh['rg'=8,'core'=2,'col'=8] {'rg','col'}, dimensions={0} | all-to-all | bytes 4194304 | tf_op jit(solution)/shard_map/all_to_all | solution.py:653
  157.1 1.6 copy.18
  (22 shorter events, 0.4 us)
Async XLA Ops:
  1.6 2.6 %collective-permute-start = (f32[160,128]{1,0:T(8,128)S(1)}, f32[160,128]{1,0:T(8,128)S(1)}, u32[]{:S(2)}, u32[]{:S(2)}) collective-permute-start(f32[160,128]{1,0:T(8,128)S(1)} %pad_maximum_fusion), channel_id=1, source_target_pairs={{0,8},{16,24},{32,40},{48,56},{64,72},{80,88},{96,104},{112,120},{... | collective-permute-start | bytes 245768 | tf_op jit(solution)/shard_map/ppermute | solution.py:608
  1.7 2.6 %collective-permute-start.1 = (f32[160,128]{1,0:T(8,128)S(1)}, f32[160,128]{1,0:T(8,128)S(1)}, u32[]{:S(2)}, u32[]{:S(2)}) collective-permute-start(f32[160,128]{1,0:T(8,128)S(1)} %pad_maximum_fusion.1), channel_id=1, source_target_pairs={{8,16},{24,32},{40,48},{56,64},{72,80},{88,96},{104,112},{16,8},{3... | collective-permute-start | bytes 245768 | tf_op jit(solution)/shard_map/ppermute | solution.py:608
  4.3 4.3 %copy-start.2 = (f32[160,128]{1,0:T(8,128)}, f32[160,128]{1,0:T(8,128)S(1)}, u32[]{:S(2)}) copy-start(f32[160,128]{1,0:T(8,128)S(1)} %collective-permute-done.rows_a_ref) | copy-start | bytes 245764
  4.3 4.2 %copy-start.3 = (f32[160,128]{1,0:T(8,128)}, f32[160,128]{1,0:T(8,128)S(1)}, u32[]{:S(2)}) copy-start(f32[160,128]{1,0:T(8,128)S(1)} %collective-permute-done.1.rows_b_ref) | copy-start | bytes 245764
  4.6 3.9 %collective-permute-start.2 = (f32[44,128]{1,0:T(8,128)S(1)}, f32[44,128]{1,0:T(8,128)S(1)}, u32[]{:S(2)}, u32[]{:S(2)}) collective-permute-start(f32[44,128]{1,0:T(8,128)S(1)} %concatenate.14), channel_id=1, source_target_pairs={{0,1},{2,3},{4,5},{6,7},{1,0},{3,2},{5,4},{7,6},{8,9},{10,11},{12,... | collective-permute-start | bytes 67592 | tf_op jit(solution)/shard_map/ppermute | solution.py:608
  6.5 2.1 %collective-permute-start.3 = (f32[44,128]{1,0:T(8,128)S(1)}, f32[44,128]{1,0:T(8,128)S(1)}, u32[]{:S(2)}, u32[]{:S(2)}) collective-permute-start(f32[44,128]{1,0:T(8,128)S(1)} %concatenate.15), channel_id=1, source_target_pairs={{1,2},{3,4},{5,6},{2,1},{4,3},{6,5},{9,10},{11,12},{13,14},{10,9},... | collective-permute-start | bytes 67592 | tf_op jit(solution)/shard_map/ppermute | solution.py:608
  8.5 0.6 copy-start.4
  8.5 0.6 copy-start.5
  64.9 24.4 %all-to-all-start.2 = ((f32[64,32,128]{2,1,0:T(8,128)}), f32[64,32,128]{2,1,0:T(8,128)S(1)}, u32[]{:S(2)}, u32[]{:S(2)}) async-start(f32[64,32,128]{2,1,0:T(8,128)} %bitcast.27), calls=%async_computation.2 | async-start | bytes 2097152 | tf_op jit(solution)/shard_map/all_to_all | solution.py:653
  89.3 4.7 %copy-start = (f32[64,32,128]{2,1,0:T(8,128)}, f32[64,32,128]{2,1,0:T(8,128)S(1)}, u32[]{:S(2)}) copy-start(f32[64,32,128]{2,1,0:T(8,128)S(1)} %all-to-all-done.2.refs_0_) | copy-start | bytes 3145732
  89.3 23.1 %all-to-all-start.1 = ((f32[64,32,128]{2,1,0:T(8,128)}), f32[64,32,128]{2,1,0:T(8,128)S(1)}, u32[]{:S(2)}, u32[]{:S(2)}) async-start(f32[64,32,128]{2,1,0:T(8,128)} %bitcast.26), calls=%async_computation.1 | async-start | bytes 2097152 | tf_op jit(solution)/shard_map/all_to_all | solution.py:653
  112.4 1.0 copy-start.1
